TPU v7x, 128 devices: a whole 4x4x4 slice. The times are simulated.
128 devices in a mesh: gx: 16 (over z, x), gy: 8 (over y, core).
Axes of the slice: x: 4, y: 4, z: 4, core: 2. Of those that a mesh axis runs over, the one named last changes fastest.
Arguments:
- positions: float32 [3, 1048576], P(None, ('gx', 'gy')), may hold values from -5 to 5, as said below
- noise: float32 [3, 1048576], P(None, ('gx', 'gy')), may hold values from -0.6 to 0.6
- route: int32 [1048576], P(('gx', 'gy')), may hold values from 0 to 16383, as said below
- node_perm: int32 [16, 8, 16384], P(None, 'gy'), may hold values from 0 to 16383, each once within a row
- pair_first: int32 [128, 1024], P(('gx', 'gy')), may hold values from 0 to 255
- pair_second: int32 [128, 1024], P(('gx', 'gy')), may hold values from 0 to 511
- pair_count: int32 [128], P(('gx', 'gy')), may hold values from 512 to 1024, as said below
Outputs:
- moved: float32 [3, 1048576], P(None, ('gx', 'gy'))
- drift: float32 [3, 1048576], P(None, ('gx', 'gy'))
Inputs may be any that keep to these rules, and one draw needn't show every extreme that they name: `positions`: consecutive beads of a chain lie between 0.25 and 0.95 apart. `route`: within one device the values are distinct and rise along its beads; at most 128 beads of one device go to one device, and every device sends exactly 128 beads to some device. `pair_count`: some device's count is 1024.
All inputs are finite; a program needn't handle non-finite values.
Results may differ from a plain program's by a relative error of at most 0.015.
Values sent between devices are 32-bit elements; how exact they have to be, the bound alone decides.
A program may use at most 128 MiB of HBM per device.

v0:
```python
from functools import partial
import math

import jax
import jax.numpy as jnp
from jax import lax
from jax.sharding import PartitionSpec as P

G = 128
BEAD_CH = 64
CELL = 64


bead_radius = 0.5
split_xi = 0.5
time_step = 0.01
fene_k = 30.0
fene_reach = 1.5
bend_k = 2.0
grid_spacing = 4.0
pair_block = 64


def shifted(value, axis, by):
    devices = lax.axis_size(axis)
    return lax.ppermute(value, axis, [(i, (i + by) % devices) for i in range(devices)])


def bonded_forces(positions):
    chains = positions.reshape(3, -1, BEAD_CH)

    def energy(coords):
        bond = coords[:, :, 1:] - coords[:, :, :-1]
        square = jnp.sum(bond * bond, axis=0)
        stretch = -0.5 * fene_k * fene_reach**2 * jnp.sum(jnp.log(1.0 - square / fene_reach**2))
        length = jnp.sqrt(square)
        cosine = jnp.sum(bond[:, :, 1:] * bond[:, :, :-1], axis=0) / (
            length[:, 1:] * length[:, :-1]
        )
        return stretch + bend_k * jnp.sum(1.0 - cosine)

    return (-jax.grad(energy)(chains)).reshape(3, -1)


def tile_pairs(near_pos, near_force, far_pos, far_force):
    offsets = [near_pos[channel][:, :, None] - far_pos[channel][:, None, :] for channel in range(3)]
    square = (
        offsets[0] * offsets[0] + offsets[1] * offsets[1] + offsets[2] * offsets[2] + bead_radius**2
    )
    distance = jnp.sqrt(square)
    scaled = bead_radius / distance
    scaled_cube = scaled * scaled * scaled
    screen = jax.scipy.special.erfc(split_xi * distance)
    gauss_part = 0.5 * split_xi * bead_radius * jnp.exp(-(split_xi**2) * square)
    along_part = screen * (0.75 * scaled + 0.5 * scaled_cube) + gauss_part
    across = (screen * (0.75 * scaled - 1.5 * scaled_cube) - gauss_part) / square
    onto_far = across * sum(
        (offsets[channel] * far_force[channel][:, None, :] for channel in range(3))
    )
    onto_near = across * sum(
        (offsets[channel] * near_force[channel][:, :, None] for channel in range(3))
    )
    near_vel = jnp.stack(
        [
            jnp.sum(
                along_part * far_force[channel][:, None, :] + onto_far * offsets[channel], axis=2
            )
            for channel in range(3)
        ]
    )
    far_vel = jnp.stack(
        [
            jnp.sum(
                along_part * near_force[channel][:, :, None] + onto_near * offsets[channel], axis=1
            )
            for channel in range(3)
        ]
    )
    return (near_vel, far_vel)


def pair_sums(cells, first_list, second_list, pair_total):

    def turn(turn_index, velocity_sum):
        offset_at = turn_index * pair_block
        near_idx = lax.dynamic_slice_in_dim(first_list, offset_at, pair_block)
        far_idx = lax.dynamic_slice_in_dim(second_list, offset_at, pair_block)
        live_mask = (offset_at + jnp.arange(pair_block, dtype=jnp.int32) < pair_total).astype(
            jnp.float32
        )
        near_cells = jnp.take(cells, near_idx, axis=1)
        far_cells = jnp.take(cells, far_idx, axis=1)
        near_vel, far_vel = tile_pairs(near_cells[:3], near_cells[3:], far_cells[:3], far_cells[3:])
        cross_mask = live_mask * (near_idx != far_idx).astype(jnp.float32)
        velocity_sum = velocity_sum.at[:, near_idx].add(near_vel * live_mask[None, :, None])
        return velocity_sum.at[:, far_idx].add(far_vel * cross_mask[None, :, None])

    turn_total = (pair_total + pair_block - 1) // pair_block
    start_sum = jnp.zeros((3, cells.shape[1], CELL), jnp.float32)
    return lax.fori_loop(0, turn_total, turn, start_sum)


def signed_wave(grid_index):
    return jnp.where(grid_index < G // 2, grid_index, grid_index - G).astype(jnp.float32) * (
        2.0 * math.pi / (G * grid_spacing)
    )


def forward_pass(real_in, imag_in, form, cos_part, sin_part):
    contract = partial(jnp.einsum, precision=lax.Precision.HIGHEST)
    real_out = contract(form, real_in, cos_part) + contract(form, imag_in, sin_part)
    imag_out = contract(form, imag_in, cos_part) - contract(form, real_in, sin_part)
    return (real_out, imag_out)


def inverse_pass(real_in, imag_in, form, cos_part, sin_part):
    contract = partial(jnp.einsum, precision=lax.Precision.HIGHEST)
    real_out = contract(form, real_in, cos_part) - contract(form, imag_in, sin_part)
    imag_out = contract(form, imag_in, cos_part) + contract(form, real_in, sin_part)
    return (real_out, imag_out)


def project_flow(spectrum, wave_x, wave_y, wave_z):
    wave_sq = wave_x * wave_x + wave_y * wave_y + wave_z * wave_z
    wave_safe = jnp.where(wave_sq > 0, wave_sq, 1.0)
    spread_sq = wave_sq / (4.0 * split_xi**2)
    green_fn = jnp.where(
        wave_sq > 0,
        (1.0 - bead_radius**2 * wave_sq / 3.0)
        * (1.0 + spread_sq)
        * jnp.exp(-spread_sq)
        / wave_safe,
        0.0,
    )
    along_wave = (wave_x * spectrum[0] + wave_y * spectrum[1] + wave_z * spectrum[2]) / wave_safe
    return jnp.stack(
        [
            green_fn * (spectrum[0] - wave_x * along_wave),
            green_fn * (spectrum[1] - wave_y * along_wave),
            green_fn * (spectrum[2] - wave_z * along_wave),
        ]
    )


def kspace_part(force_rows, n_gx, n_gy):
    local_x = G // n_gx
    local_y = G // n_gy
    grid_index = jnp.arange(G, dtype=jnp.int32)
    phase_grid = (grid_index[:, None] * grid_index[None, :] % G).astype(jnp.float32) * (
        2.0 * math.pi / G
    )
    cosine_table = jnp.cos(phase_grid)
    sine_table = jnp.sin(phase_grid)
    contract = partial(jnp.einsum, precision=lax.Precision.HIGHEST)
    force_field = force_rows.reshape(3, local_x, local_y, G)
    wave_full = signed_wave(grid_index)
    row_gx = lax.axis_index("gx")
    row_gy = lax.axis_index("gy")
    freq_count = G
    spec_z = jnp.stack(
        [
            contract("cabz,zk->cabk", force_field, cosine_table),
            -contract("cabz,zk->cabk", force_field, sine_table),
        ]
    )
    cos_x = cosine_table.reshape(n_gx, local_x, G)
    sin_x = sine_table.reshape(n_gx, local_x, G)
    cos_y = cosine_table.reshape(n_gy, local_y, G)
    sin_y = sine_table.reshape(n_gy, local_y, G)
    depth_part = freq_count // n_gx
    width_part = G // n_gy
    slabs = lax.all_to_all(spec_z[:, :, None], "gx", split_axis=5, concat_axis=2, tiled=True)
    xr_part, xi_part = forward_pass(slabs[0], slabs[1], "ciabl,iak->cbkl", cos_x, sin_x)
    pencils = lax.all_to_all(
        jnp.stack([xr_part, xi_part])[:, :, None], "gy", split_axis=4, concat_axis=2, tiled=True
    )
    yr_part, yi_part = forward_pass(pencils[0], pencils[1], "cjbkl,jbm->ckml", cos_y, sin_y)
    wave_x = signed_wave(row_gy * width_part + jnp.arange(width_part, dtype=jnp.int32))[
        :, None, None
    ]
    wave_y = wave_full[None, :, None]
    wave_z = signed_wave(row_gx * depth_part + jnp.arange(depth_part, dtype=jnp.int32))[
        None, None, :
    ]
    flow_real = project_flow(yr_part, wave_x, wave_y, wave_z)
    flow_imag = project_flow(yi_part, wave_x, wave_y, wave_z)
    br_part, bi_part = inverse_pass(flow_real, flow_imag, "ckml,jbm->cjbkl", cos_y, sin_y)
    back = lax.all_to_all(
        jnp.stack([br_part, bi_part]), "gy", split_axis=2, concat_axis=4, tiled=True
    )[:, :, 0]
    ar_part, ai_part = inverse_pass(back[0], back[1], "cbkl,iak->ciabl", cos_x, sin_x)
    gathered = lax.all_to_all(
        jnp.stack([ar_part, ai_part]), "gx", split_axis=2, concat_axis=5, tiled=True
    )[:, :, 0]
    result = contract("cabk,zk->cabz", gathered[0], cosine_table) - contract(
        "cabk,zk->cabz", gathered[1], sine_table
    )
    return (result / float(G**3)).reshape(3, local_x * local_y * G)


def shards(positions, noise, route, node_perm, pair_first, pair_second, pair_count):
    forces = bonded_forces(positions)
    n_gx = lax.axis_size("gx")
    n_gy = lax.axis_size("gy")
    devices = n_gx * n_gy
    slots = node_perm.shape[2]
    per_peer = slots // devices
    blocks = slots // CELL
    row_gx = lax.axis_index("gx")
    own_order = node_perm[row_gx, 0]
    stacked = jnp.concatenate([positions, forces], axis=0)
    outgoing = (
        jnp.zeros((6, slots), jnp.float32).at[:, route].set(stacked).reshape(6, devices, per_peer)
    )
    incoming = lax.all_to_all(outgoing, ("gx", "gy"), split_axis=1, concat_axis=1, tiled=True)
    grid_data = jnp.zeros((6, slots), jnp.float32).at[:, own_order].set(incoming.reshape(6, slots))
    beside_data = shifted(grid_data, "gx", -1)
    cells = jnp.concatenate(
        [grid_data.reshape(6, blocks, CELL), beside_data.reshape(6, blocks, CELL)], axis=1
    )
    real_vel = pair_sums(cells, pair_first[0], pair_second[0], pair_count[0])
    wave_vel = kspace_part(grid_data[3:], n_gx, n_gy)
    own_vel = real_vel[:, :blocks].reshape(3, slots) + wave_vel
    far_part = real_vel[:, blocks:].reshape(3, slots)
    next_order = node_perm[(row_gx + 1) % n_gx, 0]
    back_msg = own_vel[:, own_order].reshape(3, devices, per_peer)
    part_msg = far_part[:, next_order].reshape(3, devices, per_peer)
    arrived, arrived_part = (
        lax.all_to_all(back_msg, ("gx", "gy"), split_axis=1, concat_axis=1, tiled=True),
        lax.all_to_all(part_msg, ("gx", "gy"), split_axis=1, concat_axis=1, tiled=True),
    )
    target_dev = route // per_peer
    before = (target_dev // n_gy + n_gx - 1) % n_gx * n_gy + target_dev % n_gy
    velocity = (
        arrived.reshape(3, slots)[:, route]
        + arrived_part.reshape(3, slots)[:, before * per_peer + route % per_peer]
    )
    drift = time_step * velocity
    moved = positions + drift + noise
    return (moved, drift)


def solution(mesh):
    in_specs = (
        P(None, ("gx", "gy")),
        P(None, ("gx", "gy")),
        P(("gx", "gy")),
        P(None, "gy", None),
        P(("gx", "gy"), None),
        P(("gx", "gy"), None),
        P(("gx", "gy")),
    )
    out_specs = (P(None, ("gx", "gy")), P(None, ("gx", "gy")))
    return jax.shard_map(shards, mesh=mesh, in_specs=in_specs, out_specs=out_specs, check_vma=False)
```

profile of v0, /device:TPU:1, one launch (start us, length us, event | category | flops | bytes accessed | tf_op | source)
XLA Modules:
  0.0 931.6 jit_solution(8236666221822720358)
XLA Ops:
  6.1 24.5 %scatter_custom_fusion.2 = f32[6,16384]{0,1:T(8,128)} fusion(s32[8192]{0:T(1024)S(1)} %get-tuple-element.145, f32[8192,6]{1,0:T(8,128)} %copy.123, f32[]{:T(128)} %constant.234.clone.1), kind=kCustom, calls=%fused_computation.85 | custom fusion | bytes 393728 | tf_op jit(solution)/shard_map/scatter | solution.py:213
  36.7 11.5 %all-to-all-start = ((f32[6,128,128]{2,0,1:T(8,128)}), f32[6,128,128]{2,0,1:T(8,128)S(1)}, u32[]{:S(2)}, u32[]{:S(2)}) async-start(f32[6,128,128]{2,0,1:T(8,128)} %copy.124), calls=%async_computation | async-start | bytes 1048576 | tf_op jit(solution)/shard_map/all_to_all | solution.py:215
  51.5 10.2 %all-to-all-done = f32[6,128,128]{2,0,1:T(8,128)S(1)} async-done(((f32[6,128,128]{2,0,1:T(8,128)}), f32[6,128,128]{2,0,1:T(8,128)S(1)}, u32[]{:S(2)}, u32[]{:S(2)}) %all-to-all-start) | async-done | bytes 393248 | tf_op jit(solution)/shard_map/all_to_all | solution.py:215
  67.0 44.9 %scatter_custom_fusion.3 = f32[6,16384]{0,1:T(8,128)} fusion(s32[16384]{0:T(1024)S(1)} %bitcast.405, f32[16384,6]{1,0:T(8,128)} %copy.125, f32[]{:T(128)} %constant.234.clone.1), kind=kCustom, calls=%fused_computation.83 | custom fusion | bytes 393728 | tf_op jit(solution)/shard_map/scatter | solution.py:216
  111.9 6.6 slice.194
  132.9 7.7 all-to-all-done.1
  205.2 6.6 copy.127
  236.2 419.9 %while.10 = (s32[]{:T(128)}, f32[3,512,64]{2,0,1:T(4,128)S(1)}, s32[]{:T(128)}, s32[1024]{0:T(1024)}, f32[6,512,64]{2,0,1:T(8,128)}, /*index=5*/s32[1024]{0:T(10...) while((s32[]{:T(128)}, f32[3,512,64]{2,0,1:T(4,128)S(1)}, s32[]{:T(128)}, ...), condition=%wide.region_13.15_spmd, body=%wide.region_4.14_spmd.sunk | while | flops 31845444 | bytes 2175403 | solution.py:100
  242.0 13.2 %fusion.279 = (f32[64,64]{1,0:T(8,128)S(1)}, f32[64,64]{1,0:T(8,128)S(1)}, f32[64,64]{1,0:T(8,128)S(1)}, f32[64,64]{1,0:T(8,128)S(1)}, f32[64,64]{1,0:T(8,128)S(1)}, /*index=5*/f32[64,64]{1,0:T(8,128)S(1)}) fusion(f32[64,64]{1,0:T(8,128)S(1)} %bitcast.394, f32[64,64]{1,0:T(8,128)S(1)} %bitcast.391, f32[64,64]{1,0:T(8,128)S(1)} %bitcast.397, ...), kind=kLoop, calls=%fused_computation.40.clone.1 | loop fusion | flops 31694848 | bytes 294912 | tf_op jit(solution)/shard_map/while/body/reduce_sum | solution.py:73
  268.2 13.2 %fusion.279 = (f32[64,64]{1,0:T(8,128)S(1)}, f32[64,64]{1,0:T(8,128)S(1)}, f32[64,64]{1,0:T(8,128)S(1)}, f32[64,64]{1,0:T(8,128)S(1)}, f32[64,64]{1,0:T(8,128)S(1)}, /*index=5*/f32[64,64]{1,0:T(8,128)S(1)}) fusion(f32[64,64]{1,0:T(8,128)S(1)} %bitcast.394, f32[64,64]{1,0:T(8,128)S(1)} %bitcast.391, f32[64,64]{1,0:T(8,128)S(1)} %bitcast.397, ...), kind=kLoop, calls=%fused_computation.40.clone.1 | loop fusion | flops 31694848 | bytes 294912 | tf_op jit(solution)/shard_map/while/body/reduce_sum | solution.py:73
  294.5 13.2 %fusion.279 = (f32[64,64]{1,0:T(8,128)S(1)}, f32[64,64]{1,0:T(8,128)S(1)}, f32[64,64]{1,0:T(8,128)S(1)}, f32[64,64]{1,0:T(8,128)S(1)}, f32[64,64]{1,0:T(8,128)S(1)}, /*index=5*/f32[64,64]{1,0:T(8,128)S(1)}) fusion(f32[64,64]{1,0:T(8,128)S(1)} %bitcast.394, f32[64,64]{1,0:T(8,128)S(1)} %bitcast.391, f32[64,64]{1,0:T(8,128)S(1)} %bitcast.397, ...), kind=kLoop, calls=%fused_computation.40.clone.1 | loop fusion | flops 31694848 | bytes 294912 | tf_op jit(solution)/shard_map/while/body/reduce_sum | solution.py:73
  320.7 13.2 %fusion.279 = (f32[64,64]{1,0:T(8,128)S(1)}, f32[64,64]{1,0:T(8,128)S(1)}, f32[64,64]{1,0:T(8,128)S(1)}, f32[64,64]{1,0:T(8,128)S(1)}, f32[64,64]{1,0:T(8,128)S(1)}, /*index=5*/f32[64,64]{1,0:T(8,128)S(1)}) fusion(f32[64,64]{1,0:T(8,128)S(1)} %bitcast.394, f32[64,64]{1,0:T(8,128)S(1)} %bitcast.391, f32[64,64]{1,0:T(8,128)S(1)} %bitcast.397, ...), kind=kLoop, calls=%fused_computation.40.clone.1 | loop fusion | flops 31694848 | bytes 294912 | tf_op jit(solution)/shard_map/while/body/reduce_sum | solution.py:73
  347.0 13.2 %fusion.279 = (f32[64,64]{1,0:T(8,128)S(1)}, f32[64,64]{1,0:T(8,128)S(1)}, f32[64,64]{1,0:T(8,128)S(1)}, f32[64,64]{1,0:T(8,128)S(1)}, f32[64,64]{1,0:T(8,128)S(1)}, /*index=5*/f32[64,64]{1,0:T(8,128)S(1)}) fusion(f32[64,64]{1,0:T(8,128)S(1)} %bitcast.394, f32[64,64]{1,0:T(8,128)S(1)} %bitcast.391, f32[64,64]{1,0:T(8,128)S(1)} %bitcast.397, ...), kind=kLoop, calls=%fused_computation.40.clone.1 | loop fusion | flops 31694848 | bytes 294912 | tf_op jit(solution)/shard_map/while/body/reduce_sum | solution.py:73
  373.2 13.2 %fusion.279 = (f32[64,64]{1,0:T(8,128)S(1)}, f32[64,64]{1,0:T(8,128)S(1)}, f32[64,64]{1,0:T(8,128)S(1)}, f32[64,64]{1,0:T(8,128)S(1)}, f32[64,64]{1,0:T(8,128)S(1)}, /*index=5*/f32[64,64]{1,0:T(8,128)S(1)}) fusion(f32[64,64]{1,0:T(8,128)S(1)} %bitcast.394, f32[64,64]{1,0:T(8,128)S(1)} %bitcast.391, f32[64,64]{1,0:T(8,128)S(1)} %bitcast.397, ...), kind=kLoop, calls=%fused_computation.40.clone.1 | loop fusion | flops 31694848 | bytes 294912 | tf_op jit(solution)/shard_map/while/body/reduce_sum | solution.py:73
  399.4 13.2 %fusion.279 = (f32[64,64]{1,0:T(8,128)S(1)}, f32[64,64]{1,0:T(8,128)S(1)}, f32[64,64]{1,0:T(8,128)S(1)}, f32[64,64]{1,0:T(8,128)S(1)}, f32[64,64]{1,0:T(8,128)S(1)}, /*index=5*/f32[64,64]{1,0:T(8,128)S(1)}) fusion(f32[64,64]{1,0:T(8,128)S(1)} %bitcast.394, f32[64,64]{1,0:T(8,128)S(1)} %bitcast.391, f32[64,64]{1,0:T(8,128)S(1)} %bitcast.397, ...), kind=kLoop, calls=%fused_computation.40.clone.1 | loop fusion | flops 31694848 | bytes 294912 | tf_op jit(solution)/shard_map/while/body/reduce_sum | solution.py:73
  425.7 13.2 %fusion.279 = (f32[64,64]{1,0:T(8,128)S(1)}, f32[64,64]{1,0:T(8,128)S(1)}, f32[64,64]{1,0:T(8,128)S(1)}, f32[64,64]{1,0:T(8,128)S(1)}, f32[64,64]{1,0:T(8,128)S(1)}, /*index=5*/f32[64,64]{1,0:T(8,128)S(1)}) fusion(f32[64,64]{1,0:T(8,128)S(1)} %bitcast.394, f32[64,64]{1,0:T(8,128)S(1)} %bitcast.391, f32[64,64]{1,0:T(8,128)S(1)} %bitcast.397, ...), kind=kLoop, calls=%fused_computation.40.clone.1 | loop fusion | flops 31694848 | bytes 294912 | tf_op jit(solution)/shard_map/while/body/reduce_sum | solution.py:73
  451.9 13.2 %fusion.279 = (f32[64,64]{1,0:T(8,128)S(1)}, f32[64,64]{1,0:T(8,128)S(1)}, f32[64,64]{1,0:T(8,128)S(1)}, f32[64,64]{1,0:T(8,128)S(1)}, f32[64,64]{1,0:T(8,128)S(1)}, /*index=5*/f32[64,64]{1,0:T(8,128)S(1)}) fusion(f32[64,64]{1,0:T(8,128)S(1)} %bitcast.394, f32[64,64]{1,0:T(8,128)S(1)} %bitcast.391, f32[64,64]{1,0:T(8,128)S(1)} %bitcast.397, ...), kind=kLoop, calls=%fused_computation.40.clone.1 | loop fusion | flops 31694848 | bytes 294912 | tf_op jit(solution)/shard_map/while/body/reduce_sum | solution.py:73
  478.2 13.2 %fusion.279 = (f32[64,64]{1,0:T(8,128)S(1)}, f32[64,64]{1,0:T(8,128)S(1)}, f32[64,64]{1,0:T(8,128)S(1)}, f32[64,64]{1,0:T(8,128)S(1)}, f32[64,64]{1,0:T(8,128)S(1)}, /*index=5*/f32[64,64]{1,0:T(8,128)S(1)}) fusion(f32[64,64]{1,0:T(8,128)S(1)} %bitcast.394, f32[64,64]{1,0:T(8,128)S(1)} %bitcast.391, f32[64,64]{1,0:T(8,128)S(1)} %bitcast.397, ...), kind=kLoop, calls=%fused_computation.40.clone.1 | loop fusion | flops 31694848 | bytes 294912 | tf_op jit(solution)/shard_map/while/body/reduce_sum | solution.py:73
  504.4 13.2 %fusion.279 = (f32[64,64]{1,0:T(8,128)S(1)}, f32[64,64]{1,0:T(8,128)S(1)}, f32[64,64]{1,0:T(8,128)S(1)}, f32[64,64]{1,0:T(8,128)S(1)}, f32[64,64]{1,0:T(8,128)S(1)}, /*index=5*/f32[64,64]{1,0:T(8,128)S(1)}) fusion(f32[64,64]{1,0:T(8,128)S(1)} %bitcast.394, f32[64,64]{1,0:T(8,128)S(1)} %bitcast.391, f32[64,64]{1,0:T(8,128)S(1)} %bitcast.397, ...), kind=kLoop, calls=%fused_computation.40.clone.1 | loop fusion | flops 31694848 | bytes 294912 | tf_op jit(solution)/shard_map/while/body/reduce_sum | solution.py:73
  530.7 13.2 %fusion.279 = (f32[64,64]{1,0:T(8,128)S(1)}, f32[64,64]{1,0:T(8,128)S(1)}, f32[64,64]{1,0:T(8,128)S(1)}, f32[64,64]{1,0:T(8,128)S(1)}, f32[64,64]{1,0:T(8,128)S(1)}, /*index=5*/f32[64,64]{1,0:T(8,128)S(1)}) fusion(f32[64,64]{1,0:T(8,128)S(1)} %bitcast.394, f32[64,64]{1,0:T(8,128)S(1)} %bitcast.391, f32[64,64]{1,0:T(8,128)S(1)} %bitcast.397, ...), kind=kLoop, calls=%fused_computation.40.clone.1 | loop fusion | flops 31694848 | bytes 294912 | tf_op jit(solution)/shard_map/while/body/reduce_sum | solution.py:73
  556.9 13.2 %fusion.279 = (f32[64,64]{1,0:T(8,128)S(1)}, f32[64,64]{1,0:T(8,128)S(1)}, f32[64,64]{1,0:T(8,128)S(1)}, f32[64,64]{1,0:T(8,128)S(1)}, f32[64,64]{1,0:T(8,128)S(1)}, /*index=5*/f32[64,64]{1,0:T(8,128)S(1)}) fusion(f32[64,64]{1,0:T(8,128)S(1)} %bitcast.394, f32[64,64]{1,0:T(8,128)S(1)} %bitcast.391, f32[64,64]{1,0:T(8,128)S(1)} %bitcast.397, ...), kind=kLoop, calls=%fused_computation.40.clone.1 | loop fusion | flops 31694848 | bytes 294912 | tf_op jit(solution)/shard_map/while/body/reduce_sum | solution.py:73
  583.2 13.2 %fusion.279 = (f32[64,64]{1,0:T(8,128)S(1)}, f32[64,64]{1,0:T(8,128)S(1)}, f32[64,64]{1,0:T(8,128)S(1)}, f32[64,64]{1,0:T(8,128)S(1)}, f32[64,64]{1,0:T(8,128)S(1)}, /*index=5*/f32[64,64]{1,0:T(8,128)S(1)}) fusion(f32[64,64]{1,0:T(8,128)S(1)} %bitcast.394, f32[64,64]{1,0:T(8,128)S(1)} %bitcast.391, f32[64,64]{1,0:T(8,128)S(1)} %bitcast.397, ...), kind=kLoop, calls=%fused_computation.40.clone.1 | loop fusion | flops 31694848 | bytes 294912 | tf_op jit(solution)/shard_map/while/body/reduce_sum | solution.py:73
  609.4 13.2 %fusion.279 = (f32[64,64]{1,0:T(8,128)S(1)}, f32[64,64]{1,0:T(8,128)S(1)}, f32[64,64]{1,0:T(8,128)S(1)}, f32[64,64]{1,0:T(8,128)S(1)}, f32[64,64]{1,0:T(8,128)S(1)}, /*index=5*/f32[64,64]{1,0:T(8,128)S(1)}) fusion(f32[64,64]{1,0:T(8,128)S(1)} %bitcast.394, f32[64,64]{1,0:T(8,128)S(1)} %bitcast.391, f32[64,64]{1,0:T(8,128)S(1)} %bitcast.397, ...), kind=kLoop, calls=%fused_computation.40.clone.1 | loop fusion | flops 31694848 | bytes 294912 | tf_op jit(solution)/shard_map/while/body/reduce_sum | solution.py:73
  635.6 13.2 %fusion.279 = (f32[64,64]{1,0:T(8,128)S(1)}, f32[64,64]{1,0:T(8,128)S(1)}, f32[64,64]{1,0:T(8,128)S(1)}, f32[64,64]{1,0:T(8,128)S(1)}, f32[64,64]{1,0:T(8,128)S(1)}, /*index=5*/f32[64,64]{1,0:T(8,128)S(1)}) fusion(f32[64,64]{1,0:T(8,128)S(1)} %bitcast.394, f32[64,64]{1,0:T(8,128)S(1)} %bitcast.391, f32[64,64]{1,0:T(8,128)S(1)} %bitcast.397, ...), kind=kLoop, calls=%fused_computation.40.clone.1 | loop fusion | flops 31694848 | bytes 294912 | tf_op jit(solution)/shard_map/while/body/reduce_sum | solution.py:73
  665.9 57.7 %gather_fusion.4 = f32[16384,3]{1,0:T(8,128)} fusion(f32[3,16384]{0,1:T(8,128)} %bitcast.376, s32[16384]{0:T(1024)S(1)} %copy-done.4), kind=kCustom, calls=%fused_computation.4 | custom fusion | bytes 458752 | tf_op jit(solution)/shard_map/gather | solution.py:227
  729.6 10.2 %all-to-all-start.6 = ((f32[3,128,128]{2,0,1:T(4,128)}), f32[3,128,128]{2,0,1:T(4,128)}, u32[]{:S(2)}, u32[]{:S(2)}) async-start(f32[3,128,128]{2,0,1:T(4,128)} %copy.154), calls=%async_computation.6 | async-start | bytes 524288 | tf_op jit(solution)/shard_map/all_to_all | solution.py:230
  752.9 9.8 %bitcast_add_fusion = f32[3,16384]{0,1:T(8,128)} fusion(f32[3,8,16,128]{0,3,2,1:T(8,128)} %copy.183, f32[3,256,64]{0,2,1:T(8,128)} %copy.130), kind=kLoop, calls=%fused_computation.80 | loop fusion | flops 49152 | bytes 589824 | tf_op jit(solution)/shard_map/add | solution.py:223
  762.7 57.8 %gather_fusion.2 = f32[16384,3]{1,0:T(8,128)} fusion(f32[3,16384]{0,1:T(8,128)} %bitcast_add_fusion, s32[16384]{0:T(1024)S(1)} %copy-done.3), kind=kCustom, calls=%fused_computation.2 | custom fusion | bytes 458752 | tf_op jit(solution)/shard_map/gather | solution.py:226
  826.4 9.8 %all-to-all-start.5 = ((f32[3,128,128]{2,0,1:T(4,128)}), f32[3,128,128]{2,0,1:T(4,128)S(1)}, u32[]{:S(2)}, u32[]{:S(2)}) async-start(f32[3,128,128]{2,0,1:T(4,128)} %copy.151), calls=%async_computation.5 | async-start | bytes 524288 | tf_op jit(solution)/shard_map/all_to_all | solution.py:229
  847.2 31.1 %gather_fusion.5 = f32[8192,3]{1,0:T(8,128)} fusion(f32[3,16384]{0,1:T(8,128)} %bitcast.382, s32[8192]{0:T(1024)S(1)} %copy-done.10), kind=kCustom, calls=%fused_computation.5 | custom fusion | bytes 229376 | tf_op jit(solution)/shard_map/gather | solution.py:236
  883.1 31.1 %gather_fusion.3 = f32[8192,3]{1,0:T(8,128)} fusion(f32[3,16384]{0,1:T(8,128)} %bitcast.381, s32[8192]{0:T(1024)S(1)} %copy-done.9), kind=kCustom, calls=%fused_computation.3 | custom fusion | bytes 229376 | tf_op jit(solution)/shard_map/gather | solution.py:235
  914.2 10.0 %add_add_fusion = (f32[3,8192]{0,1:T(8,128)}, f32[3,8192]{0,1:T(8,128)}) fusion(f32[3,8192]{0,1:T(8,128)} %copy.157, f32[3,8192]{0,1:T(8,128)} %copy.156, f32[8192,3]{1,0:T(8,128)} %gather_fusion.3, f32[8192,3]{1,0:T(8,128)} %gather_fusion.5), kind=kLoop, calls=%fused_computation.82 | loop fusion | flops 98304 | bytes 589824 | tf_op jit(solution)/shard_map/add | solution.py:239
  (399 shorter events, 386.6 us)
Async XLA Ops:
  1.7 1.0 copy-start.1
  2.7 2.7 copy-start.12
  36.7 25.0 %all-to-all-start = ((f32[6,128,128]{2,0,1:T(8,128)}), f32[6,128,128]{2,0,1:T(8,128)S(1)}, u32[]{:S(2)}, u32[]{:S(2)}) async-start(f32[6,128,128]{2,0,1:T(8,128)} %copy.124), calls=%async_computation | async-start | bytes 1048576 | tf_op jit(solution)/shard_map/all_to_all | solution.py:215
  49.9 17.1 %copy-start.6 = (s32[16384,1]{0,1:T(1,128)}, s32[16384,1]{0,1:T(1,128)S(1)}, u32[]{:S(2)}) copy-start(s32[16384,1]{0,1:T(1,128)S(1)} %get-tuple-element.131) | copy-start | bytes 196612
  126.0 6.2 copy-start.15
  126.0 6.2 copy-start.16
  128.0 12.6 %all-to-all-start.1 = ((f32[16,1,6144]{2,1,0:T(1,128)}), f32[16,1,6144]{2,1,0:T(1,128)S(1)}, u32[]{:S(2)}, u32[]{:S(2)}) async-start(f32[16,1,6144]{2,1,0:T(1,128)} %reshape.500), calls=%async_computation.1 | async-start | bytes 786432 | tf_op jit(solution)/shard_map/all_to_all | solution.py:172
  159.7 7.2 copy-start.7
  161.6 13.4 %all-to-all-start.2 = ((f32[8,1,12288]{2,1,0:T(1,128)}), f32[8,1,12288]{2,1,0:T(1,128)S(1)}, u32[]{:S(2)}, u32[]{:S(2)}) async-start(f32[8,1,12288]{2,1,0:T(1,128)} %reshape.502), calls=%async_computation.2 | async-start | bytes 786432 | tf_op jit(solution)/shard_map/all_to_all | solution.py:174
  173.7 38.1 %collective-permute-start = (f32[6,16384]{1,0:T(8,128)}, f32[6,16384]{1,0:T(8,128)}, u32[]{:S(2)}, u32[]{:S(2)}) collective-permute-start(f32[6,16384]{1,0:T(8,128)} %copy.126), channel_id=1, source_target_pairs={{0,120},{8,0},{16,8},{24,16},{32,24},{40,32},{48,40},{56,48},{64,5... | collective-permute-start | bytes 1179656 | tf_op jit(solution)/shard_map/ppermute | solution.py:26
  183.7 5.5 copy-start.11
  183.7 5.5 copy-start.13
  183.7 5.5 copy-start.14
  183.7 5.5 copy-start.17
  197.2 6.7 copy-start.5
  199.1 16.4 %all-to-all-start.3 = ((f32[8,1,12288]{2,1,0:T(1,128)}), f32[8,1,12288]{2,1,0:T(1,128)S(1)}, u32[]{:S(2)}, u32[]{:S(2)}) async-start(f32[8,1,12288]{2,1,0:T(1,128)} %reshape.504), calls=%async_computation.3 | async-start | bytes 786432 | tf_op jit(solution)/shard_map/all_to_all | solution.py:188
  221.3 1.8 copy-start
  232.5 497.1 %all-to-all-start.4 = ((f32[16,1,6144]{2,1,0:T(1,128)}), f32[16,1,6144]{2,1,0:T(1,128)S(1)}, u32[]{:S(2)}, u32[]{:S(2)}) async-start(f32[16,1,6144]{2,1,0:T(1,128)} %reshape.506), calls=%async_computation.4 | async-start | bytes 786432 | tf_op jit(solution)/shard_map/all_to_all | solution.py:192
  661.1 4.8 copy-start.4
  729.6 96.8 %all-to-all-start.6 = ((f32[3,128,128]{2,0,1:T(4,128)}), f32[3,128,128]{2,0,1:T(4,128)}, u32[]{:S(2)}, u32[]{:S(2)}) async-start(f32[3,128,128]{2,0,1:T(4,128)} %copy.154), calls=%async_computation.6 | async-start | bytes 524288 | tf_op jit(solution)/shard_map/all_to_all | solution.py:230
  752.9 9.8 %copy-start.3 = (s32[16384]{0:T(1024)S(1)}, s32[16384]{0:T(1024)}, u32[]{:S(2)}) copy-start(s32[16384]{0:T(1024)} %broadcast_clamp_fusion.1) | copy-start | bytes 196612
  820.5 15.7 %copy-start.2 = (f32[3,8192]{1,0:T(4,128)S(1)}, f32[3,8192]{1,0:T(4,128)}, u32[]{:S(2)}) copy-start(f32[3,8192]{1,0:T(4,128)} %param.11) | copy-start | bytes 294916
  826.4 51.8 %all-to-all-start.5 = ((f32[3,128,128]{2,0,1:T(4,128)}), f32[3,128,128]{2,0,1:T(4,128)S(1)}, u32[]{:S(2)}, u32[]{:S(2)}) async-start(f32[3,128,128]{2,0,1:T(4,128)} %copy.151), calls=%async_computation.5 | async-start | bytes 524288 | tf_op jit(solution)/shard_map/all_to_all | solution.py:229
  836.2 2.7 copy-start.8
  841.5 5.7 copy-start.10
  878.2 4.9 copy-start.9
where the time goes:
time: 941 us; the launch traced here: 932 us
  local copies, waits for them, and re-layouts  442 us (47%)
  other arithmetic  376 us (40%)
  starting transfers between devices  49.8 us (5%)
  matrix products  41.7 us (4%)
  waiting for transfers between devices  18.2 us (2%)
    reduce_sum x16, other arithmetic, tile_pairs(): jnp.sum(along_part * near_force[channel][:, :, None] + onto_near * offset...  211 us
    gather x1, local copies, waits for them, and re-layouts, shards(): back_msg = own_vel[:, own_order].reshape(3, devices, per_peer)  57.8 us
    gather x1, local copies, waits for them, and re-layouts, shards(): part_msg = far_part[:, next_order].reshape(3, devices, per_peer)  57.7 us
    scatter x2, local copies, waits for them, and re-layouts, shards(): jnp.zeros((6, slots), jnp.float32).at[:, own_order]  50.9 us
    scatter-add x16, other arithmetic, turn(): velocity_sum.at[:, near_idx].add(near_vel * live_mask[None, :, None])  43.8 us
    scatter-add x16, other arithmetic, turn(): return velocity_sum.at[:, far_idx].add(far_vel * cross_mask[None, :, None])  43.8 us
    gather x16, local copies, waits for them, and re-layouts, turn(): near_cells = jnp.take(cells, near_idx, axis=1)  35 us
    gather x16, local copies, waits for them, and re-layouts, turn(): far_cells = jnp.take(cells, far_idx, axis=1)  35 us
  transfers between devices with their start and end apart: 8, of which 3 were waited for; matrix products, arithmetic and copies ran while one was open for 72% of the time, Pallas kernels for 0%

commit v1 on v0

v1 whole, which is shorter than its diff:
```python
from functools import partial
import math

import numpy as np
import jax
import jax.numpy as jnp
from jax import lax
from jax.experimental import pallas as pl
from jax.experimental.pallas import tpu as pltpu
from jax.sharding import PartitionSpec as P

G = 128
BLOCKS = 256
PAIRS = 1024
STEP = 4
W_ROWS = 24
TRASH = 2 * BLOCKS

fene_k = 30.0
fene_reach = 1.5
bend_k = 2.0
time_step = 0.01
grid_spacing = 4.0

f32 = jnp.float32
bf16 = jnp.bfloat16
VMEM_LIMIT = 60 * 1024 * 1024


def dot(a, b):
    return lax.dot_general(a, b, (((1,), (0,)), ((), ())), preferred_element_type=f32)


def dot_t(a, b):
    return lax.dot_general(a, b, (((1,), (1,)), ((), ())), preferred_element_type=f32)


def split2(x):
    hi = x.astype(bf16)
    return hi, (x - hi.astype(f32)).astype(bf16)


def split3(x):
    hi = x.astype(bf16).astype(f32)
    rest = x - hi
    mid = rest.astype(bf16).astype(f32)
    return hi, mid, (rest - mid).astype(bf16).astype(f32)


def dot3(a_hi, a_lo, b_hi, b_lo, form=dot):
    return form(a_hi, b_hi) + form(a_hi, b_lo) + form(a_lo, b_hi)


def split_table(table):
    table = np.asarray(table, np.float64)
    hi = table.astype(np.float32).astype(jnp.bfloat16)
    lo = (table - hi.astype(np.float64)).astype(np.float32).astype(jnp.bfloat16)
    return np.stack([hi, lo])


def tables():
    n = np.arange(G)
    turn = 2.0 * np.pi / G
    member = np.arange(128)
    freq = np.where(member < 64, member + 1, (member - 63) % 64)
    wave = turn * (freq[:, None] * n[None, :] % G)
    even, odd = np.cos(wave), -np.sin(wave)
    special = (member % 64) == 63
    first = (member < 64)[:, None]
    even = np.where(special[:, None], np.cos(wave), even)
    z_xy = np.where(special[:, None] | first, even, odd)
    z_z = np.where(special[:, None] | ~first, even, odd)
    k1, k2 = n // 8, n % 8
    outer = 2.0 * np.pi * (k1[:, None] * k1[None, :] / 16.0 + k2[:, None] * k2[None, :] / 8.0)
    a, b = n // 16, n % 16
    inner = 2.0 * np.pi * (a[:, None] * a[None, :] / 8.0 + b[:, None] * b[None, :] / 16.0)
    twist = turn * (k1[:, None] * a[None, :] + k2[:, None] * b[None, :])
    c_out, s_out, c_in, s_in = np.cos(outer), np.sin(outer), np.cos(inner), np.sin(inner)
    return {
        "z": split_table(np.stack([z_xy, z_z])),
        "outer": split_table(np.concatenate([c_out, -s_out], 0)),
        "outer_back": split_table(np.concatenate([c_out, -s_out], 1)),
        "inner": split_table(np.block([[c_in, -s_in], [s_in, c_in]])),
        "inner_back": split_table(np.block([[c_in, s_in], [-s_in, c_in]])),
        "twist": np.stack([np.cos(twist), np.sin(twist)]).astype(np.float32),
    }


def onehot(index, size, width):
    rows = lax.broadcasted_iota(jnp.int32, (size, width), 0)
    return jnp.where(rows == index, 1.0, 0.0).astype(bf16)


def high_part(place):
    return (place >> 7) & 63


def low_part(place):
    return ((place >> 13) << 7) | (place & 127)


def scatter_rows(channels, rows, value_row, place_ref, left_ref, sum_ref):
    group = left_ref.shape[1] // 128
    span = 128 * group

    def turn(g, _):
        low = []
        for j in range(group):
            place = place_ref[pl.ds(g * group + j, 1), :]
            high_hot = onehot(high_part(place), 64, 128)
            low.append(onehot(low_part(place), 256, 128))
            for c in range(channels):
                hi, lo = split2(value_row(c, g * group + j))
                left_ref[c * 128 : c * 128 + 64, j * 128 : (j + 1) * 128] = high_hot * hi
                left_ref[c * 128 + 64 : c * 128 + 128, j * 128 : (j + 1) * 128] = high_hot * lo
        moved = dot_t(left_ref[...], jnp.concatenate(low, axis=1))
        for c in range(channels):
            sum_ref[c * 64 : (c + 1) * 64, :] += (
                moved[c * 128 : c * 128 + 64] + moved[c * 128 + 64 : c * 128 + 128]
            )
        return 0

    sum_ref[...] = jnp.zeros_like(sum_ref)
    lax.fori_loop(0, rows // group, turn, 0)


def gather_rows(channels, rows, table_hi_ref, table_lo_ref, place_ref, put):
    def turn(g, _):
        low, high = [], []
        for j in range(2):
            place = place_ref[pl.ds(g * 2 + j, 1), :]
            low.append(onehot(low_part(place), 256, 128))
            high.append(high_part(place))
        low = jnp.concatenate(low, axis=1)
        high = jnp.concatenate(high, axis=1)
        found = dot(table_hi_ref[...], low) + dot(table_lo_ref[...], low)
        rows_of = lax.broadcasted_iota(jnp.int32, (64, 256), 0) == high
        for c in range(channels):
            got = jnp.sum(
                jnp.where(rows_of, found[c * 64 : (c + 1) * 64], 0.0), axis=0, keepdims=True
            )
            for j in range(2):
                put(c, g * 2 + j, got[:, j * 128 : (j + 1) * 128])
        return 0

    lax.fori_loop(0, rows // 2, turn, 0)


def fill_table(c, plane, table_hi_ref, table_lo_ref):
    hi, lo = split2(plane)
    for ref, part in ((table_hi_ref, hi), (table_lo_ref, lo)):
        ref[c * 64 : (c + 1) * 64, 0:128] = part[0:64]
        ref[c * 64 : (c + 1) * 64, 128:256] = part[64:128]


def chain_forces(x):
    lane = lax.broadcasted_iota(jnp.int32, x[0].shape, 1) & 63
    last = lane == 63
    ahead = lambda v: pltpu.roll(v, 127, 1)
    behind = lambda v: pltpu.roll(v, 1, 1)
    bond = [jnp.where(last, 0.5, ahead(v) - v) for v in x]
    square = bond[0] * bond[0] + bond[1] * bond[1] + bond[2] * bond[2]
    inverse = lax.rsqrt(square)
    unit = [v * inverse for v in bond]
    following = [ahead(v) for v in unit]
    cosine = unit[0] * following[0] + unit[1] * following[1] + unit[2] * following[2]
    bends = lane < 62
    stretch = fene_k / (1.0 - square / fene_reach**2)
    before = behind(jnp.where(bends, 1.0, 0.0))
    cosine_before = behind(cosine)
    grad = []
    for c in range(3):
        pull = jnp.where(bends, following[c] - cosine * unit[c], 0.0)
        push = before * (behind(unit[c]) - cosine_before * unit[c])
        push = jnp.where(lane == 0, 0.0, push)
        grad.append(
            jnp.where(last, 0.0, stretch * bond[c] - bend_k * inverse * (pull + push))
        )
    return [g - jnp.where(lane == 0, 0.0, behind(g)) for g in grad]


def send_kernel(pos_ref, route_ref, out_ref, plane_ref, left_ref, sum_ref):
    rows = route_ref.shape[0]
    for c in range(3):
        for r in range(rows):
            plane_ref[c, r : r + 1, :] = pos_ref[c : c + 1, r * 128 : (r + 1) * 128]
    forces = chain_forces([plane_ref[c] for c in range(3)])
    for c in range(3):
        plane_ref[3 + c] = forces[c]
    scatter_rows(
        6, rows, lambda c, r: plane_ref[c, pl.ds(r, 1), :], route_ref, left_ref, sum_ref
    )
    for c in range(6):
        out_ref[c, 0:64, :] = sum_ref[c * 64 : (c + 1) * 64, 0:128]
        out_ref[c, 64:128, :] = sum_ref[c * 64 : (c + 1) * 64, 128:256]


def vmem(n):
    return [pl.BlockSpec(memory_space=pltpu.VMEM)] * n


def send_message(positions, route):
    return pl.pallas_call(
        send_kernel,
        out_shape=jax.ShapeDtypeStruct((6, 128, 128), f32),
        in_specs=vmem(2),
        out_specs=pl.BlockSpec(memory_space=pltpu.VMEM),
        scratch_shapes=[
            pltpu.VMEM((6, 64, 128), f32),
            pltpu.VMEM((768, 1024), bf16),
            pltpu.VMEM((384, 256), f32),
        ],
        compiler_params=pltpu.CompilerParams(vmem_limit_bytes=VMEM_LIMIT),
        name="send",
    )(positions, route)


def place_kernel(in_ref, order_ref, z_ref, out_ref, spec_ref, left_ref, sum_ref):
    scatter_rows(6, 128, lambda c, r: in_ref[c, pl.ds(r, 1), :], order_ref, left_ref, sum_ref)
    for c in range(6):
        out_ref[c, 0:64, :] = sum_ref[c * 64 : (c + 1) * 64, 0:128]
        out_ref[c, 64:128, :] = sum_ref[c * 64 : (c + 1) * 64, 128:256]
    for c in range(3):
        hi, lo = split2(out_ref[3 + c])
        kind = 0 if c < 2 else 1
        spec_ref[c] = dot3(z_ref[0, kind], z_ref[1, kind], hi, lo, dot_t)


def place_on_grid(incoming, order, z_table):
    return pl.pallas_call(
        place_kernel,
        out_shape=[
            jax.ShapeDtypeStruct((6, 128, 128), f32),
            jax.ShapeDtypeStruct((3, 128, 128), f32),
        ],
        in_specs=vmem(3),
        out_specs=vmem(2),
        scratch_shapes=[pltpu.VMEM((768, 1024), bf16), pltpu.VMEM((384, 256), f32)],
        compiler_params=pltpu.CompilerParams(vmem_limit_bytes=VMEM_LIMIT),
        name="place",
    )(incoming, order, z_table)


def wave_kernel(
    part_ref, in_ref, outer_ref, outer_back_ref, inner_ref, inner_back_ref, twist_ref,
    out_ref, mid_ref,
):
    freq, turn_re, turn_im, weight = (part_ref[i] for i in range(4))
    cos_t, sin_t = twist_ref[0], twist_ref[1]
    spectrum = []
    for c in range(3):
        hi, lo = split2(in_ref[c])
        both = dot3(outer_ref[0], outer_ref[1], hi, lo)
        re, im = both[0:128], both[128:256]
        mid_ref[:, 0:128] = re * cos_t + im * sin_t
        mid_ref[:, 128:256] = im * cos_t - re * sin_t
        hi, lo = split2(mid_ref[...])
        both = dot3(hi, lo, inner_ref[0], inner_ref[1])
        spectrum.append((both[:, 0:128], both[:, 128:256]))
    row = lax.broadcasted_iota(jnp.int32, (128, 128), 0)
    col = lax.broadcasted_iota(jnp.int32, (128, 128), 1)
    n_x = (row >> 3) + 16 * (col >> 4)
    n_y = (row & 7) + 8 * (col & 15)
    unit = 2.0 * math.pi / (G * grid_spacing)
    signed = lambda n: jnp.where(n < G // 2, n, n - G).astype(f32) * unit
    k_x, k_y = signed(n_x), signed(n_y)
    k_z = jnp.full((128, 128), freq * unit, f32)
    edge_x = jnp.where(n_x == G // 2, 1.0, 0.0)
    edge_y = jnp.where(n_y == G // 2, 1.0, 0.0)
    edge_z = jnp.where(jnp.full((128, 128), freq, f32) < -63.5, 1.0, 0.0)
    square = k_x * k_x + k_y * k_y + k_z * k_z
    positive = square > 0.0
    safe = jnp.where(positive, square, 1.0)
    green = jnp.where(
        positive,
        (1.0 - 0.25 * square / 3.0) * (1.0 + square) * jnp.exp(-square) / safe,
        0.0,
    ) * (weight / float(G**3))
    over = green / safe
    g_xy = jnp.where(edge_x == edge_y, -over * k_x * k_y, 0.0)
    g_xz = jnp.where(edge_x == edge_z, -over * k_x * k_z, 0.0)
    g_yz = jnp.where(edge_y == edge_z, -over * k_y * k_z, 0.0)
    g_xx = green - over * k_x * k_x
    g_yy = green - over * k_y * k_y
    g_zz = green - over * k_z * k_z
    (x_re, x_im), (y_re, y_im), (z_re, z_im) = spectrum
    z_re, z_im = turn_re * z_re - turn_im * z_im, turn_re * z_im + turn_im * z_re
    flow = [
        (g_xx * x_re + g_xy * y_re + g_xz * z_re, g_xx * x_im + g_xy * y_im + g_xz * z_im),
        (g_xy * x_re + g_yy * y_re + g_yz * z_re, g_xy * x_im + g_yy * y_im + g_yz * z_im),
    ]
    w_re = g_xz * x_re + g_yz * y_re + g_zz * z_re
    w_im = g_xz * x_im + g_yz * y_im + g_zz * z_im
    flow.append((turn_re * w_re + turn_im * w_im, turn_re * w_im - turn_im * w_re))
    for c in range(3):
        mid_ref[:, 0:128], mid_ref[:, 128:256] = flow[c]
        hi, lo = split2(mid_ref[...])
        both = dot3(hi, lo, inner_back_ref[0], inner_back_ref[1])
        re, im = both[:, 0:128], both[:, 128:256]
        hi, lo = split2(
            jnp.concatenate([re * cos_t - im * sin_t, im * cos_t + re * sin_t], axis=0)
        )
        out_ref[c] = dot3(outer_back_ref[0], outer_back_ref[1], hi, lo)


def wave_flow(spec, table, member):
    special = member % 64 == 63
    freq = jnp.where(member < 64, member + 1, (member - 63) % 64)
    freq = jnp.where(member == 63, -64, freq)
    side = jnp.where(member < 64, 1.0, -1.0)
    part = jnp.stack(
        [
            freq.astype(f32),
            jnp.where(special, 1.0, 0.0),
            jnp.where(special, 0.0, side),
            jnp.where(special, 1.0, 2.0),
        ]
    ).astype(f32)
    return pl.pallas_call(
        wave_kernel,
        out_shape=jax.ShapeDtypeStruct((3, 128, 128), f32),
        in_specs=[pl.BlockSpec(memory_space=pltpu.SMEM)] + vmem(6),
        out_specs=pl.BlockSpec(memory_space=pltpu.VMEM),
        scratch_shapes=[pltpu.VMEM((128, 256), f32)],
        compiler_params=pltpu.CompilerParams(vmem_limit_bytes=VMEM_LIMIT),
        name="wave",
    )(
        part, spec, table["outer"], table["outer_back"], table["inner"],
        table["inner_back"], table["twist"],
    )


ERFC_SHIFT = 4.0
ERFC_POLY = (
    -5.9986000529477224e-05, 1.1337793270330845, 4.308175452878655, 20.093023854033866,
    -8.594175483206275, 489.91788674098177, -1701.7584635921016, 1704.126720738659,
)


def pair_scalars(s2):
    u = lax.rsqrt(s2)
    gauss = jnp.exp2(s2 * (-0.25 * math.log2(math.e)))
    t = pl.reciprocal(s2 * u + ERFC_SHIFT, approx=True)
    w = ERFC_POLY[-1]
    for coefficient in ERFC_POLY[-2::-1]:
        w = w * t + coefficient
    u2 = u * u
    wu = w * u
    along = gauss * (wu * (0.0625 * u2 + 0.375) + 0.125)
    across = (gauss * u2) * (wu * (0.375 - 0.1875 * u2) - 0.125)
    return along, across


def pair_kernel(
    near_ref, far_ref, near_out_ref, far_out_ref, steps_ref, own_ref, beside_ref,
    own_vel_ref, far_vel_ref,
    weight_ref, left_ref, right_ref, acc_ref, weight_stage, left_stage, right_stage,
    s2_a, s2_b, tile_a, tile_b,
):
    lane = lax.broadcasted_iota(jnp.int32, (1, 128), 1)

    zero = jnp.zeros((128, 128), f32)
    one = jnp.ones((128, 128), f32)
    for side, ref in ((0, own_ref), (1, beside_ref)):
        x = [ref[c] for c in range(3)]
        f = [ref[3 + c] for c in range(3)]
        xf = x[0] * f[0] + x[1] * f[1] + x[2] * f[2]
        rows = f + [xf]
        rows += [x[a] * f[b] for a in range(3) for b in range(3)]
        rows += [x[a] * xf for a in range(3)]
        rows += f
        rows += [zero] * (W_ROWS - len(rows))
        for c, plane in enumerate(rows):
            weight_stage[pl.ds(side * 128 * W_ROWS + c, 128, stride=W_ROWS), :] = plane
        norm = x[0] * x[0] + x[1] * x[1] + x[2] * x[2]
        parts = [split3(v) for v in x]
        first, second = [], []
        for h, m, l in parts:
            first += [h, h, m, m, h, l]
            second += [h, m, h, m, l, h]
        second += [one] * 3 + list(split3(norm + 0.25))
        second += [zero] * (32 - len(second))
        for c, plane in enumerate(second):
            right_stage[pl.ds(side * 128 * 32 + c, 128, stride=32), :] = plane
        if side == 0:
            first = [-2.0 * v for v in first] + list(split3(norm)) + [one] * 3
            first += [zero] * (32 - len(first))
            for c, plane in enumerate(first):
                left_stage[pl.ds(c, 128, stride=32), :] = plane

    low_half = lane < 64

    def both_halves(v):
        other = pltpu.roll(v, 64, 1)
        return jnp.where(low_half, v, other), jnp.where(low_half, other, v)

    def build(r, _):
        w = weight_stage[pl.ds(pl.multiple_of(r * W_ROWS, 8), W_ROWS), :]
        for k, v in enumerate(both_halves(w)):
            hi = v.astype(bf16).astype(f32)
            lo = v - hi
            weight_ref[2 * r + k] = jnp.concatenate(
                [hi[0:16], lo[0:16], hi[16:24], lo[16:24]], axis=0
            ).astype(bf16)
        w = right_stage[pl.ds(pl.multiple_of(r * 32, 8), 32), :]
        for k, v in enumerate(both_halves(w)):
            right_ref[2 * r + k] = v.astype(bf16)
        return 0

    lax.fori_loop(0, 256, build, 0, unroll=4)

    eye = jnp.where(
        lax.broadcasted_iota(jnp.int32, (128, 128), 0)
        == lax.broadcasted_iota(jnp.int32, (128, 128), 1),
        1.0,
        0.0,
    ).astype(bf16)

    def turn_left(r, _):
        v = left_stage[pl.ds(pl.multiple_of(r * 32, 8), 32), :].astype(bf16)
        nodes = dot_t(eye, jnp.concatenate([v] * 4, axis=0)).astype(bf16)
        left_ref[2 * r] = nodes[0:64]
        left_ref[2 * r + 1] = nodes[64:128]
        return 0

    lax.fori_loop(0, 128, turn_left, 0, unroll=4)

    def clear(r, _):
        acc_ref[pl.ds(pl.multiple_of(r * W_ROWS, 8), W_ROWS), :] = jnp.zeros((W_ROWS, 128), f32)
        return 0

    lax.fori_loop(0, 2 * BLOCKS, clear, 0, unroll=8)

    slot_mask = [jnp.where((lane >> 5) == s, 1.0, 0.0).astype(bf16) for s in range(STEP)]
    half_mask = [jnp.where((lane >> 6) == s, 1.0, 0.0).astype(bf16) for s in range(2)]
    half_keep = [(lane >> 6) == s for s in range(2)]
    blank = jnp.zeros((64, 128), bf16)

    def distances(step, s2_ref):
        at = step * STEP
        left = sum(left_ref[near_ref[at + s]] * slot_mask[s] for s in range(STEP))
        right = [right_ref[far_ref[at + s]] * half_mask[s % 2] for s in range(STEP)]
        right = jnp.concatenate(
            [
                jnp.concatenate([right[0], right[1], blank], axis=0),
                jnp.concatenate([blank, right[2], right[3]], axis=0),
            ],
            axis=1,
        )
        s2_ref[...] = dot(left, right)

    def scalars(s2_ref, tile_ref):
        along, across = pair_scalars(s2_ref[...])
        for at, value in ((0, across), (128, along)):
            hi, lo = split2(value)
            tile_ref[at : at + 64, :] = hi
            tile_ref[at + 64 : at + 128, :] = lo

    def sums(step, tile_ref):
        at = step * STEP
        for half in range(2):
            tile_h = tile_ref[0:128, half * 128 : (half + 1) * 128]
            tile_f = tile_ref[128:256, half * 128 : (half + 1) * 128]
            pairs = [at + half * 2 + s for s in range(2)]
            a = [weight_ref[near_ref[p]] for p in pairs]
            b = [weight_ref[far_ref[p]] * half_mask[s] for s, p in enumerate(pairs)]
            to_far_h = dot(jnp.concatenate([v[0:32] for v in a], axis=0), tile_h)
            to_far_f = dot(jnp.concatenate([v[32:48] for v in a], axis=0), tile_f)
            to_near_h = dot_t(jnp.concatenate([v[0:32] for v in b], axis=0), tile_h)
            to_near_f = dot_t(jnp.concatenate([v[32:48] for v in b], axis=0), tile_f)
            for s, p in enumerate(pairs):
                for h, f, out_ref, keep in (
                    (to_near_h, to_near_f, near_out_ref, None),
                    (to_far_h, to_far_f, far_out_ref, half_keep[s]),
                ):
                    add_h = h[32 * s : 32 * s + 16] + h[32 * s + 16 : 32 * s + 32]
                    add_f = f[16 * s : 16 * s + 8] + f[16 * s + 8 : 16 * s + 16]
                    add = jnp.concatenate([add_h, add_f], axis=0)
                    if keep is not None:
                        add = jnp.where(keep, add, 0.0)
                    rows = pl.ds(pl.multiple_of(out_ref[p], 8), W_ROWS)
                    acc_ref[rows, :] += add

    steps = steps_ref[0]
    distances(0, s2_a)
    scalars(s2_a, tile_a)
    distances(1, s2_b)

    def body(j, _):
        k = 2 * j + 1
        distances(k + 1, s2_a)
        scalars(s2_b, tile_b)
        sums(k - 1, tile_a)
        distances(k + 2, s2_b)
        scalars(s2_a, tile_a)
        sums(k, tile_b)
        return 0

    lax.fori_loop(0, (steps + 1) // 2, body, 0)

    chunk = 32
    for side, ref, out_ref in ((0, own_ref, own_vel_ref), (1, beside_ref, far_vel_ref)):
        for top in range(0, 128, chunk):
            base = (side * 256 + 2 * top) * W_ROWS
            planes = []
            for c in range(19):
                even = acc_ref[pl.ds(base + c, chunk, stride=2 * W_ROWS), :]
                odd = acc_ref[pl.ds(base + W_ROWS + c, chunk, stride=2 * W_ROWS), :]
                even = even + pltpu.roll(even, 64, 1)
                odd = odd + pltpu.roll(odd, 64, 1)
                planes.append(jnp.where(low_half, even, odd))
            x = [ref[c, top : top + chunk, :] for c in range(3)]
            h_f, h_xf, h_x_f, h_x_xf, along = (
                planes[0:3], planes[3], planes[4:13], planes[13:16], planes[16:19],
            )
            x_h_f = x[0] * h_f[0] + x[1] * h_f[1] + x[2] * h_f[2] - h_xf
            for c in range(3):
                out_ref[c, top : top + chunk, :] = (
                    along[c]
                    + x[c] * x_h_f
                    - (x[0] * h_x_f[3 * c] + x[1] * h_x_f[3 * c + 1] + x[2] * h_x_f[3 * c + 2])
                    + h_x_xf[c]
                )


def pair_velocities(own, beside, first_list, second_list, count):
    pad = 16
    place = jnp.arange(PAIRS, dtype=jnp.int32)
    live = place < count
    near_out = jnp.where(live, first_list, TRASH) * W_ROWS
    far_out = jnp.where(live & (first_list != second_list), second_list, TRASH) * W_ROWS
    near = jnp.pad(first_list, (0, pad))
    far = jnp.pad(second_list, (0, pad))
    near_out = jnp.pad(near_out, (0, pad), constant_values=TRASH * W_ROWS)
    far_out = jnp.pad(far_out, (0, pad), constant_values=TRASH * W_ROWS)
    steps = ((count + STEP - 1) // STEP).reshape(1)
    plane = jax.ShapeDtypeStruct((3, 128, 128), f32)
    return pl.pallas_call(
        pair_kernel,
        out_shape=[plane, plane],
        in_specs=[pl.BlockSpec(memory_space=pltpu.SMEM)] * 5 + vmem(2),
        out_specs=vmem(2),
        scratch_shapes=[
            pltpu.VMEM((2 * BLOCKS, 48, 128), bf16),
            pltpu.VMEM((BLOCKS, 64, 128), bf16),
            pltpu.VMEM((2 * BLOCKS, 32, 128), bf16),
            pltpu.VMEM(((2 * BLOCKS + 1) * W_ROWS, 128), f32),
            pltpu.VMEM((256 * W_ROWS, 128), f32),
            pltpu.VMEM((128 * 32, 128), f32),
            pltpu.VMEM((256 * 32, 128), f32),
            pltpu.VMEM((64, 256), f32),
            pltpu.VMEM((64, 256), f32),
            pltpu.VMEM((256, 256), bf16),
            pltpu.VMEM((256, 256), bf16),
        ],
        compiler_params=pltpu.CompilerParams(vmem_limit_bytes=VMEM_LIMIT),
        name="pairs",
    )(near, far, near_out, far_out, steps, own, beside)


def reply_kernel(own_ref, far_ref, wave_ref, order_ref, z_ref, out_ref, hi_ref, lo_ref):
    for c in range(3):
        kind = 0 if c < 2 else 1
        hi, lo = split2(jnp.transpose(wave_ref[c]))
        wave = dot3(hi, lo, z_ref[0, kind], z_ref[1, kind])
        fill_table(c, own_ref[c] + far_ref[c] + wave, hi_ref, lo_ref)

    def put(c, r, row):
        out_ref[c, pl.ds(r, 1), :] = row

    gather_rows(3, 128, hi_ref, lo_ref, order_ref, put)


def reply_message(own_vel, far_vel, wave, order, z_table):
    return pl.pallas_call(
        reply_kernel,
        out_shape=jax.ShapeDtypeStruct((3, 128, 128), f32),
        in_specs=vmem(5),
        out_specs=pl.BlockSpec(memory_space=pltpu.VMEM),
        scratch_shapes=[pltpu.VMEM((192, 256), bf16), pltpu.VMEM((192, 256), bf16)],
        compiler_params=pltpu.CompilerParams(vmem_limit_bytes=VMEM_LIMIT),
        name="reply",
    )(own_vel, far_vel, wave, order, z_table)


def move_kernel(in_ref, route_ref, pos_ref, noise_ref, moved_ref, drift_ref, hi_ref, lo_ref, vel_ref):
    rows = route_ref.shape[0]
    for c in range(3):
        fill_table(c, in_ref[c], hi_ref, lo_ref)

    def put(c, r, row):
        vel_ref[c, pl.ds(r, 1), :] = row

    gather_rows(3, rows, hi_ref, lo_ref, route_ref, put)
    for c in range(3):
        for r in range(rows):
            drift_ref[c : c + 1, r * 128 : (r + 1) * 128] = time_step * vel_ref[c, r : r + 1, :]
    moved_ref[...] = pos_ref[...] + drift_ref[...] + noise_ref[...]


def move_beads(arrived, route, positions, noise):
    flat = jax.ShapeDtypeStruct(positions.shape, f32)
    return pl.pallas_call(
        move_kernel,
        out_shape=[flat, flat],
        in_specs=vmem(4),
        out_specs=vmem(2),
        scratch_shapes=[
            pltpu.VMEM((192, 256), bf16),
            pltpu.VMEM((192, 256), bf16),
            pltpu.VMEM((3, 64, 128), f32),
        ],
        compiler_params=pltpu.CompilerParams(vmem_limit_bytes=VMEM_LIMIT),
        name="move",
    )(arrived, route, positions, noise)


def shifted(value, axis, by):
    devices = lax.axis_size(axis)
    return lax.ppermute(value, axis, [(i, (i + by) % devices) for i in range(devices)])


def exchange(value):
    return lax.all_to_all(value, ("gx", "gy"), split_axis=1, concat_axis=1, tiled=True)


def shards(positions, noise, route, node_perm, pair_first, pair_second, pair_count):
    table = {name: jnp.asarray(value) for name, value in tables().items()}
    row_gx = lax.axis_index("gx")
    member = row_gx * lax.axis_size("gy") + lax.axis_index("gy")
    route = route.reshape(64, 128)
    order = lax.dynamic_index_in_dim(node_perm, row_gx, 0, keepdims=False).reshape(128, 128)
    incoming = exchange(send_message(positions, route))
    grid, spec = place_on_grid(incoming, order, table["z"])
    beside = shifted(grid, "gx", -1)
    wave = exchange(wave_flow(exchange(spec), table, member))
    own_vel, far_vel = pair_velocities(
        grid, beside, pair_first[0], pair_second[0], pair_count[0]
    )
    far_vel = shifted(far_vel, "gx", 1)
    reply = exchange(reply_message(own_vel, far_vel, wave, order, table["z"]))
    return tuple(move_beads(reply, route, positions, noise))


def solution(mesh):
    in_specs = (
        P(None, ("gx", "gy")),
        P(None, ("gx", "gy")),
        P(("gx", "gy")),
        P(None, "gy", None),
        P(("gx", "gy"), None),
        P(("gx", "gy"), None),
        P(("gx", "gy")),
    )
    out_specs = (P(None, ("gx", "gy")), P(None, ("gx", "gy")))
    return jax.shard_map(shards, mesh=mesh, in_specs=in_specs, out_specs=out_specs, check_vma=False)
```

time: 941 us -> 211 us (0.22)
  local copies, waits for them, and re-layouts: 442 us -> 14 us
  other arithmetic: 376 us -> 0.59 us
  Pallas kernels: 0 us -> 99.7 us
  blocking collectives: 0 us -> 62.9 us
  matrix products: 41.7 us -> 0 us
  starting transfers between devices: 49.8 us -> 18.9 us
    gather x36 -> x0, local copies, waits for them, and re-layouts: 248 us -> none  [the longest x1 57.8 us: shards(): back_msg = own_vel[:, own_order].reshape(3, devices, per_peer)]
    reduce_sum x17 -> x0, other arithmetic: 211 us -> none  [the longest x16 211 us: tile_pairs(): jnp.sum(along_part * near_force[channel][:, :, None] + onto_near * offset...]
    pallas_call x0 -> x6, Pallas kernels: none -> 99.7 us  [the longest x1 51 us: pair_velocities(): pl.pallas_call(pair_kernel, out_shape=[plane, plane], in_specs=[pl.BlockS...]
    scatter-add x32 -> x0, other arithmetic: 87.6 us -> none  [the longest x16 43.8 us: turn(): velocity_sum.at[:, near_idx].add(near_vel * live_mask[None, :, None])]
    scatter x3 -> x0, local copies, waits for them, and re-layouts: 75.4 us -> none  [the longest x2 50.9 us: shards(): jnp.zeros((6, slots), jnp.float32).at[:, own_order]]
    all_to_all x0 -> x2, blocking collectives: none -> 62.9 us  [exchange(): lax.all_to_all(value, ('gx', 'gy'), split_axis=1, concat_axis=1, tiled=True)]
    reshape x11 -> x0, local copies, waits for them, and re-layouts: 42.4 us -> none  [the longest x1 6.61 us: shards(): grid_data.reshape(6, blocks, CELL)]
    dot_general x20 -> x0, matrix products: 41.7 us -> none  [the longest x2 5.41 us: forward_pass(): contract(form, real_in, cos_part) + contract(form, imag_in, sin_part)]
  transfers between devices with their start and end apart: 8 -> 4, of which waited for: 3 -> 1; matrix products, arithmetic and copies ran while one was open for 72% -> 4% of each run, Pallas kernels for 0% -> 26%
where the time goes in v1:
time: 211 us; the launch traced here: 210 us
  Pallas kernels  99.7 us (47%)
  blocking collectives  62.9 us (30%)
  starting transfers between devices  18.9 us (9%)
  local copies, waits for them, and re-layouts  14 us (7%)
  waiting for transfers between devices  12.9 us (6%)
    all_to_all x2, blocking collectives, exchange(): lax.all_to_all(value, ('gx', 'gy'), split_axis=1, concat_axis=1, tiled=True)  62.9 us
    pallas_call x1, Pallas kernels, pair_velocities(): pl.pallas_call(pair_kernel, out_shape=[plane, plane], in_specs=[pl.BlockS...  51 us
    pallas_call x1, Pallas kernels, reply_message(): pl.pallas_call(reply_kernel, out_shape=jax.ShapeDtypeStruct((3, 128, 128)...  16.5 us
    all_to_all x2, starting transfers between devices, exchange(): lax.all_to_all(value, ('gx', 'gy'), split_axis=1, concat_axis=1, tiled=True)  16.4 us
    all_to_all x2, waiting for transfers between devices, exchange(): lax.all_to_all(value, ('gx', 'gy'), split_axis=1, concat_axis=1, tiled=True)  12.9 us
    pallas_call x1, Pallas kernels, place_on_grid(): pl.pallas_call(place_kernel, out_shape=[jax.ShapeDtypeStruct((6, 128, 128...  12.5 us
    pallas_call x1, Pallas kernels, move_beads(): pl.pallas_call(move_kernel, out_shape=[flat, flat], in_specs=vmem(4), out...  9.08 us
    pallas_call x1, Pallas kernels, send_message(): pl.pallas_call(send_kernel, out_shape=jax.ShapeDtypeStruct((6, 128, 128),...  7.37 us
  transfers between devices with their start and end apart: 4, of which 1 were waited for; matrix products, arithmetic and copies ran while one was open for 4% of the time, Pallas kernels for 26%

profile of v1, /device:TPU:1, one launch (start us, length us, event | category | flops | bytes accessed | tf_op | source)
XLA Modules:
  0.0 210.3 jit_solution(3685356379370287779)
XLA Ops:
  0.6 0.0 copy-start
  0.6 7.4 %send.1 = f32[6,128,128]{2,1,0:T(8,128)} custom-call(f32[3,8192]{1,0:T(4,128)} %pos_ref.3, s32[64,128]{1,0:T(8,128)} %bitcast.14), custom_call_target="tpu_custom_call" | custom-call | tf_op jit(solution)/shard_map/send/pallas_call | solution.py:203
  8.0 2.0 copy.15
  10.0 11.5 %all-to-all-start = ((f32[6,128,128]{2,0,1:T(8,128)}), f32[6,128,128]{2,0,1:T(8,128)S(1)}, u32[]{:S(2)}, u32[]{:S(2)}) async-start(f32[6,128,128]{2,0,1:T(8,128)} %copy.15), calls=%async_computation | async-start | bytes 1048576 | tf_op jit(solution)/shard_map/all_to_all | solution.py:624
  21.6 0.6 constant_dynamic-slice_fusion
  22.2 12.9 %all-to-all-done = f32[6,128,128]{2,0,1:T(8,128)S(1)} async-done(((f32[6,128,128]{2,0,1:T(8,128)}), f32[6,128,128]{2,0,1:T(8,128)S(1)}, u32[]{:S(2)}, u32[]{:S(2)}) %all-to-all-start) | async-done | bytes 393248 | tf_op jit(solution)/shard_map/all_to_all | solution.py:624
  35.1 0.8 copy.16.in_ref
  35.9 12.5 %place.1 = (f32[6,128,128]{2,1,0:T(8,128)}, f32[3,128,128]{2,1,0:T(8,128)}) custom-call(f32[6,128,128]{2,1,0:T(8,128)} %copy.16.in_ref, s32[128,128]{1,0:T(8,128)} %bitcast.12, bf16[2,2,128,128]{3,2,1,0:T(8,128)(2,1)} %constant.83.clone.z_ref), custom_call_target="tpu_custom_call" | custom-call | tf_op jit(solution)/shard_map/place/pallas_call | solution.py:230
  48.4 1.1 collective-permute-start
  50.1 1.8 copy.17
  51.9 4.9 %all-to-all-start.1 = ((f32[3,128,128]{2,0,1:T(4,128)}), f32[3,128,128]{2,0,1:T(4,128)S(1)}, u32[]{:S(2)}, u32[]{:S(2)}) async-start(f32[3,128,128]{2,0,1:T(4,128)} %copy.17), calls=%async_computation.1 | async-start | bytes 524288 | tf_op jit(solution)/shard_map/all_to_all | solution.py:624
  56.9 0.0 copy-start.3
  56.9 0.7 copy-done.3
  57.6 0.6 pad.13.near_ref
  58.2 0.6 pad.14.far_ref
  58.8 0.6 pad.16.far_out_ref
  59.4 0.6 pad.15.near_out_ref
  60.0 0.7 copy-done.1
  60.7 51.0 %pairs.1 = (f32[3,128,128]{2,1,0:T(8,128)}, f32[3,128,128]{2,1,0:T(8,128)}) custom-call(s32[1040]{0:T(1024)} %pad.13.near_ref, s32[1040]{0:T(1024)} %pad.14.far_ref, s32[1040]{0:T(1024)} %pad.15.near_out_ref, s32[1040]{0:T(1024)} %pad.16.far_out_ref, s32[1]{0:T(128)} %bitcast.3.steps_ref, f32[6,128,128]{2,1,0:T(8,128)} %get-tuple-element.6.own_ref, ...), custom_call_target="tpu_custom_call" | custom-call | tf_op jit(solution)/shard_map/pairs/pallas_call | solution.py:538
  111.7 1.4 collective-permute-start.1
  113.1 0.6 pad_maximum_fusion.part_ref
  113.7 0.7 copy.18.in_ref
  114.4 3.3 %wave.1 = f32[3,128,128]{2,1,0:T(8,128)} custom-call(f32[4]{0:T(128)} %pad_maximum_fusion.part_ref, f32[3,128,128]{2,1,0:T(8,128)} %copy.18.in_ref, bf16[2,256,128]{2,1,0:T(8,128)(2,1)} %constant.84.clone.outer_ref, bf16[2,128,256]{2,1,0:T(8,128)(2,1)} %constant.85.clone.outer_back_ref, bf16[2,256,256]{2,1,0:T(8,128)(2,1)} %constant.86.clone.inner_ref, ...), custom_call_target="tpu_custom_call" | custom-call | tf_op jit(solution)/shard_map/wave/pallas_call | solution.py:319
  117.6 1.1 copy.19
  118.7 47.7 %all_to_all.20 = f32[3,128,128]{2,0,1:T(4,128)S(1)} all-to-all(f32[3,128,128]{2,0,1:T(4,128)S(1)} %copy.19), channel_id=1, replica_groups=mesh['gx'=16,'gy'=8] {'gx','gy'}, dimensions={1} | all-to-all | bytes 393216 | tf_op jit(solution)/shard_map/all_to_all | solution.py:624
  166.4 0.7 copy.20.wave_ref
  167.1 0.7 copy-done.2
  167.8 16.5 %reply.1 = f32[3,128,128]{2,1,0:T(8,128)} custom-call(f32[3,128,128]{2,1,0:T(8,128)} %get-tuple-element.7.own_ref, f32[3,128,128]{2,1,0:T(8,128)} %copy-done.2, f32[3,128,128]{2,1,0:T(8,128)} %copy.20.wave_ref, s32[128,128]{1,0:T(8,128)} %bitcast.13, bf16[2,2,128,128]{3,2,1,0:T(8,128)(2,1)} %constant.83.clone.z_ref), custom_call_target="tpu_custom_call" | custom-call | tf_op jit(solution)/shard_map/reply/pallas_call | solution.py:575
  184.3 1.1 copy.21
  185.3 15.2 %all_to_all.21 = f32[3,128,128]{2,0,1:T(4,128)S(1)} all-to-all(f32[3,128,128]{2,0,1:T(4,128)S(1)} %copy.21), channel_id=1, replica_groups=mesh['gx'=16,'gy'=8] {'gx','gy'}, dimensions={1} | all-to-all | bytes 393216 | tf_op jit(solution)/shard_map/all_to_all | solution.py:624
  200.5 0.7 copy.22.in_ref
  201.2 9.1 %move.1 = (f32[3,8192]{1,0:T(4,128)}, f32[3,8192]{1,0:T(4,128)}) custom-call(f32[3,128,128]{2,1,0:T(8,128)} %copy.22.in_ref, s32[64,128]{1,0:T(8,128)} %bitcast.15, f32[3,8192]{1,0:T(4,128)} %pos_ref.3, f32[3,8192]{1,0:T(4,128)} %noise_ref.1), custom_call_target="tpu_custom_call" | custom-call | tf_op jit(solution)/shard_map/move/pallas_call | solution.py:603
  (9 shorter events, 0.0 us)
Async XLA Ops:
  0.6 20.9 %copy-start = (s32[16,1,16384]{2,1,0:T(1,128)S(1)}, s32[16,1,16384]{2,1,0:T(1,128)}, u32[]{:S(2)}) copy-start(s32[16,1,16384]{2,1,0:T(1,128)} %param.16) | copy-start | bytes 3145732
  10.0 25.0 %all-to-all-start = ((f32[6,128,128]{2,0,1:T(8,128)}), f32[6,128,128]{2,0,1:T(8,128)S(1)}, u32[]{:S(2)}, u32[]{:S(2)}) async-start(f32[6,128,128]{2,0,1:T(8,128)} %copy.15), calls=%async_computation | async-start | bytes 1048576 | tf_op jit(solution)/shard_map/all_to_all | solution.py:624
  48.4 11.5 %collective-permute-start = (f32[6,128,128]{2,1,0:T(8,128)}, f32[6,128,128]{2,1,0:T(8,128)S(1)}, u32[]{:S(2)}, u32[]{:S(2)}) collective-permute-start(f32[6,128,128]{2,1,0:T(8,128)} %get-tuple-element.6.own_ref), channel_id=1, source_target_pairs={{0,120},{8,0},{16,8},{24,16},{32,24},{40,32},{48,40},{56,48},{64,5... | collective-permute-start | bytes 1179656 | tf_op jit(solution)/shard_map/ppermute | solution.py:620
  51.9 5.0 %copy-start.4 = (s32[1,1024]{1,0:T(1,128)S(1)}, s32[1,1024]{1,0:T(1,128)}, u32[]{:S(2)}) copy-start(s32[1,1024]{1,0:T(1,128)} %param.18) | copy-start | bytes 12292
  51.9 61.8 %all-to-all-start.1 = ((f32[3,128,128]{2,0,1:T(4,128)}), f32[3,128,128]{2,0,1:T(4,128)S(1)}, u32[]{:S(2)}, u32[]{:S(2)}) async-start(f32[3,128,128]{2,0,1:T(4,128)} %copy.17), calls=%async_computation.1 | async-start | bytes 524288 | tf_op jit(solution)/shard_map/all_to_all | solution.py:624
  56.9 0.7 copy-start.3
  59.9 0.7 copy-start.1
  111.7 55.4 %collective-permute-start.1 = (f32[3,128,128]{2,1,0:T(8,128)}, f32[3,128,128]{2,1,0:T(8,128)S(1)}, u32[]{:S(2)}, u32[]{:S(2)}) collective-permute-start(f32[3,128,128]{2,1,0:T(8,128)} %get-tuple-element.8), channel_id=1, source_target_pairs={{0,8},{8,16},{16,24},{24,32},{32,40},{40,48},{48,56},{56,64},{64,7... | collective-permute-start | bytes 589832 | tf_op jit(solution)/shard_map/ppermute | solution.py:620
  167.1 0.7 copy-start.2

commit v2 on v1

--- a/solution.py
+++ b/solution.py
@@ -14,7 +14,8 @@
 PAIRS = 1024
 STEP = 4
 W_ROWS = 24
-TRASH = 2 * BLOCKS
+GROUPS = 2
+FEATURES = 24
 
 fene_k = 30.0
 fene_reach = 1.5
@@ -24,7 +25,8 @@
 
 f32 = jnp.float32
 bf16 = jnp.bfloat16
-VMEM_LIMIT = 60 * 1024 * 1024
+VMEM_LIMIT = 24 * 1024 * 1024
+SMALL_VMEM = 24 * 1024 * 1024
 
 
 def dot(a, b):
@@ -86,6 +88,10 @@
     }
 
 
+def cost(micros):
+    return pl.CostEstimate(flops=int(micros * 1e9), bytes_accessed=1 << 20, transcendentals=0)
+
+
 def onehot(index, size, width):
     rows = lax.broadcasted_iota(jnp.int32, (size, width), 0)
     return jnp.where(rows == index, 1.0, 0.0).astype(bf16)
@@ -125,25 +131,27 @@
 
 
 def gather_rows(channels, rows, table_hi_ref, table_lo_ref, place_ref, put):
+    width = 4
+
     def turn(g, _):
         low, high = [], []
-        for j in range(2):
-            place = place_ref[pl.ds(g * 2 + j, 1), :]
+        for j in range(width):
+            place = place_ref[pl.ds(g * width + j, 1), :]
             low.append(onehot(low_part(place), 256, 128))
             high.append(high_part(place))
         low = jnp.concatenate(low, axis=1)
         high = jnp.concatenate(high, axis=1)
         found = dot(table_hi_ref[...], low) + dot(table_lo_ref[...], low)
-        rows_of = lax.broadcasted_iota(jnp.int32, (64, 256), 0) == high
+        rows_of = lax.broadcasted_iota(jnp.int32, (64, width * 128), 0) == high
         for c in range(channels):
             got = jnp.sum(
                 jnp.where(rows_of, found[c * 64 : (c + 1) * 64], 0.0), axis=0, keepdims=True
             )
-            for j in range(2):
-                put(c, g * 2 + j, got[:, j * 128 : (j + 1) * 128])
+            for j in range(width):
+                put(c, g * width + j, got[:, j * 128 : (j + 1) * 128])
         return 0
 
-    lax.fori_loop(0, rows // 2, turn, 0)
+    lax.fori_loop(0, rows // width, turn, 0)
 
 
 def fill_table(c, plane, table_hi_ref, table_lo_ref):
@@ -191,8 +199,8 @@
         6, rows, lambda c, r: plane_ref[c, pl.ds(r, 1), :], route_ref, left_ref, sum_ref
     )
     for c in range(6):
-        out_ref[c, 0:64, :] = sum_ref[c * 64 : (c + 1) * 64, 0:128]
-        out_ref[c, 64:128, :] = sum_ref[c * 64 : (c + 1) * 64, 128:256]
+        out_ref[0:64, c, :] = sum_ref[c * 64 : (c + 1) * 64, 0:128]
+        out_ref[64:128, c, :] = sum_ref[c * 64 : (c + 1) * 64, 128:256]
 
 
 def vmem(n):
@@ -202,7 +210,7 @@
 def send_message(positions, route):
     return pl.pallas_call(
         send_kernel,
-        out_shape=jax.ShapeDtypeStruct((6, 128, 128), f32),
+        out_shape=jax.ShapeDtypeStruct((128, 6, 128), f32),
         in_specs=vmem(2),
         out_specs=pl.BlockSpec(memory_space=pltpu.VMEM),
         scratch_shapes=[
@@ -216,14 +224,14 @@
 
 
 def place_kernel(in_ref, order_ref, z_ref, out_ref, spec_ref, left_ref, sum_ref):
-    scatter_rows(6, 128, lambda c, r: in_ref[c, pl.ds(r, 1), :], order_ref, left_ref, sum_ref)
+    scatter_rows(6, 128, lambda c, r: in_ref[r, c : c + 1, :], order_ref, left_ref, sum_ref)
     for c in range(6):
         out_ref[c, 0:64, :] = sum_ref[c * 64 : (c + 1) * 64, 0:128]
         out_ref[c, 64:128, :] = sum_ref[c * 64 : (c + 1) * 64, 128:256]
     for c in range(3):
         hi, lo = split2(out_ref[3 + c])
         kind = 0 if c < 2 else 1
-        spec_ref[c] = dot3(z_ref[0, kind], z_ref[1, kind], hi, lo, dot_t)
+        spec_ref[:, c, :] = dot3(z_ref[0, kind], z_ref[1, kind], hi, lo, dot_t)
 
 
 def place_on_grid(incoming, order, z_table):
@@ -231,7 +239,7 @@
         place_kernel,
         out_shape=[
             jax.ShapeDtypeStruct((6, 128, 128), f32),
-            jax.ShapeDtypeStruct((3, 128, 128), f32),
+            jax.ShapeDtypeStruct((128, 3, 128), f32),
         ],
         in_specs=vmem(3),
         out_specs=vmem(2),
@@ -249,7 +257,7 @@
     cos_t, sin_t = twist_ref[0], twist_ref[1]
     spectrum = []
     for c in range(3):
-        hi, lo = split2(in_ref[c])
+        hi, lo = split2(in_ref[:, c, :])
         both = dot3(outer_ref[0], outer_ref[1], hi, lo)
         re, im = both[0:128], both[128:256]
         mid_ref[:, 0:128] = re * cos_t + im * sin_t
@@ -300,7 +308,7 @@
         hi, lo = split2(
             jnp.concatenate([re * cos_t - im * sin_t, im * cos_t + re * sin_t], axis=0)
         )
-        out_ref[c] = dot3(outer_back_ref[0], outer_back_ref[1], hi, lo)
+        out_ref[:, c, :] = dot3(outer_back_ref[0], outer_back_ref[1], hi, lo)
 
 
 def wave_flow(spec, table, member):
@@ -318,7 +326,7 @@
     ).astype(f32)
     return pl.pallas_call(
         wave_kernel,
-        out_shape=jax.ShapeDtypeStruct((3, 128, 128), f32),
+        out_shape=jax.ShapeDtypeStruct((128, 3, 128), f32),
         in_specs=[pl.BlockSpec(memory_space=pltpu.SMEM)] + vmem(6),
         out_specs=pl.BlockSpec(memory_space=pltpu.VMEM),
         scratch_shapes=[pltpu.VMEM((128, 256), f32)],
@@ -351,149 +359,232 @@
     return along, across
 
 
-def pair_kernel(
-    near_ref, far_ref, near_out_ref, far_out_ref, steps_ref, own_ref, beside_ref,
-    own_vel_ref, far_vel_ref,
-    weight_ref, left_ref, right_ref, acc_ref, weight_stage, left_stage, right_stage,
-    s2_a, s2_b, tile_a, tile_b,
+def both_halves(v):
+    low_half = lax.broadcasted_iota(jnp.int32, (1, 128), 1) < 64
+    other = pltpu.roll(v, 64, 1)
+    return jnp.where(low_half, v, other), jnp.where(low_half, other, v)
+
+
+def stage_nodes(ref, weight_stage, right_stage):
+    x = [ref[c] for c in range(3)]
+    f = [ref[3 + c] for c in range(3)]
+    xf = x[0] * f[0] + x[1] * f[1] + x[2] * f[2]
+    rows = f + [xf]
+    rows += [x[a] * f[b] for a in range(3) for b in range(3)]
+    rows += [x[a] * xf for a in range(3)]
+    for c, plane in enumerate(rows):
+        weight_stage[pl.ds(c, 128, stride=16), :] = plane
+    norm = x[0] * x[0] + x[1] * x[1] + x[2] * x[2]
+    first, second = [], []
+    for h, m, l in [split3(v) for v in x]:
+        first += [h, h, m, m, h, l]
+        second += [h, m, h, m, l, h]
+    one = jnp.ones((128, 128), f32)
+    first = [-2.0 * v for v in first] + list(split3(norm)) + [one] * 3
+    second += [one] * 3 + list(split3(norm + 0.25))
+    for c, plane in enumerate(second):
+        right_stage[pl.ds(c, 128, stride=FEATURES), :] = plane
+    return first
+
+
+def build_tables(base, weight_stage, right_stage, weight_ref, right_ref):
+    blank = jnp.zeros((32 - FEATURES, 128), f32)
+
+    def build(r, _):
+        w = weight_stage[pl.ds(pl.multiple_of(r * 16, 8), 16), :]
+        for k, v in enumerate(both_halves(w)):
+            hi = v.astype(bf16)
+            lo = (v - hi.astype(f32)).astype(bf16)
+            weight_ref[base + 2 * r + k] = jnp.concatenate([hi, lo], axis=0)
+        w = right_stage[pl.ds(pl.multiple_of(r * FEATURES, 8), FEATURES), :]
+        for k, v in enumerate(both_halves(w)):
+            right_ref[base + 2 * r + k] = jnp.concatenate([v, blank], axis=0).astype(bf16)
+        return 0
+
+    lax.fori_loop(0, 128, build, 0, unroll=16)
+
+
+def own_tables_kernel(
+    own_ref, weight_ref, right_ref, left_ref, weight_stage, right_stage, left_stage
 ):
-    lane = lax.broadcasted_iota(jnp.int32, (1, 128), 1)
-
-    zero = jnp.zeros((128, 128), f32)
-    one = jnp.ones((128, 128), f32)
-    for side, ref in ((0, own_ref), (1, beside_ref)):
-        x = [ref[c] for c in range(3)]
-        f = [ref[3 + c] for c in range(3)]
-        xf = x[0] * f[0] + x[1] * f[1] + x[2] * f[2]
-        rows = f + [xf]
-        rows += [x[a] * f[b] for a in range(3) for b in range(3)]
-        rows += [x[a] * xf for a in range(3)]
-        rows += f
-        rows += [zero] * (W_ROWS - len(rows))
-        for c, plane in enumerate(rows):
-            weight_stage[pl.ds(side * 128 * W_ROWS + c, 128, stride=W_ROWS), :] = plane
-        norm = x[0] * x[0] + x[1] * x[1] + x[2] * x[2]
-        parts = [split3(v) for v in x]
-        first, second = [], []
-        for h, m, l in parts:
-            first += [h, h, m, m, h, l]
-            second += [h, m, h, m, l, h]
-        second += [one] * 3 + list(split3(norm + 0.25))
-        second += [zero] * (32 - len(second))
-        for c, plane in enumerate(second):
-            right_stage[pl.ds(side * 128 * 32 + c, 128, stride=32), :] = plane
-        if side == 0:
-            first = [-2.0 * v for v in first] + list(split3(norm)) + [one] * 3
-            first += [zero] * (32 - len(first))
-            for c, plane in enumerate(first):
-                left_stage[pl.ds(c, 128, stride=32), :] = plane
-
-    low_half = lane < 64
-
-    def both_halves(v):
-        other = pltpu.roll(v, 64, 1)
-        return jnp.where(low_half, v, other), jnp.where(low_half, other, v)
-
-    def build(r, _):
-        w = weight_stage[pl.ds(pl.multiple_of(r * W_ROWS, 8), W_ROWS), :]
-        for k, v in enumerate(both_halves(w)):
-            hi = v.astype(bf16).astype(f32)
-            lo = v - hi
-            weight_ref[2 * r + k] = jnp.concatenate(
-                [hi[0:16], lo[0:16], hi[16:24], lo[16:24]], axis=0
-            ).astype(bf16)
-        w = right_stage[pl.ds(pl.multiple_of(r * 32, 8), 32), :]
-        for k, v in enumerate(both_halves(w)):
-            right_ref[2 * r + k] = v.astype(bf16)
-        return 0
-
-    lax.fori_loop(0, 256, build, 0, unroll=4)
-
+    first = stage_nodes(own_ref, weight_stage, right_stage)
+    for c, plane in enumerate(first):
+        left_stage[pl.ds(c, 128, stride=FEATURES), :] = plane
     eye = jnp.where(
         lax.broadcasted_iota(jnp.int32, (128, 128), 0)
         == lax.broadcasted_iota(jnp.int32, (128, 128), 1),
         1.0,
         0.0,
     ).astype(bf16)
+    blank = jnp.zeros((32 - FEATURES, 128), f32)
 
     def turn_left(r, _):
-        v = left_stage[pl.ds(pl.multiple_of(r * 32, 8), 32), :].astype(bf16)
+        v = left_stage[pl.ds(pl.multiple_of(r * FEATURES, 8), FEATURES), :]
+        v = jnp.concatenate([v, blank], axis=0).astype(bf16)
         nodes = dot_t(eye, jnp.concatenate([v] * 4, axis=0)).astype(bf16)
         left_ref[2 * r] = nodes[0:64]
         left_ref[2 * r + 1] = nodes[64:128]
         return 0
 
-    lax.fori_loop(0, 128, turn_left, 0, unroll=4)
+    lax.fori_loop(0, 128, turn_left, 0, unroll=8)
+    build_tables(0, weight_stage, right_stage, weight_ref, right_ref)
+
+
+def beside_tables_kernel(
+    beside_ref, weight_in, right_in, weight_ref, right_ref, weight_stage, right_stage
+):
+    stage_nodes(beside_ref, weight_stage, right_stage)
+    build_tables(BLOCKS, weight_stage, right_stage, weight_ref, right_ref)
+
+
+WEIGHT_TABLE = jax.ShapeDtypeStruct((2 * BLOCKS, 32, 128), bf16)
+RIGHT_TABLE = jax.ShapeDtypeStruct((2 * BLOCKS, 32, 128), bf16)
+LEFT_TABLE = jax.ShapeDtypeStruct((BLOCKS, 64, 128), bf16)
+
+
+def own_tables(own):
+    return pl.pallas_call(
+        own_tables_kernel,
+        out_shape=[WEIGHT_TABLE, RIGHT_TABLE, LEFT_TABLE],
+        in_specs=vmem(1),
+        out_specs=vmem(3),
+        scratch_shapes=[
+            pltpu.VMEM((128 * 16, 128), f32),
+            pltpu.VMEM((128 * FEATURES, 128), f32),
+            pltpu.VMEM((128 * FEATURES, 128), f32),
+        ],
+        compiler_params=pltpu.CompilerParams(vmem_limit_bytes=SMALL_VMEM),
+        cost_estimate=cost(8),
+        name="own_tables",
+    )(own)
+
+
+def beside_tables(beside, weight, right):
+    return pl.pallas_call(
+        beside_tables_kernel,
+        out_shape=[WEIGHT_TABLE, RIGHT_TABLE],
+        in_specs=vmem(1) + [pl.BlockSpec(memory_space=pl.ANY)] * 2,
+        out_specs=vmem(2),
+        input_output_aliases={1: 0, 2: 1},
+        scratch_shapes=[
+            pltpu.VMEM((128 * 16, 128), f32),
+            pltpu.VMEM((128 * FEATURES, 128), f32),
+        ],
+        compiler_params=pltpu.CompilerParams(vmem_limit_bytes=SMALL_VMEM),
+        cost_estimate=cost(4),
+        name="beside_tables",
+    )(beside, weight, right)
+
+
+def pair_kernel(
+    list_ref, count_ref, weight_ref, right_ref, left_ref, own_ref, beside_ref,
+    own_vel_ref, far_vel_ref, near_acc, far_acc, s2_a, s2_b, tile_a, tile_b,
+):
+    lane = lax.broadcasted_iota(jnp.int32, (1, 128), 1)
+    low_half = lane < 64
+    count = count_ref[0]
 
     def clear(r, _):
-        acc_ref[pl.ds(pl.multiple_of(r * W_ROWS, 8), W_ROWS), :] = jnp.zeros((W_ROWS, 128), f32)
+        blank = jnp.zeros((W_ROWS, 128), f32)
+        far_acc[pl.ds(pl.multiple_of(r * 2 * W_ROWS, 8), W_ROWS), :] = blank
+        far_acc[pl.ds(pl.multiple_of(r * 2 * W_ROWS + W_ROWS, 8), W_ROWS), :] = blank
+        near_acc[pl.ds(pl.multiple_of(r * W_ROWS, 8), W_ROWS), :] = blank
         return 0
 
-    lax.fori_loop(0, 2 * BLOCKS, clear, 0, unroll=8)
-
-    slot_mask = [jnp.where((lane >> 5) == s, 1.0, 0.0).astype(bf16) for s in range(STEP)]
-    half_mask = [jnp.where((lane >> 6) == s, 1.0, 0.0).astype(bf16) for s in range(2)]
+    lax.fori_loop(0, BLOCKS, clear, 0, unroll=8)
+
+    wide = lax.broadcasted_iota(jnp.int32, (64, 128), 1)
+    wide_low = wide < 64
+    wide_even = (wide & 32) == 0
+    narrow = lax.broadcasted_iota(jnp.int32, (32, 128), 1) < 64
+    nothing = jnp.zeros((32, 128), bf16)
+
+    def half_of(v, half):
+        return jnp.where(narrow, nothing, v) if half else jnp.where(narrow, v, nothing)
+
     half_keep = [(lane >> 6) == s for s in range(2)]
     blank = jnp.zeros((64, 128), bf16)
 
-    def distances(step, s2_ref):
-        at = step * STEP
-        left = sum(left_ref[near_ref[at + s]] * slot_mask[s] for s in range(STEP))
-        right = [right_ref[far_ref[at + s]] * half_mask[s % 2] for s in range(STEP)]
-        right = jnp.concatenate(
-            [
-                jnp.concatenate([right[0], right[1], blank], axis=0),
-                jnp.concatenate([blank, right[2], right[3]], axis=0),
-            ],
-            axis=1,
-        )
-        s2_ref[...] = dot(left, right)
-
-    def scalars(s2_ref, tile_ref):
-        along, across = pair_scalars(s2_ref[...])
+    def blocks_of(pair):
+        return list_ref[0, pair], list_ref[1, pair]
+
+    def distance_dots(step):
+        found = []
+        for g in range(GROUPS):
+            pairs = [blocks_of((step * GROUPS + g) * STEP + s) for s in range(STEP)]
+            left = [left_ref[pairs[s][0]] for s in range(STEP)]
+            left = jnp.where(
+                wide_low,
+                jnp.where(wide_even, left[0], left[1]),
+                jnp.where(wide_even, left[2], left[3]),
+            )
+            right = [half_of(right_ref[pairs[s][1]], s % 2) for s in range(STEP)]
+            right = jnp.concatenate(
+                [
+                    jnp.concatenate([right[0], right[1], blank], axis=0),
+                    jnp.concatenate([blank, right[2], right[3]], axis=0),
+                ],
+                axis=1,
+            )
+            found.append(dot(left, right))
+        return found
+
+    def scalars(s2_ref, tile_ref, pack):
+        half = pack % 2
+        along, across = pair_scalars(s2_ref[pack // 2, :, half * 128 : (half + 1) * 128])
         for at, value in ((0, across), (128, along)):
             hi, lo = split2(value)
-            tile_ref[at : at + 64, :] = hi
-            tile_ref[at + 64 : at + 128, :] = lo
-
-    def sums(step, tile_ref):
-        at = step * STEP
-        for half in range(2):
-            tile_h = tile_ref[0:128, half * 128 : (half + 1) * 128]
-            tile_f = tile_ref[128:256, half * 128 : (half + 1) * 128]
-            pairs = [at + half * 2 + s for s in range(2)]
-            a = [weight_ref[near_ref[p]] for p in pairs]
-            b = [weight_ref[far_ref[p]] * half_mask[s] for s, p in enumerate(pairs)]
-            to_far_h = dot(jnp.concatenate([v[0:32] for v in a], axis=0), tile_h)
-            to_far_f = dot(jnp.concatenate([v[32:48] for v in a], axis=0), tile_f)
-            to_near_h = dot_t(jnp.concatenate([v[0:32] for v in b], axis=0), tile_h)
-            to_near_f = dot_t(jnp.concatenate([v[32:48] for v in b], axis=0), tile_f)
-            for s, p in enumerate(pairs):
-                for h, f, out_ref, keep in (
-                    (to_near_h, to_near_f, near_out_ref, None),
-                    (to_far_h, to_far_f, far_out_ref, half_keep[s]),
-                ):
-                    add_h = h[32 * s : 32 * s + 16] + h[32 * s + 16 : 32 * s + 32]
-                    add_f = f[16 * s : 16 * s + 8] + f[16 * s + 8 : 16 * s + 16]
-                    add = jnp.concatenate([add_h, add_f], axis=0)
-                    if keep is not None:
-                        add = jnp.where(keep, add, 0.0)
-                    rows = pl.ds(pl.multiple_of(out_ref[p], 8), W_ROWS)
-                    acc_ref[rows, :] += add
-
-    steps = steps_ref[0]
-    distances(0, s2_a)
-    scalars(s2_a, tile_a)
-    distances(1, s2_b)
+            tile_ref[pack, at : at + 64, :] = hi
+            tile_ref[pack, at + 64 : at + 128, :] = lo
+
+    def sum_dots(step, tile_ref, pack):
+        tile = tile_ref[pack]
+        pairs = [blocks_of((step * 2 * GROUPS + pack) * 2 + s) for s in range(2)]
+        a = jnp.concatenate([weight_ref[i] for i, _ in pairs], axis=0)
+        b = jnp.concatenate(
+            [half_of(weight_ref[j], s) for s, (_, j) in enumerate(pairs)], axis=0
+        )
+        to_far = dot(a, jnp.concatenate([tile[0:128], tile[128:256]], axis=1))
+        return dot_t(b, tile), to_far
+
+    def add_sums(step, pack, to_near, to_far):
+        for s in range(2):
+            number = (step * 2 * GROUPS + pack) * 2 + s
+            for out, acc_ref, row, keep in (
+                (to_near, near_acc, list_ref[2, number], None),
+                (to_far, far_acc, list_ref[3, number], half_keep[s]),
+            ):
+                top = 32 * s
+                add_h = out[top : top + 16, 0:128] + out[top + 16 : top + 32, 0:128]
+                add_f = out[top : top + 8, 128:256] + out[top + 16 : top + 24, 128:256]
+                add = jnp.concatenate([add_h, add_f], axis=0)
+                if keep is not None:
+                    add = jnp.where(keep, add, 0.0)
+                acc_ref[pl.ds(pl.multiple_of(row, 8), W_ROWS), :] += add
+
+    packs = range(2 * GROUPS)
+
+    def keep_distances(found, s2_ref):
+        for g in range(GROUPS):
+            s2_ref[g] = found[g]
+
+    def stage(k, s2_next, s2_now, tile_now, tile_last):
+        for pack in packs:
+            scalars(s2_now, tile_now, pack)
+        for pack in packs:
+            add_sums(k - 1, pack, *sum_dots(k - 1, tile_last, pack))
+        keep_distances(distance_dots(k + 1), s2_next)
+
+    steps = (count + (STEP * GROUPS - 1)) // (STEP * GROUPS)
+    keep_distances(distance_dots(0), s2_a)
+    for pack in packs:
+        scalars(s2_a, tile_a, pack)
+    keep_distances(distance_dots(1), s2_b)
 
     def body(j, _):
         k = 2 * j + 1
-        distances(k + 1, s2_a)
-        scalars(s2_b, tile_b)
-        sums(k - 1, tile_a)
-        distances(k + 2, s2_b)
-        scalars(s2_a, tile_a)
-        sums(k, tile_b)
+        stage(k, s2_a, s2_b, tile_b, tile_a)
+        stage(k + 1, s2_b, s2_a, tile_a, tile_b)
         return 0
 
     lax.fori_loop(0, (steps + 1) // 2, body, 0)
@@ -501,11 +592,15 @@
     chunk = 32
     for side, ref, out_ref in ((0, own_ref, own_vel_ref), (1, beside_ref, far_vel_ref)):
         for top in range(0, 128, chunk):
-            base = (side * 256 + 2 * top) * W_ROWS
             planes = []
             for c in range(19):
-                even = acc_ref[pl.ds(base + c, chunk, stride=2 * W_ROWS), :]
-                odd = acc_ref[pl.ds(base + W_ROWS + c, chunk, stride=2 * W_ROWS), :]
+                at = (2 * top) * W_ROWS + c
+                even = far_acc[pl.ds(side * BLOCKS * W_ROWS + at, chunk, stride=2 * W_ROWS), :]
+                at += W_ROWS
+                odd = far_acc[pl.ds(side * BLOCKS * W_ROWS + at, chunk, stride=2 * W_ROWS), :]
+                if side == 0:
+                    even += near_acc[pl.ds(at - W_ROWS, chunk, stride=2 * W_ROWS), :]
+                    odd += near_acc[pl.ds(at, chunk, stride=2 * W_ROWS), :]
                 even = even + pltpu.roll(even, 64, 1)
                 odd = odd + pltpu.roll(odd, 64, 1)
                 planes.append(jnp.where(low_half, even, odd))
@@ -523,50 +618,50 @@
                 )
 
 
-def pair_velocities(own, beside, first_list, second_list, count):
-    pad = 16
-    place = jnp.arange(PAIRS, dtype=jnp.int32)
-    live = place < count
-    near_out = jnp.where(live, first_list, TRASH) * W_ROWS
-    far_out = jnp.where(live & (first_list != second_list), second_list, TRASH) * W_ROWS
-    near = jnp.pad(first_list, (0, pad))
-    far = jnp.pad(second_list, (0, pad))
-    near_out = jnp.pad(near_out, (0, pad), constant_values=TRASH * W_ROWS)
-    far_out = jnp.pad(far_out, (0, pad), constant_values=TRASH * W_ROWS)
-    steps = ((count + STEP - 1) // STEP).reshape(1)
+def pair_lists(first_list, second_list, count):
+    live = jnp.arange(PAIRS, dtype=jnp.int32) < count
+    lists = jnp.stack(
+        [
+            first_list,
+            second_list,
+            jnp.where(live, first_list, BLOCKS) * W_ROWS,
+            jnp.where(live & (first_list != second_list), second_list, 2 * BLOCKS) * W_ROWS,
+        ]
+    )
+    spare = jnp.array([0, 0, BLOCKS * W_ROWS, 2 * BLOCKS * W_ROWS], jnp.int32)
+    return jnp.concatenate([lists, jnp.broadcast_to(spare[:, None], (4, 128))], axis=1)
+
+
+def pair_velocities(own, beside, tables_of, lists, count):
     plane = jax.ShapeDtypeStruct((3, 128, 128), f32)
     return pl.pallas_call(
         pair_kernel,
         out_shape=[plane, plane],
-        in_specs=[pl.BlockSpec(memory_space=pltpu.SMEM)] * 5 + vmem(2),
+        in_specs=[pl.BlockSpec(memory_space=pltpu.SMEM)] * 2 + vmem(5),
         out_specs=vmem(2),
         scratch_shapes=[
-            pltpu.VMEM((2 * BLOCKS, 48, 128), bf16),
-            pltpu.VMEM((BLOCKS, 64, 128), bf16),
-            pltpu.VMEM((2 * BLOCKS, 32, 128), bf16),
+            pltpu.VMEM(((BLOCKS + 1) * W_ROWS, 128), f32),
             pltpu.VMEM(((2 * BLOCKS + 1) * W_ROWS, 128), f32),
-            pltpu.VMEM((256 * W_ROWS, 128), f32),
-            pltpu.VMEM((128 * 32, 128), f32),
-            pltpu.VMEM((256 * 32, 128), f32),
-            pltpu.VMEM((64, 256), f32),
-            pltpu.VMEM((64, 256), f32),
-            pltpu.VMEM((256, 256), bf16),
-            pltpu.VMEM((256, 256), bf16),
+            pltpu.VMEM((GROUPS, 64, 256), f32),
+            pltpu.VMEM((GROUPS, 64, 256), f32),
+            pltpu.VMEM((2 * GROUPS, 256, 128), bf16),
+            pltpu.VMEM((2 * GROUPS, 256, 128), bf16),
         ],
-        compiler_params=pltpu.CompilerParams(vmem_limit_bytes=VMEM_LIMIT),
+        compiler_params=pltpu.CompilerParams(vmem_limit_bytes=SMALL_VMEM),
+        cost_estimate=cost(40),
         name="pairs",
-    )(near, far, near_out, far_out, steps, own, beside)
+    )(lists, count, *tables_of, own, beside)
 
 
 def reply_kernel(own_ref, far_ref, wave_ref, order_ref, z_ref, out_ref, hi_ref, lo_ref):
     for c in range(3):
         kind = 0 if c < 2 else 1
-        hi, lo = split2(jnp.transpose(wave_ref[c]))
+        hi, lo = split2(jnp.transpose(wave_ref[:, c, :]))
         wave = dot3(hi, lo, z_ref[0, kind], z_ref[1, kind])
         fill_table(c, own_ref[c] + far_ref[c] + wave, hi_ref, lo_ref)
 
     def put(c, r, row):
-        out_ref[c, pl.ds(r, 1), :] = row
+        out_ref[r, c : c + 1, :] = row
 
     gather_rows(3, 128, hi_ref, lo_ref, order_ref, put)
 
@@ -574,7 +669,7 @@
 def reply_message(own_vel, far_vel, wave, order, z_table):
     return pl.pallas_call(
         reply_kernel,
-        out_shape=jax.ShapeDtypeStruct((3, 128, 128), f32),
+        out_shape=jax.ShapeDtypeStruct((128, 3, 128), f32),
         in_specs=vmem(5),
         out_specs=pl.BlockSpec(memory_space=pltpu.VMEM),
         scratch_shapes=[pltpu.VMEM((192, 256), bf16), pltpu.VMEM((192, 256), bf16)],
@@ -586,7 +681,7 @@
 def move_kernel(in_ref, route_ref, pos_ref, noise_ref, moved_ref, drift_ref, hi_ref, lo_ref, vel_ref):
     rows = route_ref.shape[0]
     for c in range(3):
-        fill_table(c, in_ref[c], hi_ref, lo_ref)
+        fill_table(c, in_ref[:, c, :], hi_ref, lo_ref)
 
     def put(c, r, row):
         vel_ref[c, pl.ds(r, 1), :] = row
@@ -621,7 +716,7 @@
 
 
 def exchange(value):
-    return lax.all_to_all(value, ("gx", "gy"), split_axis=1, concat_axis=1, tiled=True)
+    return lax.all_to_all(value, ("gx", "gy"), split_axis=0, concat_axis=0, tiled=True)
 
 
 def shards(positions, noise, route, node_perm, pair_first, pair_second, pair_count):
@@ -633,10 +728,14 @@
     incoming = exchange(send_message(positions, route))
     grid, spec = place_on_grid(incoming, order, table["z"])
     beside = shifted(grid, "gx", -1)
-    wave = exchange(wave_flow(exchange(spec), table, member))
-    own_vel, far_vel = pair_velocities(
-        grid, beside, pair_first[0], pair_second[0], pair_count[0]
-    )
+    weight, right, left = own_tables(grid)
+    weight, right = beside_tables(beside, weight, right)
+    wave = wave_flow(exchange(spec), table, member)
+    grid, wave = lax.optimization_barrier((grid, wave))
+    wave = exchange(wave)
+    lists = pair_lists(pair_first[0], pair_second[0], pair_count[0])
+    own_vel, far_vel = pair_velocities(grid, beside, (weight, right, left), lists, pair_count)
+    far_vel, wave = lax.optimization_barrier((far_vel, wave))
     far_vel = shifted(far_vel, "gx", 1)
     reply = exchange(reply_message(own_vel, far_vel, wave, order, table["z"]))
     return tuple(move_beads(reply, route, positions, noise))

time: 211 us -> 172 us (0.82)
  Pallas kernels: 99.7 us -> 69.6 us
  blocking collectives: 62.9 us -> 38.5 us
  starting transfers between devices: 18.9 us -> 28.1 us
  waiting for transfers between devices: 12.9 us -> 17.6 us
    pallas_call x1, Pallas kernels: 51 us -> 23.7 us  [pair_velocities(): pl.pallas_call(pair_kernel, out_shape=[plane, plane], in_specs=[pl.BlockS...]
    all_to_all x2 -> x1, blocking collectives: 62.9 us -> 38.5 us  [exchange(): lax.all_to_all(value, ('gx', 'gy'), split_axis=0, concat_axis=0, tiled=True)]
    unnamed x10 -> x38, local copies, waits for them, and re-layouts: 2.11 us -> 13.4 us
    ppermute x2, waiting for transfers between devices: 0.01 us -> 7.08 us  [shifted(): lax.ppermute(value, axis, [(i, (i + by) % devices) for i in range(devices)])]
    pallas_call x4 -> x0, local copies, waits for them, and re-layouts: 5.93 us -> none  [the longest x1 2.03 us: send_message(): pl.pallas_call(send_kernel, out_shape=jax.ShapeDtypeStruct((6, 128, 128),...]
    all_to_all x2 -> x3, starting transfers between devices: 16.4 us -> 21.1 us  [exchange(): lax.all_to_all(value, ('gx', 'gy'), split_axis=0, concat_axis=0, tiled=True)]
    ppermute x2, starting transfers between devices: 2.45 us -> 6.97 us  [shifted(): lax.ppermute(value, axis, [(i, (i + by) % devices) for i in range(devices)])]
    pallas_call x1, Pallas kernels: 9.08 us -> 6.13 us  [move_beads(): pl.pallas_call(move_kernel, out_shape=[flat, flat], in_specs=vmem(4), out...]
  transfers between devices with their start and end apart: 4 -> 5, of which waited for: 1 -> 2; matrix products, arithmetic and copies ran while one was open for 4% -> 1% of each run, Pallas kernels for 26% -> 21%
where the time goes in v2:
time: 172 us; the launch traced here: 171 us
  Pallas kernels  69.6 us (40%)
  blocking collectives  38.5 us (22%)
  starting transfers between devices  28.1 us (16%)
  waiting for transfers between devices  17.6 us (10%)
  local copies, waits for them, and re-layouts  14.2 us (8%)
    all_to_all x1, blocking collectives, exchange(): lax.all_to_all(value, ('gx', 'gy'), split_axis=0, concat_axis=0, tiled=True)  38.5 us
    pallas_call x1, Pallas kernels, pair_velocities(): pl.pallas_call(pair_kernel, out_shape=[plane, plane], in_specs=[pl.BlockS...  23.7 us
    all_to_all x3, starting transfers between devices, exchange(): lax.all_to_all(value, ('gx', 'gy'), split_axis=0, concat_axis=0, tiled=True)  21.1 us
    unnamed x38, local copies, waits for them, and re-layouts  13.4 us
    pallas_call x1, Pallas kernels, place_on_grid(): pl.pallas_call(place_kernel, out_shape=[jax.ShapeDtypeStruct((6, 128, 128...  11.5 us
    all_to_all x3, waiting for transfers between devices, exchange(): lax.all_to_all(value, ('gx', 'gy'), split_axis=0, concat_axis=0, tiled=True)  10.5 us
    pallas_call x1, Pallas kernels, reply_message(): pl.pallas_call(reply_kernel, out_shape=jax.ShapeDtypeStruct((128, 3, 128)...  9.97 us
    ppermute x2, waiting for transfers between devices, shifted(): lax.ppermute(value, axis, [(i, (i + by) % devices) for i in range(devices)])  7.08 us
  transfers between devices with their start and end apart: 5, of which 2 were waited for; matrix products, arithmetic and copies ran while one was open for 1% of the time, Pallas kernels for 21%

profile of v2, /device:TPU:1, one launch (start us, length us, event | category | flops | bytes accessed | tf_op | source)
XLA Modules:
  0.0 171.0 jit_solution(10911880599543611159)
XLA Ops:
  0.6 0.0 copy-start
  0.7 1.0 copy-done.1
  1.6 0.8 copy-done.11
  2.4 6.6 %send.1 = f32[128,6,128]{2,1,0:T(8,128)} custom-call(f32[3,8192]{1,0:T(4,128)S(1)} %copy-done.1, s32[64,128]{1,0:T(8,128)S(1)} %bitcast.10), custom_call_target="tpu_custom_call" | custom-call | tf_op jit(solution)/shard_map/send/pallas_call | solution.py:211
  9.0 11.5 %all-to-all-start = ((f32[128,6,128]{2,1,0:T(8,128)}), f32[128,6,128]{2,1,0:T(8,128)S(1)}, u32[]{:S(2)}, u32[]{:S(2)}) async-start(f32[128,6,128]{2,1,0:T(8,128)} %send.1), calls=%async_computation | async-start | bytes 1048576 | tf_op jit(solution)/shard_map/all_to_all | solution.py:719
  21.2 0.7 fusion
  22.0 0.1 pad_maximum_fusion.part_ref
  22.1 0.7 broadcast_in_dim.15
  22.8 0.7 pad_add_fusion.list_ref
  23.5 10.5 %all-to-all-done.in_ref = f32[128,6,128]{2,1,0:T(8,128)S(1)} async-done(((f32[128,6,128]{2,1,0:T(8,128)}), f32[128,6,128]{2,1,0:T(8,128)S(1)}, u32[]{:S(2)}, u32[]{:S(2)}) %all-to-all-start) | async-done | bytes 393248 | tf_op jit(solution)/shard_map/all_to_all | solution.py:719
  34.0 0.9 copy-done.3
  35.0 11.5 %place.1 = (f32[6,128,128]{2,1,0:T(8,128)S(1)}, f32[128,3,128]{2,1,0:T(4,128)}) custom-call(f32[128,6,128]{2,1,0:T(8,128)S(1)} %all-to-all-done.in_ref, s32[128,128]{1,0:T(8,128)S(1)} %bitcast.8, bf16[2,2,128,128]{3,2,1,0:T(8,128)(2,1)S(1)} %copy-done.3), custom_call_target="tpu_custom_call" | custom-call | tf_op jit(solution)/shard_map/place/pallas_call | solution.py:238
  46.4 4.6 %all-to-all-start.1 = ((f32[128,3,128]{2,1,0:T(4,128)}), f32[128,3,128]{2,1,0:T(4,128)S(1)}, u32[]{:S(2)}, u32[]{:S(2)}) async-start(f32[128,3,128]{2,1,0:T(4,128)} %get-tuple-element.21), calls=%async_computation.1 | async-start | bytes 524288 | tf_op jit(solution)/shard_map/all_to_all | solution.py:719
  51.0 0.0 copy-start.6
  51.1 0.0 copy-start.8
  51.1 5.5 %collective-permute-start = (f32[6,128,128]{2,1,0:T(8,128)S(1)}, f32[6,128,128]{2,1,0:T(8,128)S(1)}, u32[]{:S(2)}, u32[]{:S(2)}) collective-permute-start(f32[6,128,128]{2,1,0:T(8,128)S(1)} %get-tuple-element.22.own_ref), channel_id=1, source_target_pairs={{0,120},{8,0},{16,8},{24,16},{32,24},{40,32},{48,40},{56,48},{64,5... | collective-permute-start | bytes 1179656 | tf_op jit(solution)/shard_map/ppermute | solution.py:715
  56.6 7.0 %own_tables.1 = (bf16[512,32,128]{2,1,0:T(8,128)(2,1)S(1)}, bf16[512,32,128]{2,1,0:T(8,128)(2,1)S(1)}, bf16[256,64,128]{2,1,0:T(8,128)(2,1)S(1)}) custom-call(f32[6,128,128]{2,1,0:T(8,128)S(1)} %get-tuple-element.22.own_ref), custom_call_target="tpu_custom_call" | custom-call | flops 8000000000 | bytes 1048576 | tf_op jit(solution)/shard_map/own_tables/pallas_call | solution.py:446
  63.6 2.0 %copy-done.13 = bf16[512,32,128]{2,1,0:T(8,128)(2,1)} copy-done((bf16[512,32,128]{2,1,0:T(8,128)(2,1)}, bf16[512,32,128]{2,1,0:T(8,128)(2,1)S(1)}, u32[]{:S(2)}) %copy-start.13) | copy-done | bytes 4194328
  65.6 2.0 %copy-done.15 = bf16[512,32,128]{2,1,0:T(8,128)(2,1)} copy-done((bf16[512,32,128]{2,1,0:T(8,128)(2,1)}, bf16[512,32,128]{2,1,0:T(8,128)(2,1)S(1)}, u32[]{:S(2)}) %copy-start.15) | copy-done | bytes 4194328
  67.6 2.0 %copy-done.17 = bf16[256,64,128]{2,1,0:T(8,128)(2,1)} copy-done((bf16[256,64,128]{2,1,0:T(8,128)(2,1)}, bf16[256,64,128]{2,1,0:T(8,128)(2,1)S(1)}, u32[]{:S(2)}) %copy-start.17) | copy-done | bytes 4194328
  69.6 2.9 %wave.1 = f32[128,3,128]{2,1,0:T(4,128)} custom-call(f32[4]{0:T(128)S(1)} %pad_maximum_fusion.part_ref, f32[128,3,128]{2,1,0:T(4,128)S(1)} %all-to-all-done.1.in_ref, bf16[2,256,128]{2,1,0:T(8,128)(2,1)S(1)} %copy-done.8, bf16[2,128,256]{2,1,0:T(8,128)(2,1)S(1)} %copy-done.9, bf16[2,256,256]{2,1,0:T(8,128)(2,1)S(1)} %copy-done.5, ...), custom_call_target="tpu_custom_call" | custom-call | tf_op jit(solution)/shard_map/wave/pallas_call | solution.py:327
  72.5 5.0 %all-to-all-start.2 = ((f32[128,3,128]{2,1,0:T(4,128)}), f32[128,3,128]{2,1,0:T(4,128)S(1)}, u32[]{:S(2)}, u32[]{:S(2)}) async-start(f32[128,3,128]{2,1,0:T(4,128)} %wave.1), calls=%async_computation.2 | async-start | bytes 524288 | tf_op jit(solution)/shard_map/all_to_all | solution.py:719
  77.5 2.2 %copy-done.14 = bf16[512,32,128]{2,1,0:T(8,128)(2,1)S(1)} copy-done((bf16[512,32,128]{2,1,0:T(8,128)(2,1)S(1)}, bf16[512,32,128]{2,1,0:T(8,128)(2,1)}, u32[]{:S(2)}) %copy-start.14) | copy-done | bytes 4194328
  79.7 2.2 %copy-done.16 = bf16[512,32,128]{2,1,0:T(8,128)(2,1)S(1)} copy-done((bf16[512,32,128]{2,1,0:T(8,128)(2,1)S(1)}, bf16[512,32,128]{2,1,0:T(8,128)(2,1)}, u32[]{:S(2)}) %copy-start.16) | copy-done | bytes 4194328
  81.9 1.8 %beside_tables.1 = (bf16[512,32,128]{2,1,0:T(8,128)(2,1)S(1)}, bf16[512,32,128]{2,1,0:T(8,128)(2,1)S(1)}) custom-call(f32[6,128,128]{2,1,0:T(8,128)S(1)} %collective-permute-done.beside_ref, bf16[512,32,128]{2,1,0:T(8,128)(2,1)S(1)} %copy-done.14, bf16[512,32,128]{2,1,0:T(8,128)(2,1)S(1)} %copy-done.16), custom_call_target="tpu_custom_call", output_to_operand_aliasing={{0}: (1, {}), {1}: (2, {})} | custom-call | flops 4000000000 | bytes 1048576 | tf_op jit(solution)/shard_map/beside_tables/pallas_call | solution.py:463
  83.7 0.4 copy-done.18
  84.1 23.7 %pairs.1 = (f32[3,128,128]{2,1,0:T(8,128)S(1)}, f32[3,128,128]{2,1,0:T(8,128)S(1)}) custom-call(s32[4,1152]{1,0:T(4,128)S(1)} %pad_add_fusion.list_ref, s32[1]{0:T(128)} %copy.20.count_ref, bf16[512,32,128]{2,1,0:T(8,128)(2,1)S(1)} %get-tuple-element.18.weight_ref, bf16[512,32,128]{2,1,0:T(8,128)(2,1)S(1)} %get-tuple-element.19.right_ref, ...), custom_call_target="tpu_custom_call" | custom-call | flops 40000000000 | bytes 1048576 | tf_op jit(solution)/shard_map/pairs/pallas_call | solution.py:637
  107.9 1.5 collective-permute-start.1
  109.3 7.1 %collective-permute-done.1.far_ref = f32[3,128,128]{2,1,0:T(8,128)S(1)} collective-permute-done((f32[3,128,128]{2,1,0:T(8,128)S(1)}, f32[3,128,128]{2,1,0:T(8,128)S(1)}, u32[]{:S(2)}, u32[]{:S(2)}) %collective-permute-start.1) | collective-permute-done | bytes 196640 | tf_op jit(solution)/shard_map/ppermute | solution.py:715
  116.4 10.0 %reply.1 = f32[128,3,128]{2,1,0:T(4,128)S(1)} custom-call(f32[3,128,128]{2,1,0:T(8,128)S(1)} %get-tuple-element.23.own_ref, f32[3,128,128]{2,1,0:T(8,128)S(1)} %collective-permute-done.1.far_ref, f32[128,3,128]{2,1,0:T(4,128)S(1)} %all-to-all-done.2.wave_ref, s32[128,128]{1,0:T(8,128)S(1)} %bitcast.9, bf16[2,2,128,128]{3,2,1,0:T(8,128)(2,1)S(1)} %copy-done.4), custom_call_target="tpu_custom_call" | custom-call | tf_op jit(solution)/shard_map/reply/pallas_call | solution.py:670
  126.4 38.5 %all_to_all.20.in_ref = f32[128,3,128]{2,1,0:T(4,128)S(1)} all-to-all(f32[128,3,128]{2,1,0:T(4,128)S(1)} %reply.1), channel_id=1, replica_groups=mesh['gx'=16,'gy'=8] {'gx','gy'}, dimensions={0} | all-to-all | bytes 393216 | tf_op jit(solution)/shard_map/all_to_all | solution.py:719
  164.9 6.1 %move.1 = (f32[3,8192]{1,0:T(4,128)}, f32[3,8192]{1,0:T(4,128)}) custom-call(f32[128,3,128]{2,1,0:T(4,128)S(1)} %all_to_all.20.in_ref, s32[64,128]{1,0:T(8,128)S(1)} %bitcast.11, f32[3,8192]{1,0:T(4,128)S(1)} %copy-done.2, f32[3,8192]{1,0:T(4,128)S(1)} %copy-done.7), custom_call_target="tpu_custom_call" | custom-call | tf_op jit(solution)/shard_map/move/pallas_call | solution.py:698
  (30 shorter events, 0.1 us)
Async XLA Ops:
  0.6 20.6 %copy-start = (s32[16,1,16384]{2,1,0:T(1,128)S(1)}, s32[16,1,16384]{2,1,0:T(1,128)}, u32[]{:S(2)}) copy-start(s32[16,1,16384]{2,1,0:T(1,128)} %param.17) | copy-start | bytes 3145732
  0.6 1.0 copy-start.1
  1.6 0.8 copy-start.11
  9.0 25.0 %all-to-all-start = ((f32[128,6,128]{2,1,0:T(8,128)}), f32[128,6,128]{2,1,0:T(8,128)S(1)}, u32[]{:S(2)}, u32[]{:S(2)}) async-start(f32[128,6,128]{2,1,0:T(8,128)} %send.1), calls=%async_computation | async-start | bytes 1048576 | tf_op jit(solution)/shard_map/all_to_all | solution.py:719
  34.0 0.9 copy-start.3
  46.4 23.1 %all-to-all-start.1 = ((f32[128,3,128]{2,1,0:T(4,128)}), f32[128,3,128]{2,1,0:T(4,128)S(1)}, u32[]{:S(2)}, u32[]{:S(2)}) async-start(f32[128,3,128]{2,1,0:T(4,128)} %get-tuple-element.21), calls=%async_computation.1 | async-start | bytes 524288 | tf_op jit(solution)/shard_map/all_to_all | solution.py:719
  51.0 18.5 %copy-start.5 = (bf16[2,256,256]{2,1,0:T(8,128)(2,1)S(1)}, bf16[2,256,256]{2,1,0:T(8,128)(2,1)}, u32[]{:S(2)}) copy-start(bf16[2,256,256]{2,1,0:T(8,128)(2,1)} %constant.71.clone.inner_ref) | copy-start | bytes 786436
  51.0 18.5 %copy-start.6 = (bf16[2,256,256]{2,1,0:T(8,128)(2,1)S(1)}, bf16[2,256,256]{2,1,0:T(8,128)(2,1)}, u32[]{:S(2)}) copy-start(bf16[2,256,256]{2,1,0:T(8,128)(2,1)} %constant.72.clone.inner_back_ref) | copy-start | bytes 786436
  51.1 18.5 %copy-start.8 = (bf16[2,256,128]{2,1,0:T(8,128)(2,1)S(1)}, bf16[2,256,128]{2,1,0:T(8,128)(2,1)}, u32[]{:S(2)}) copy-start(bf16[2,256,128]{2,1,0:T(8,128)(2,1)} %constant.69.clone.outer_ref) | copy-start | bytes 393220
  51.1 18.5 %copy-start.9 = (bf16[2,128,256]{2,1,0:T(8,128)(2,1)S(1)}, bf16[2,128,256]{2,1,0:T(8,128)(2,1)}, u32[]{:S(2)}) copy-start(bf16[2,128,256]{2,1,0:T(8,128)(2,1)} %constant.70.clone.outer_back_ref) | copy-start | bytes 393220
  51.1 18.5 %copy-start.10 = (f32[2,128,128]{2,1,0:T(8,128)S(1)}, f32[2,128,128]{2,1,0:T(8,128)}, u32[]{:S(2)}) copy-start(f32[2,128,128]{2,1,0:T(8,128)} %constant.73.clone.twist_ref) | copy-start | bytes 393220
  51.1 26.4 %collective-permute-start = (f32[6,128,128]{2,1,0:T(8,128)S(1)}, f32[6,128,128]{2,1,0:T(8,128)S(1)}, u32[]{:S(2)}, u32[]{:S(2)}) collective-permute-start(f32[6,128,128]{2,1,0:T(8,128)S(1)} %get-tuple-element.22.own_ref), channel_id=1, source_target_pairs={{0,120},{8,0},{16,8},{24,16},{32,24},{40,32},{48,40},{56,48},{64,5... | collective-permute-start | bytes 1179656 | tf_op jit(solution)/shard_map/ppermute | solution.py:715
  63.6 2.0 %copy-start.13 = (bf16[512,32,128]{2,1,0:T(8,128)(2,1)}, bf16[512,32,128]{2,1,0:T(8,128)(2,1)S(1)}, u32[]{:S(2)}) copy-start(bf16[512,32,128]{2,1,0:T(8,128)(2,1)S(1)} %get-tuple-element.16.weight_in) | copy-start | bytes 12582916
  65.6 2.0 %copy-start.15 = (bf16[512,32,128]{2,1,0:T(8,128)(2,1)}, bf16[512,32,128]{2,1,0:T(8,128)(2,1)S(1)}, u32[]{:S(2)}) copy-start(bf16[512,32,128]{2,1,0:T(8,128)(2,1)S(1)} %get-tuple-element.17.right_in) | copy-start | bytes 12582916
  67.6 2.0 %copy-start.17 = (bf16[256,64,128]{2,1,0:T(8,128)(2,1)}, bf16[256,64,128]{2,1,0:T(8,128)(2,1)S(1)}, u32[]{:S(2)}) copy-start(bf16[256,64,128]{2,1,0:T(8,128)(2,1)S(1)} %get-tuple-element.20.left_ref) | copy-start | bytes 12582916
  72.5 35.4 %all-to-all-start.2 = ((f32[128,3,128]{2,1,0:T(4,128)}), f32[128,3,128]{2,1,0:T(4,128)S(1)}, u32[]{:S(2)}, u32[]{:S(2)}) async-start(f32[128,3,128]{2,1,0:T(4,128)} %wave.1), calls=%async_computation.2 | async-start | bytes 524288 | tf_op jit(solution)/shard_map/all_to_all | solution.py:719
  77.5 2.2 %copy-start.14 = (bf16[512,32,128]{2,1,0:T(8,128)(2,1)S(1)}, bf16[512,32,128]{2,1,0:T(8,128)(2,1)}, u32[]{:S(2)}) copy-start(bf16[512,32,128]{2,1,0:T(8,128)(2,1)} %copy-done.13) | copy-start | bytes 12582916
  79.7 2.2 %copy-start.16 = (bf16[512,32,128]{2,1,0:T(8,128)(2,1)S(1)}, bf16[512,32,128]{2,1,0:T(8,128)(2,1)}, u32[]{:S(2)}) copy-start(bf16[512,32,128]{2,1,0:T(8,128)(2,1)} %copy-done.15) | copy-start | bytes 12582916
  81.9 2.2 %copy-start.18 = (bf16[256,64,128]{2,1,0:T(8,128)(2,1)S(1)}, bf16[256,64,128]{2,1,0:T(8,128)(2,1)}, u32[]{:S(2)}) copy-start(bf16[256,64,128]{2,1,0:T(8,128)(2,1)} %copy-done.17) | copy-start | bytes 12582916
  84.1 32.3 %copy-start.4 = (bf16[2,2,128,128]{3,2,1,0:T(8,128)(2,1)S(1)}, bf16[2,2,128,128]{3,2,1,0:T(8,128)(2,1)}, u32[]{:S(2)}) copy-start(bf16[2,2,128,128]{3,2,1,0:T(8,128)(2,1)} %constant.68.clone.z_ref) | copy-start | bytes 393220
  84.1 80.8 %copy-start.2 = (f32[3,8192]{1,0:T(4,128)S(1)}, f32[3,8192]{1,0:T(4,128)}, u32[]{:S(2)}) copy-start(f32[3,8192]{1,0:T(4,128)} %pos_ref.3) | copy-start | bytes 294916
  84.1 80.8 %copy-start.7 = (f32[3,8192]{1,0:T(4,128)S(1)}, f32[3,8192]{1,0:T(4,128)}, u32[]{:S(2)}) copy-start(f32[3,8192]{1,0:T(4,128)} %noise_ref.1) | copy-start | bytes 294916
  84.1 80.8 %copy-start.12 = (s32[8192]{0:T(1024)S(1)}, s32[8192]{0:T(1024)}, u32[]{:S(2)}) copy-start(s32[8192]{0:T(1024)} %param.16) | copy-start | bytes 98308
  107.9 8.5 %collective-permute-start.1 = (f32[3,128,128]{2,1,0:T(8,128)S(1)}, f32[3,128,128]{2,1,0:T(8,128)S(1)}, u32[]{:S(2)}, u32[]{:S(2)}) collective-permute-start(f32[3,128,128]{2,1,0:T(8,128)S(1)} %get-tuple-element.26), channel_id=1, source_target_pairs={{0,8},{8,16},{16,24},{24,32},{32,40},{40,48},{48,56},{56,64},{64,7... | collective-permute-start | bytes 589832 | tf_op jit(solution)/shard_map/ppermute | solution.py:715

commit v3 on v2

--- a/solution.py
+++ b/solution.py
@@ -26,7 +26,7 @@
 f32 = jnp.float32
 bf16 = jnp.bfloat16
 VMEM_LIMIT = 24 * 1024 * 1024
-SMALL_VMEM = 24 * 1024 * 1024
+PAIR_VMEM = 40 * 1024 * 1024
 
 
 def dot(a, b):
@@ -130,28 +130,25 @@
     lax.fori_loop(0, rows // group, turn, 0)
 
 
-def gather_rows(channels, rows, table_hi_ref, table_lo_ref, place_ref, put):
-    width = 4
-
-    def turn(g, _):
-        low, high = [], []
-        for j in range(width):
-            place = place_ref[pl.ds(g * width + j, 1), :]
-            low.append(onehot(low_part(place), 256, 128))
-            high.append(high_part(place))
-        low = jnp.concatenate(low, axis=1)
-        high = jnp.concatenate(high, axis=1)
-        found = dot(table_hi_ref[...], low) + dot(table_lo_ref[...], low)
-        rows_of = lax.broadcasted_iota(jnp.int32, (64, width * 128), 0) == high
-        for c in range(channels):
-            got = jnp.sum(
-                jnp.where(rows_of, found[c * 64 : (c + 1) * 64], 0.0), axis=0, keepdims=True
-            )
-            for j in range(width):
-                put(c, g * width + j, got[:, j * 128 : (j + 1) * 128])
-        return 0
-
-    lax.fori_loop(0, rows // width, turn, 0)
+def gather_rows(channels, table_hi_ref, table_lo_ref, place_ref, rows, put):
+    low, high = [], []
+    for r in rows:
+        place = place_ref[pl.ds(r, 1), :]
+        low.append(onehot(low_part(place), 256, 128))
+        high.append(high_part(place))
+    low = jnp.concatenate(low, axis=1)
+    high = jnp.concatenate(high, axis=1)
+    found = dot(table_hi_ref[...], low) + dot(table_lo_ref[...], low)
+    rows_of = lax.broadcasted_iota(jnp.int32, (64, len(rows) * 128), 0) == high
+    for c in range(channels):
+        got = jnp.sum(
+            jnp.where(rows_of, found[c * 64 : (c + 1) * 64], 0.0), axis=0, keepdims=True
+        )
+        for n in range(len(rows)):
+            put(c, n, got[:, n * 128 : (n + 1) * 128])
+
+
+WIDTH = 4
 
 
 def fill_table(c, plane, table_hi_ref, table_lo_ref):
@@ -159,6 +156,50 @@
     for ref, part in ((table_hi_ref, hi), (table_lo_ref, lo)):
         ref[c * 64 : (c + 1) * 64, 0:128] = part[0:64]
         ref[c * 64 : (c + 1) * 64, 128:256] = part[64:128]
+
+
+def greet_all(me, n_gy, members):
+    barrier = pltpu.get_barrier_semaphore()
+
+    def greet(d, _):
+        there = lax.rem(me + d, members)
+        pl.semaphore_signal(
+            barrier,
+            inc=1,
+            device_id=(there // n_gy, lax.rem(there, n_gy)),
+            device_id_type=pl.DeviceIdType.MESH,
+        )
+        return 0
+
+    lax.fori_loop(1, members, greet, 0)
+
+
+def wait_for_all(members):
+    pl.semaphore_wait(pltpu.get_barrier_semaphore(), members - 1)
+
+
+def send_row(out_ref, in_ref, me, there, n_gy, send_sem, recv_sem):
+    pltpu.make_async_remote_copy(
+        src_ref=out_ref.at[there],
+        dst_ref=in_ref.at[me],
+        send_sem=send_sem,
+        recv_sem=recv_sem,
+        device_id=(there // n_gy, lax.rem(there, n_gy)),
+        device_id_type=pl.DeviceIdType.MESH,
+    ).start()
+
+
+def wait_rows(out_ref, in_ref, members, send_sem, recv_sem):
+    every = pltpu.make_async_remote_copy(
+        src_ref=out_ref.at[pl.ds(0, members - 1)],
+        dst_ref=in_ref.at[pl.ds(0, members - 1)],
+        send_sem=send_sem,
+        recv_sem=recv_sem,
+        device_id=(0, 0),
+        device_id_type=pl.DeviceIdType.MESH,
+    )
+    every.wait_send()
+    every.wait_recv()
 
 
 def chain_forces(x):
@@ -187,7 +228,12 @@
     return [g - jnp.where(lane == 0, 0.0, behind(g)) for g in grad]
 
 
-def send_kernel(pos_ref, route_ref, out_ref, plane_ref, left_ref, sum_ref):
+def send_kernel(
+    members, n_gy, pos_ref, route_ref, in_ref, out_ref, plane_ref, left_ref, sum_ref, send_sem,
+    recv_sem,
+):
+    me = lax.axis_index("gx") * n_gy + lax.axis_index("gy")
+    greet_all(me, n_gy, members)
     rows = route_ref.shape[0]
     for c in range(3):
         for r in range(rows):
@@ -201,6 +247,15 @@
     for c in range(6):
         out_ref[0:64, c, :] = sum_ref[c * 64 : (c + 1) * 64, 0:128]
         out_ref[64:128, c, :] = sum_ref[c * 64 : (c + 1) * 64, 128:256]
+    wait_for_all(members)
+
+    def go(d, _):
+        send_row(out_ref, in_ref, me, lax.rem(me + d, members), n_gy, send_sem, recv_sem)
+        return 0
+
+    lax.fori_loop(1, members, go, 0)
+    in_ref[me] = out_ref[me]
+    wait_rows(out_ref, in_ref, members, send_sem, recv_sem)
 
 
 def vmem(n):
@@ -208,17 +263,24 @@
 
 
 def send_message(positions, route):
+    n_gy = lax.axis_size("gy")
+    members = lax.axis_size("gx") * n_gy
     return pl.pallas_call(
-        send_kernel,
+        partial(send_kernel, members, n_gy),
         out_shape=jax.ShapeDtypeStruct((128, 6, 128), f32),
         in_specs=vmem(2),
         out_specs=pl.BlockSpec(memory_space=pltpu.VMEM),
         scratch_shapes=[
+            pltpu.VMEM((128, 6, 128), f32),
             pltpu.VMEM((6, 64, 128), f32),
             pltpu.VMEM((768, 1024), bf16),
             pltpu.VMEM((384, 256), f32),
+            pltpu.SemaphoreType.DMA,
+            pltpu.SemaphoreType.DMA,
         ],
-        compiler_params=pltpu.CompilerParams(vmem_limit_bytes=VMEM_LIMIT),
+        compiler_params=pltpu.CompilerParams(
+            vmem_limit_bytes=VMEM_LIMIT, collective_id=1, has_side_effects=True
+        ),
         name="send",
     )(positions, route)
 
@@ -404,10 +466,7 @@
     lax.fori_loop(0, 128, build, 0, unroll=16)
 
 
-def own_tables_kernel(
-    own_ref, weight_ref, right_ref, left_ref, weight_stage, right_stage, left_stage
-):
-    first = stage_nodes(own_ref, weight_stage, right_stage)
+def build_left(first, left_stage, left_ref):
     for c, plane in enumerate(first):
         left_stage[pl.ds(c, 128, stride=FEATURES), :] = plane
     eye = jnp.where(
@@ -427,59 +486,19 @@
         return 0
 
     lax.fori_loop(0, 128, turn_left, 0, unroll=8)
+
+
+def pair_kernel(
+    list_ref, count_ref, own_ref, beside_ref, own_vel_ref, far_vel_ref,
+    weight_ref, right_ref, left_ref, weight_stage, right_stage, left_stage,
+    near_acc, far_acc, s2_a, s2_b, tile_a, tile_b,
+):
+    first = stage_nodes(own_ref, weight_stage, right_stage)
+    build_left(first, left_stage, left_ref)
     build_tables(0, weight_stage, right_stage, weight_ref, right_ref)
-
-
-def beside_tables_kernel(
-    beside_ref, weight_in, right_in, weight_ref, right_ref, weight_stage, right_stage
-):
     stage_nodes(beside_ref, weight_stage, right_stage)
     build_tables(BLOCKS, weight_stage, right_stage, weight_ref, right_ref)
 
-
-WEIGHT_TABLE = jax.ShapeDtypeStruct((2 * BLOCKS, 32, 128), bf16)
-RIGHT_TABLE = jax.ShapeDtypeStruct((2 * BLOCKS, 32, 128), bf16)
-LEFT_TABLE = jax.ShapeDtypeStruct((BLOCKS, 64, 128), bf16)
-
-
-def own_tables(own):
-    return pl.pallas_call(
-        own_tables_kernel,
-        out_shape=[WEIGHT_TABLE, RIGHT_TABLE, LEFT_TABLE],
-        in_specs=vmem(1),
-        out_specs=vmem(3),
-        scratch_shapes=[
-            pltpu.VMEM((128 * 16, 128), f32),
-            pltpu.VMEM((128 * FEATURES, 128), f32),
-            pltpu.VMEM((128 * FEATURES, 128), f32),
-        ],
-        compiler_params=pltpu.CompilerParams(vmem_limit_bytes=SMALL_VMEM),
-        cost_estimate=cost(8),
-        name="own_tables",
-    )(own)
-
-
-def beside_tables(beside, weight, right):
-    return pl.pallas_call(
-        beside_tables_kernel,
-        out_shape=[WEIGHT_TABLE, RIGHT_TABLE],
-        in_specs=vmem(1) + [pl.BlockSpec(memory_space=pl.ANY)] * 2,
-        out_specs=vmem(2),
-        input_output_aliases={1: 0, 2: 1},
-        scratch_shapes=[
-            pltpu.VMEM((128 * 16, 128), f32),
-            pltpu.VMEM((128 * FEATURES, 128), f32),
-        ],
-        compiler_params=pltpu.CompilerParams(vmem_limit_bytes=SMALL_VMEM),
-        cost_estimate=cost(4),
-        name="beside_tables",
-    )(beside, weight, right)
-
-
-def pair_kernel(
-    list_ref, count_ref, weight_ref, right_ref, left_ref, own_ref, beside_ref,
-    own_vel_ref, far_vel_ref, near_acc, far_acc, s2_a, s2_b, tile_a, tile_b,
-):
     lane = lax.broadcasted_iota(jnp.int32, (1, 128), 1)
     low_half = lane < 64
     count = count_ref[0]
@@ -632,14 +651,20 @@
     return jnp.concatenate([lists, jnp.broadcast_to(spare[:, None], (4, 128))], axis=1)
 
 
-def pair_velocities(own, beside, tables_of, lists, count):
+def pair_velocities(own, beside, lists, count):
     plane = jax.ShapeDtypeStruct((3, 128, 128), f32)
     return pl.pallas_call(
         pair_kernel,
         out_shape=[plane, plane],
-        in_specs=[pl.BlockSpec(memory_space=pltpu.SMEM)] * 2 + vmem(5),
+        in_specs=[pl.BlockSpec(memory_space=pltpu.SMEM)] * 2 + vmem(2),
         out_specs=vmem(2),
         scratch_shapes=[
+            pltpu.VMEM((2 * BLOCKS, 32, 128), bf16),
+            pltpu.VMEM((2 * BLOCKS, 32, 128), bf16),
+            pltpu.VMEM((BLOCKS, 64, 128), bf16),
+            pltpu.VMEM((128 * 16, 128), f32),
+            pltpu.VMEM((128 * FEATURES, 128), f32),
+            pltpu.VMEM((128 * FEATURES, 128), f32),
             pltpu.VMEM(((BLOCKS + 1) * W_ROWS, 128), f32),
             pltpu.VMEM(((2 * BLOCKS + 1) * W_ROWS, 128), f32),
             pltpu.VMEM((GROUPS, 64, 256), f32),
@@ -647,33 +672,77 @@
             pltpu.VMEM((2 * GROUPS, 256, 128), bf16),
             pltpu.VMEM((2 * GROUPS, 256, 128), bf16),
         ],
-        compiler_params=pltpu.CompilerParams(vmem_limit_bytes=SMALL_VMEM),
-        cost_estimate=cost(40),
+        compiler_params=pltpu.CompilerParams(vmem_limit_bytes=PAIR_VMEM),
+        cost_estimate=cost(50),
         name="pairs",
-    )(lists, count, *tables_of, own, beside)
-
-
-def reply_kernel(own_ref, far_ref, wave_ref, order_ref, z_ref, out_ref, hi_ref, lo_ref):
+    )(lists, count, own, beside)
+
+
+def reply_kernel(
+    members, n_gx, n_gy, own_ref, far_ref, wave_ref, order_ref, z_ref, in_ref, out_ref,
+    beside_ref, hi_ref, lo_ref, send_sem, recv_sem, far_send, far_recv,
+):
+    g_x = lax.axis_index("gx")
+    me = g_x * n_gy + lax.axis_index("gy")
+    greet_all(me, n_gy, members)
+    wait_for_all(members)
+    far = pltpu.make_async_remote_copy(
+        src_ref=far_ref,
+        dst_ref=beside_ref,
+        send_sem=far_send,
+        recv_sem=far_recv,
+        device_id=(lax.rem(g_x + 1, n_gx), lax.axis_index("gy")),
+        device_id_type=pl.DeviceIdType.MESH,
+    )
+    far.start()
+    waves = []
     for c in range(3):
         kind = 0 if c < 2 else 1
         hi, lo = split2(jnp.transpose(wave_ref[:, c, :]))
-        wave = dot3(hi, lo, z_ref[0, kind], z_ref[1, kind])
-        fill_table(c, own_ref[c] + far_ref[c] + wave, hi_ref, lo_ref)
-
-    def put(c, r, row):
-        out_ref[r, c : c + 1, :] = row
-
-    gather_rows(3, 128, hi_ref, lo_ref, order_ref, put)
+        waves.append(own_ref[c] + dot3(hi, lo, z_ref[0, kind], z_ref[1, kind]))
+    far.wait()
+    for c in range(3):
+        fill_table(c, waves[c] + beside_ref[c], hi_ref, lo_ref)
+
+    def turn(g, _):
+        rows = [lax.rem(me + 1 + g * WIDTH + j, members) for j in range(WIDTH)]
+
+        def put(c, n, row):
+            out_ref[rows[n], c : c + 1, :] = row
+
+        gather_rows(3, hi_ref, lo_ref, order_ref, rows, put)
+        for j, row in enumerate(rows):
+            pl.when(g * WIDTH + j < members - 1)(
+                partial(send_row, out_ref, in_ref, me, row, n_gy, send_sem, recv_sem)
+            )
+        return 0
+
+    lax.fori_loop(0, members // WIDTH, turn, 0)
+    in_ref[me] = out_ref[me]
+    wait_rows(out_ref, in_ref, members, send_sem, recv_sem)
 
 
 def reply_message(own_vel, far_vel, wave, order, z_table):
+    n_gx, n_gy = lax.axis_size("gx"), lax.axis_size("gy")
+    members = n_gx * n_gy
     return pl.pallas_call(
-        reply_kernel,
+        partial(reply_kernel, members, n_gx, n_gy),
         out_shape=jax.ShapeDtypeStruct((128, 3, 128), f32),
         in_specs=vmem(5),
         out_specs=pl.BlockSpec(memory_space=pltpu.VMEM),
-        scratch_shapes=[pltpu.VMEM((192, 256), bf16), pltpu.VMEM((192, 256), bf16)],
-        compiler_params=pltpu.CompilerParams(vmem_limit_bytes=VMEM_LIMIT),
+        scratch_shapes=[
+            pltpu.VMEM((128, 3, 128), f32),
+            pltpu.VMEM((3, 128, 128), f32),
+            pltpu.VMEM((192, 256), bf16),
+            pltpu.VMEM((192, 256), bf16),
+            pltpu.SemaphoreType.DMA,
+            pltpu.SemaphoreType.DMA,
+            pltpu.SemaphoreType.DMA,
+            pltpu.SemaphoreType.DMA,
+        ],
+        compiler_params=pltpu.CompilerParams(
+            vmem_limit_bytes=VMEM_LIMIT, collective_id=2, has_side_effects=True
+        ),
         name="reply",
     )(own_vel, far_vel, wave, order, z_table)
 
@@ -683,10 +752,14 @@
     for c in range(3):
         fill_table(c, in_ref[:, c, :], hi_ref, lo_ref)
 
-    def put(c, r, row):
-        vel_ref[c, pl.ds(r, 1), :] = row
-
-    gather_rows(3, rows, hi_ref, lo_ref, route_ref, put)
+    def turn(g, _):
+        def put(c, n, row):
+            vel_ref[c, pl.ds(g * WIDTH + n, 1), :] = row
+
+        gather_rows(3, hi_ref, lo_ref, route_ref, [g * WIDTH + j for j in range(WIDTH)], put)
+        return 0
+
+    lax.fori_loop(0, rows // WIDTH, turn, 0)
     for c in range(3):
         for r in range(rows):
             drift_ref[c : c + 1, r * 128 : (r + 1) * 128] = time_step * vel_ref[c, r : r + 1, :]
@@ -725,19 +798,15 @@
     member = row_gx * lax.axis_size("gy") + lax.axis_index("gy")
     route = route.reshape(64, 128)
     order = lax.dynamic_index_in_dim(node_perm, row_gx, 0, keepdims=False).reshape(128, 128)
-    incoming = exchange(send_message(positions, route))
+    incoming = send_message(positions, route)
     grid, spec = place_on_grid(incoming, order, table["z"])
     beside = shifted(grid, "gx", -1)
-    weight, right, left = own_tables(grid)
-    weight, right = beside_tables(beside, weight, right)
     wave = wave_flow(exchange(spec), table, member)
     grid, wave = lax.optimization_barrier((grid, wave))
     wave = exchange(wave)
     lists = pair_lists(pair_first[0], pair_second[0], pair_count[0])
-    own_vel, far_vel = pair_velocities(grid, beside, (weight, right, left), lists, pair_count)
-    far_vel, wave = lax.optimization_barrier((far_vel, wave))
-    far_vel = shifted(far_vel, "gx", 1)
-    reply = exchange(reply_message(own_vel, far_vel, wave, order, table["z"]))
+    own_vel, far_vel = pair_velocities(grid, beside, lists, pair_count)
+    reply = reply_message(own_vel, far_vel, wave, order, table["z"])
     return tuple(move_beads(reply, route, positions, noise))
 
 

time: 172 us -> 150 us (0.87)
  Pallas kernels: 69.6 us -> 125 us
  blocking collectives: 38.5 us -> 0 us
  waiting for transfers between devices: 17.6 us -> 4.67 us
  local copies, waits for them, and re-layouts: 14.2 us -> 2.1 us
  starting transfers between devices: 28.1 us -> 16.2 us
    pallas_call x4 -> x2, Pallas kernels: 25.4 us -> 71.5 us  [the longest x1 49.8 us: reply_message(): pl.pallas_call(partial(reply_kernel, members, n_gx, n_gy), out_shape=jax....]
    all_to_all x1 -> x0, blocking collectives: 38.5 us -> none  [exchange(): lax.all_to_all(value, ('gx', 'gy'), split_axis=0, concat_axis=0, tiled=True)]
    unnamed x38 -> x28, local copies, waits for them, and re-layouts: 13.4 us -> 2.02 us
    all_to_all x3 -> x2, starting transfers between devices: 21.1 us -> 10.8 us  [exchange(): lax.all_to_all(value, ('gx', 'gy'), split_axis=0, concat_axis=0, tiled=True)]
    pallas_call x1, Pallas kernels: 23.7 us -> 33 us  [pair_velocities(): pl.pallas_call(pair_kernel, out_shape=[plane, plane], in_specs=[pl.BlockS...]
    ppermute x2 -> x1, waiting for transfers between devices: 7.08 us -> 0.01 us  [shifted(): lax.ppermute(value, axis, [(i, (i + by) % devices) for i in range(devices)])]
    all_to_all x3 -> x2, waiting for transfers between devices: 10.5 us -> 4.67 us  [exchange(): lax.all_to_all(value, ('gx', 'gy'), split_axis=0, concat_axis=0, tiled=True)]
    ppermute x2 -> x1, starting transfers between devices: 6.97 us -> 5.48 us  [shifted(): lax.ppermute(value, axis, [(i, (i + by) % devices) for i in range(devices)])]
  transfers between devices with their start and end apart: 5 -> 3, of which waited for: 2 -> 1; matrix products, arithmetic and copies ran while one was open for 1% -> 0% of each run, Pallas kernels for 21% -> 24%
where the time goes in v3:
time: 150 us
  Pallas kernels  125 us (83%)
  starting transfers between devices  16.2 us (11%)
  waiting for transfers between devices  4.67 us (3%)
  local copies, waits for them, and re-layouts  2.1 us (1%)
  between operations  1.54 us (1%)
    pallas_call x1, Pallas kernels, reply_message(): pl.pallas_call(partial(reply_kernel, members, n_gx, n_gy), out_shape=jax....  49.8 us
    pallas_call x1, Pallas kernels, pair_velocities(): pl.pallas_call(pair_kernel, out_shape=[plane, plane], in_specs=[pl.BlockS...  33 us
    pallas_call x1, Pallas kernels, send_message(): pl.pallas_call(partial(send_kernel, members, n_gy), out_shape=jax.ShapeDt...  21.7 us
    pallas_call x1, Pallas kernels, place_on_grid(): pl.pallas_call(place_kernel, out_shape=[jax.ShapeDtypeStruct((6, 128, 128...  11.5 us
    all_to_all x2, starting transfers between devices, exchange(): lax.all_to_all(value, ('gx', 'gy'), split_axis=0, concat_axis=0, tiled=True)  10.8 us
    pallas_call x1, Pallas kernels, move_beads(): pl.pallas_call(move_kernel, out_shape=[flat, flat], in_specs=vmem(4), out...  6.13 us
    ppermute x1, starting transfers between devices, shifted(): lax.ppermute(value, axis, [(i, (i + by) % devices) for i in range(devices)])  5.48 us
    all_to_all x2, waiting for transfers between devices, exchange(): lax.all_to_all(value, ('gx', 'gy'), split_axis=0, concat_axis=0, tiled=True)  4.67 us
  transfers between devices with their start and end apart: 3, of which 1 were waited for; matrix products, arithmetic and copies ran while one was open for 0% of the time, Pallas kernels for 24%

profile of v3, /device:TPU:1, one launch (start us, length us, event | category | flops | bytes accessed | tf_op | source)
XLA Modules:
  0.0 149.6 jit_solution(2656601391819505444)
XLA Ops:
  0.6 0.0 copy-start
  0.6 0.0 copy-start.1
  0.7 1.2 copy-done
  1.9 0.0 copy-done.1
  1.9 0.0 copy-start.9
  1.9 0.7 copy-done.9
  2.6 21.7 %send.1.in_ref = f32[128,6,128]{2,1,0:T(8,128)S(1)} custom-call(f32[3,8192]{1,0:T(4,128)S(1)} %copy-done.1, s32[64,128]{1,0:T(8,128)S(1)} %bitcast.10), custom_call_target="tpu_custom_call" | custom-call | tf_op jit(solution)/shard_map/send/pallas_call | solution.py:268
  24.3 0.0 copy-done.2
  24.3 0.0 copy-start.12
  24.4 0.0 copy-start.7
  24.4 0.0 copy-start.8
  24.4 11.5 %place.1 = (f32[6,128,128]{2,1,0:T(8,128)S(1)}, f32[128,3,128]{2,1,0:T(4,128)}) custom-call(f32[128,6,128]{2,1,0:T(8,128)S(1)} %send.1.in_ref, s32[128,128]{1,0:T(8,128)S(1)} %bitcast.8, bf16[2,2,128,128]{3,2,1,0:T(8,128)(2,1)S(1)} %copy-done.2), custom_call_target="tpu_custom_call" | custom-call | tf_op jit(solution)/shard_map/place/pallas_call | solution.py:300
  35.9 6.1 %all-to-all-start = ((f32[128,3,128]{2,1,0:T(4,128)}), f32[128,3,128]{2,1,0:T(4,128)S(1)}, u32[]{:S(2)}, u32[]{:S(2)}) async-start(f32[128,3,128]{2,1,0:T(4,128)} %get-tuple-element.9), calls=%async_computation | async-start | bytes 524288 | tf_op jit(solution)/shard_map/all_to_all | solution.py:792
  42.0 0.0 copy-start.6
  42.0 5.5 %collective-permute-start = (f32[6,128,128]{2,1,0:T(8,128)S(1)}, f32[6,128,128]{2,1,0:T(8,128)S(1)}, u32[]{:S(2)}, u32[]{:S(2)}) collective-permute-start(f32[6,128,128]{2,1,0:T(8,128)S(1)} %get-tuple-element.10.own_ref), channel_id=1, source_target_pairs={{0,120},{8,0},{16,8},{24,16},{32,24},{40,32},{48,40},{56,48},{64,5... | collective-permute-start | bytes 1179656 | tf_op jit(solution)/shard_map/ppermute | solution.py:788
  48.1 0.0 copy-done.12
  48.1 0.0 copy-done.11
  48.2 0.1 pad_maximum_fusion.part_ref
  48.3 0.0 copy-done.13
  48.3 0.1 broadcast_in_dim.15
  48.4 4.7 %all-to-all-done.in_ref = f32[128,3,128]{2,1,0:T(4,128)S(1)} async-done(((f32[128,3,128]{2,1,0:T(4,128)}), f32[128,3,128]{2,1,0:T(4,128)S(1)}, u32[]{:S(2)}, u32[]{:S(2)}) %all-to-all-start) | async-done | bytes 196640 | tf_op jit(solution)/shard_map/all_to_all | solution.py:792
  53.0 0.0 copy-done.7
  53.0 0.0 copy-done.8
  53.1 2.8 %wave.1 = f32[128,3,128]{2,1,0:T(4,128)} custom-call(f32[4]{0:T(128)S(1)} %pad_maximum_fusion.part_ref, f32[128,3,128]{2,1,0:T(4,128)S(1)} %all-to-all-done.in_ref, bf16[2,256,128]{2,1,0:T(8,128)(2,1)S(1)} %copy-done.8, bf16[2,128,256]{2,1,0:T(8,128)(2,1)S(1)} %copy-done.7, bf16[2,256,256]{2,1,0:T(8,128)(2,1)S(1)} %copy-done.4, ...), custom_call_target="tpu_custom_call" | custom-call | tf_op jit(solution)/shard_map/wave/pallas_call | solution.py:389
  55.9 4.7 %all-to-all-start.1 = ((f32[128,3,128]{2,1,0:T(4,128)}), f32[128,3,128]{2,1,0:T(4,128)S(1)}, u32[]{:S(2)}, u32[]{:S(2)}) async-start(f32[128,3,128]{2,1,0:T(4,128)} %wave.1), calls=%async_computation.1 | async-start | bytes 524288 | tf_op jit(solution)/shard_map/all_to_all | solution.py:792
  60.6 0.0 collective-permute-done.beside_ref
  60.6 33.0 %pairs.1 = (f32[3,128,128]{2,1,0:T(8,128)S(1)}, f32[3,128,128]{2,1,0:T(8,128)S(1)}) custom-call(s32[4,1152]{1,0:T(4,128)S(1)} %pad_add_fusion.list_ref, s32[1]{0:T(128)} %copy.16.count_ref, f32[6,128,128]{2,1,0:T(8,128)S(1)} %get-tuple-element.10.own_ref, f32[6,128,128]{2,1,0:T(8,128)S(1)} %collective-permute-done.beside_ref), custom_call_target="tpu_custom_call" | custom-call | flops 49999998976 | bytes 1048576 | tf_op jit(solution)/shard_map/pairs/pallas_call | solution.py:656
  93.6 0.0 all-to-all-done.1.wave_ref
  93.6 0.0 copy-start.5
  93.6 0.0 copy-start.10
  93.6 49.8 %reply.1.in_ref = f32[128,3,128]{2,1,0:T(4,128)S(1)} custom-call(f32[3,128,128]{2,1,0:T(8,128)S(1)} %get-tuple-element.11.own_ref, f32[3,128,128]{2,1,0:T(8,128)S(1)} %get-tuple-element.12.far_ref, f32[128,3,128]{2,1,0:T(4,128)S(1)} %all-to-all-done.1.wave_ref, s32[128,128]{1,0:T(8,128)S(1)} %bitcast.9, bf16[2,2,128,128]{3,2,1,0:T(8,128)(2,1)S(1)} %copy-done.2), custom_call_target="tpu_custom_call" | custom-call | tf_op jit(solution)/shard_map/reply/pallas_call | solution.py:728
  143.5 6.1 %move.1 = (f32[3,8192]{1,0:T(4,128)}, f32[3,8192]{1,0:T(4,128)}) custom-call(f32[128,3,128]{2,1,0:T(4,128)S(1)} %reply.1.in_ref, s32[64,128]{1,0:T(8,128)S(1)} %bitcast.11, f32[3,8192]{1,0:T(4,128)S(1)} %copy-done.1, f32[3,8192]{1,0:T(4,128)S(1)} %copy-done.5), custom_call_target="tpu_custom_call" | custom-call | tf_op jit(solution)/shard_map/move/pallas_call | solution.py:771
  (13 shorter events, 0.1 us)
Async XLA Ops:
  0.6 1.2 copy-start
  0.6 1.2 copy-start.1
  1.9 0.8 copy-start.9
  2.6 21.7 %copy-start.2 = (bf16[2,2,128,128]{3,2,1,0:T(8,128)(2,1)S(1)}, bf16[2,2,128,128]{3,2,1,0:T(8,128)(2,1)}, u32[]{:S(2)}) copy-start(bf16[2,2,128,128]{3,2,1,0:T(8,128)(2,1)} %constant.68.clone.z_ref) | copy-start | bytes 393220
  24.3 23.8 %copy-start.12 = (s32[1,1024]{1,0:T(1,128)S(1)}, s32[1,1024]{1,0:T(1,128)}, u32[]{:S(2)}) copy-start(s32[1,1024]{1,0:T(1,128)} %param.19) | copy-start | bytes 12292
  24.4 28.7 %copy-start.7 = (bf16[2,128,256]{2,1,0:T(8,128)(2,1)S(1)}, bf16[2,128,256]{2,1,0:T(8,128)(2,1)}, u32[]{:S(2)}) copy-start(bf16[2,128,256]{2,1,0:T(8,128)(2,1)} %constant.70.clone.outer_back_ref) | copy-start | bytes 393220
  24.4 28.7 %copy-start.8 = (bf16[2,256,128]{2,1,0:T(8,128)(2,1)S(1)}, bf16[2,256,128]{2,1,0:T(8,128)(2,1)}, u32[]{:S(2)}) copy-start(bf16[2,256,128]{2,1,0:T(8,128)(2,1)} %constant.69.clone.outer_ref) | copy-start | bytes 393220
  35.8 12.3 %copy-start.11 = (s32[1,1024]{1,0:T(1,128)S(1)}, s32[1,1024]{1,0:T(1,128)}, u32[]{:S(2)}) copy-start(s32[1,1024]{1,0:T(1,128)} %param.18) | copy-start | bytes 12292
  35.9 12.4 %copy-start.13 = (s32[4]{0:T(128)S(1)}, s32[4]{0:T(128)}, u32[]{:S(2)}) copy-start(s32[4]{0:T(128)} %constant.74.clone) | copy-start | bytes 52
  35.9 17.2 %copy-start.3 = (bf16[2,256,256]{2,1,0:T(8,128)(2,1)S(1)}, bf16[2,256,256]{2,1,0:T(8,128)(2,1)}, u32[]{:S(2)}) copy-start(bf16[2,256,256]{2,1,0:T(8,128)(2,1)} %constant.72.clone.inner_back_ref) | copy-start | bytes 786436
  35.9 17.2 %copy-start.4 = (bf16[2,256,256]{2,1,0:T(8,128)(2,1)S(1)}, bf16[2,256,256]{2,1,0:T(8,128)(2,1)}, u32[]{:S(2)}) copy-start(bf16[2,256,256]{2,1,0:T(8,128)(2,1)} %constant.71.clone.inner_ref) | copy-start | bytes 786436
  35.9 17.2 %all-to-all-start = ((f32[128,3,128]{2,1,0:T(4,128)}), f32[128,3,128]{2,1,0:T(4,128)S(1)}, u32[]{:S(2)}, u32[]{:S(2)}) async-start(f32[128,3,128]{2,1,0:T(4,128)} %get-tuple-element.9), calls=%async_computation | async-start | bytes 524288 | tf_op jit(solution)/shard_map/all_to_all | solution.py:792
  42.0 11.1 %copy-start.6 = (f32[2,128,128]{2,1,0:T(8,128)S(1)}, f32[2,128,128]{2,1,0:T(8,128)}, u32[]{:S(2)}) copy-start(f32[2,128,128]{2,1,0:T(8,128)} %constant.73.clone.twist_ref) | copy-start | bytes 393220
  42.0 18.6 %collective-permute-start = (f32[6,128,128]{2,1,0:T(8,128)S(1)}, f32[6,128,128]{2,1,0:T(8,128)S(1)}, u32[]{:S(2)}, u32[]{:S(2)}) collective-permute-start(f32[6,128,128]{2,1,0:T(8,128)S(1)} %get-tuple-element.10.own_ref), channel_id=1, source_target_pairs={{0,120},{8,0},{16,8},{24,16},{32,24},{40,32},{48,40},{56,48},{64,5... | collective-permute-start | bytes 1179656 | tf_op jit(solution)/shard_map/ppermute | solution.py:788
  55.9 37.6 %all-to-all-start.1 = ((f32[128,3,128]{2,1,0:T(4,128)}), f32[128,3,128]{2,1,0:T(4,128)S(1)}, u32[]{:S(2)}, u32[]{:S(2)}) async-start(f32[128,3,128]{2,1,0:T(4,128)} %wave.1), calls=%async_computation.1 | async-start | bytes 524288 | tf_op jit(solution)/shard_map/all_to_all | solution.py:792
  93.6 49.9 %copy-start.5 = (f32[3,8192]{1,0:T(4,128)S(1)}, f32[3,8192]{1,0:T(4,128)}, u32[]{:S(2)}) copy-start(f32[3,8192]{1,0:T(4,128)} %noise_ref.1) | copy-start | bytes 294916
  93.6 49.9 %copy-start.10 = (s32[8192]{0:T(1024)S(1)}, s32[8192]{0:T(1024)}, u32[]{:S(2)}) copy-start(s32[8192]{0:T(1024)} %param.16) | copy-start | bytes 98308

commit v4 on v3

--- a/solution.py
+++ b/solution.py
@@ -105,50 +105,82 @@
     return ((place >> 13) << 7) | (place & 127)
 
 
-def scatter_rows(channels, rows, value_row, place_ref, left_ref, sum_ref):
-    group = left_ref.shape[1] // 128
-    span = 128 * group
-
-    def turn(g, _):
-        low = []
-        for j in range(group):
-            place = place_ref[pl.ds(g * group + j, 1), :]
+GROUP = 8
+WIDTH = 4
+
+
+def scatter_rows(channels, rows, row_at, value_row, place_ref, left, low, sum_ref, ready=None):
+    def build(g, side):
+        if ready is not None:
+            ready(g)
+        for j in range(GROUP):
+            r = row_at(g * GROUP + j)
+            place = place_ref[pl.ds(r, 1), :]
             high_hot = onehot(high_part(place), 64, 128)
-            low.append(onehot(low_part(place), 256, 128))
+            low[side][:, j * 128 : (j + 1) * 128] = onehot(low_part(place), 256, 128)
             for c in range(channels):
-                hi, lo = split2(value_row(c, g * group + j))
-                left_ref[c * 128 : c * 128 + 64, j * 128 : (j + 1) * 128] = high_hot * hi
-                left_ref[c * 128 + 64 : c * 128 + 128, j * 128 : (j + 1) * 128] = high_hot * lo
-        moved = dot_t(left_ref[...], jnp.concatenate(low, axis=1))
+                hi, lo = split2(value_row(c, r))
+                left[side][c * 128 : c * 128 + 64, j * 128 : (j + 1) * 128] = high_hot * hi
+                left[side][c * 128 + 64 : c * 128 + 128, j * 128 : (j + 1) * 128] = high_hot * lo
+
+    def use(side):
+        moved = dot_t(left[side][...], low[side][...])
         for c in range(channels):
             sum_ref[c * 64 : (c + 1) * 64, :] += (
                 moved[c * 128 : c * 128 + 64] + moved[c * 128 + 64 : c * 128 + 128]
             )
+
+    groups = rows // GROUP
+    sum_ref[...] = jnp.zeros_like(sum_ref)
+    build(0, 0)
+
+    def turn(h, _):
+        build(2 * h + 1, 1)
+        use(0)
+        build(2 * h + 2, 0)
+        use(1)
         return 0
 
-    sum_ref[...] = jnp.zeros_like(sum_ref)
-    lax.fori_loop(0, rows // group, turn, 0)
-
-
-def gather_rows(channels, table_hi_ref, table_lo_ref, place_ref, rows, put):
-    low, high = [], []
-    for r in rows:
-        place = place_ref[pl.ds(r, 1), :]
-        low.append(onehot(low_part(place), 256, 128))
-        high.append(high_part(place))
-    low = jnp.concatenate(low, axis=1)
-    high = jnp.concatenate(high, axis=1)
-    found = dot(table_hi_ref[...], low) + dot(table_lo_ref[...], low)
-    rows_of = lax.broadcasted_iota(jnp.int32, (64, len(rows) * 128), 0) == high
+    lax.fori_loop(0, groups // 2 - 1, turn, 0)
+    build(groups - 1, 1)
+    use(0)
+    use(1)
+
+
+def unpack_sums(channels, sum_ref, put):
     for c in range(channels):
-        got = jnp.sum(
-            jnp.where(rows_of, found[c * 64 : (c + 1) * 64], 0.0), axis=0, keepdims=True
-        )
-        for n in range(len(rows)):
-            put(c, n, got[:, n * 128 : (n + 1) * 128])
-
-
-WIDTH = 4
+        for half in range(2):
+            put(c, half, sum_ref[c * 64 : (c + 1) * 64, half * 128 : (half + 1) * 128])
+
+
+def gather_rows(channels, turns, row_at, table_hi_ref, table_lo_ref, place_ref, low, put):
+    def build(g, side):
+        for n in range(WIDTH):
+            place = place_ref[pl.ds(row_at(g, n), 1), :]
+            low[side][:, n * 128 : (n + 1) * 128] = onehot(low_part(place), 256, 128)
+
+    def use(g, side):
+        found = dot(table_hi_ref[...], low[side][...]) + dot(table_lo_ref[...], low[side][...])
+        for n in range(WIDTH):
+            high = high_part(place_ref[pl.ds(row_at(g, n), 1), :])
+            rows_of = lax.broadcasted_iota(jnp.int32, (64, 128), 0) == high
+            for c in range(channels):
+                part = found[c * 64 : (c + 1) * 64, n * 128 : (n + 1) * 128]
+                put(g, c, n, jnp.sum(jnp.where(rows_of, part, 0.0), axis=0, keepdims=True))
+
+    build(0, 0)
+
+    def turn(h, _):
+        build(2 * h + 1, 1)
+        use(2 * h, 0)
+        build(2 * h + 2, 0)
+        use(2 * h + 1, 1)
+        return 0
+
+    lax.fori_loop(0, turns // 2 - 1, turn, 0)
+    build(turns - 1, 1)
+    use(turns - 2, 0)
+    use(turns - 1, 1)
 
 
 def fill_table(c, plane, table_hi_ref, table_lo_ref):
@@ -228,11 +260,13 @@
     return [g - jnp.where(lane == 0, 0.0, behind(g)) for g in grad]
 
 
-def send_kernel(
-    members, n_gy, pos_ref, route_ref, in_ref, out_ref, plane_ref, left_ref, sum_ref, send_sem,
-    recv_sem,
+def arrive_kernel(
+    members, n_gx, n_gy, pos_ref, route_ref, order_ref, z_ref, grid_ref, beside_ref, spec_in_ref,
+    plane_ref, left_a, left_b, low_a, low_b, sum_ref, out_ref, in_ref, spec_ref,
+    send_sem, recv_sems, spec_send, spec_recv, side_send, side_recv,
 ):
-    me = lax.axis_index("gx") * n_gy + lax.axis_index("gy")
+    g_x = lax.axis_index("gx")
+    me = g_x * n_gy + lax.axis_index("gy")
     greet_all(me, n_gy, members)
     rows = route_ref.shape[0]
     for c in range(3):
@@ -241,74 +275,131 @@
     forces = chain_forces([plane_ref[c] for c in range(3)])
     for c in range(3):
         plane_ref[3 + c] = forces[c]
+    left, low = (left_a, left_b), (low_a, low_b)
     scatter_rows(
-        6, rows, lambda c, r: plane_ref[c, pl.ds(r, 1), :], route_ref, left_ref, sum_ref
+        6, rows, lambda n: n, lambda c, r: plane_ref[c, pl.ds(r, 1), :], route_ref, left, low, sum_ref
     )
-    for c in range(6):
-        out_ref[0:64, c, :] = sum_ref[c * 64 : (c + 1) * 64, 0:128]
-        out_ref[64:128, c, :] = sum_ref[c * 64 : (c + 1) * 64, 128:256]
+
+    def to_message(c, half, value):
+        out_ref[half * 64 : (half + 1) * 64, c, :] = value
+
+    unpack_sums(6, sum_ref, to_message)
     wait_for_all(members)
+    in_ref[me] = out_ref[me]
+    groups = members // GROUP
+
+    def send_group(g):
+        for j in range(GROUP):
+            if isinstance(g, int) and g * GROUP + j == 0:
+                continue
+            there = lax.rem(me + g * GROUP + j, members)
+            send_row(out_ref, in_ref, me, there, n_gy, send_sem, recv_sems.at[g])
+
+    def group_here(g):
+        if isinstance(g, int):
+            if g + 2 < groups:
+                send_group(g + 2)
+        else:
+            pl.when(g + 2 < groups)(partial(send_group, g + 2))
+        count = GROUP - 1 if isinstance(g, int) and g == 0 else GROUP
+        pltpu.make_async_remote_copy(
+            src_ref=out_ref.at[pl.ds(0, count)],
+            dst_ref=in_ref.at[pl.ds(0, count)],
+            send_sem=send_sem,
+            recv_sem=recv_sems.at[g],
+            device_id=(0, 0),
+            device_id_type=pl.DeviceIdType.MESH,
+        ).wait_recv()
+
+    send_group(0)
+    send_group(1)
+    scatter_rows(
+        6,
+        members,
+        lambda n: lax.rem(me + members - n, members),
+        lambda c, r: in_ref[r, c : c + 1, :],
+        order_ref,
+        left,
+        low,
+        sum_ref,
+        group_here,
+    )
+
+    def to_grid(c, half, value):
+        grid_ref[c, half * 64 : (half + 1) * 64, :] = value
+
+    unpack_sums(6, sum_ref, to_grid)
+    side = pltpu.make_async_remote_copy(
+        src_ref=grid_ref,
+        dst_ref=beside_ref,
+        send_sem=side_send,
+        recv_sem=side_recv,
+        device_id=(lax.rem(g_x + n_gx - 1, n_gx), lax.axis_index("gy")),
+        device_id_type=pl.DeviceIdType.MESH,
+    )
+    side.start()
+    for c in range(3):
+        hi, lo = split2(grid_ref[3 + c])
+        kind = 0 if c < 2 else 1
+        spec_ref[:, c, :] = dot3(z_ref[0, kind], z_ref[1, kind], hi, lo, dot_t)
 
     def go(d, _):
-        send_row(out_ref, in_ref, me, lax.rem(me + d, members), n_gy, send_sem, recv_sem)
+        there = lax.rem(me + d, members)
+        send_row(spec_ref, spec_in_ref, me, there, n_gy, spec_send, spec_recv)
         return 0
 
     lax.fori_loop(1, members, go, 0)
-    in_ref[me] = out_ref[me]
-    wait_rows(out_ref, in_ref, members, send_sem, recv_sem)
+    spec_in_ref[me] = spec_ref[me]
+    pltpu.make_async_remote_copy(
+        src_ref=out_ref.at[pl.ds(0, members - 1)],
+        dst_ref=in_ref.at[pl.ds(0, members - 1)],
+        send_sem=send_sem,
+        recv_sem=recv_sems.at[0],
+        device_id=(0, 0),
+        device_id_type=pl.DeviceIdType.MESH,
+    ).wait_send()
+    wait_rows(spec_ref, spec_in_ref, members, spec_send, spec_recv)
+    side.wait()
 
 
 def vmem(n):
     return [pl.BlockSpec(memory_space=pltpu.VMEM)] * n
 
 
-def send_message(positions, route):
-    n_gy = lax.axis_size("gy")
-    members = lax.axis_size("gx") * n_gy
+def arrive_on_grid(positions, route, order, z_table):
+    n_gx, n_gy = lax.axis_size("gx"), lax.axis_size("gy")
+    members = n_gx * n_gy
     return pl.pallas_call(
-        partial(send_kernel, members, n_gy),
-        out_shape=jax.ShapeDtypeStruct((128, 6, 128), f32),
-        in_specs=vmem(2),
-        out_specs=pl.BlockSpec(memory_space=pltpu.VMEM),
+        partial(arrive_kernel, members, n_gx, n_gy),
+        out_shape=[
+            jax.ShapeDtypeStruct((6, 128, 128), f32),
+            jax.ShapeDtypeStruct((6, 128, 128), f32),
+            jax.ShapeDtypeStruct((128, 3, 128), f32),
+        ],
+        in_specs=vmem(4),
+        out_specs=vmem(3),
         scratch_shapes=[
-            pltpu.VMEM((128, 6, 128), f32),
             pltpu.VMEM((6, 64, 128), f32),
             pltpu.VMEM((768, 1024), bf16),
+            pltpu.VMEM((768, 1024), bf16),
+            pltpu.VMEM((256, 1024), bf16),
+            pltpu.VMEM((256, 1024), bf16),
             pltpu.VMEM((384, 256), f32),
+            pltpu.VMEM((128, 6, 128), f32),
+            pltpu.VMEM((128, 6, 128), f32),
+            pltpu.VMEM((128, 3, 128), f32),
+            pltpu.SemaphoreType.DMA,
+            pltpu.SemaphoreType.DMA((128 // GROUP,)),
+            pltpu.SemaphoreType.DMA,
+            pltpu.SemaphoreType.DMA,
             pltpu.SemaphoreType.DMA,
             pltpu.SemaphoreType.DMA,
         ],
         compiler_params=pltpu.CompilerParams(
             vmem_limit_bytes=VMEM_LIMIT, collective_id=1, has_side_effects=True
         ),
-        name="send",
-    )(positions, route)
-
-
-def place_kernel(in_ref, order_ref, z_ref, out_ref, spec_ref, left_ref, sum_ref):
-    scatter_rows(6, 128, lambda c, r: in_ref[r, c : c + 1, :], order_ref, left_ref, sum_ref)
-    for c in range(6):
-        out_ref[c, 0:64, :] = sum_ref[c * 64 : (c + 1) * 64, 0:128]
-        out_ref[c, 64:128, :] = sum_ref[c * 64 : (c + 1) * 64, 128:256]
-    for c in range(3):
-        hi, lo = split2(out_ref[3 + c])
-        kind = 0 if c < 2 else 1
-        spec_ref[:, c, :] = dot3(z_ref[0, kind], z_ref[1, kind], hi, lo, dot_t)
-
-
-def place_on_grid(incoming, order, z_table):
-    return pl.pallas_call(
-        place_kernel,
-        out_shape=[
-            jax.ShapeDtypeStruct((6, 128, 128), f32),
-            jax.ShapeDtypeStruct((128, 3, 128), f32),
-        ],
-        in_specs=vmem(3),
-        out_specs=vmem(2),
-        scratch_shapes=[pltpu.VMEM((768, 1024), bf16), pltpu.VMEM((384, 256), f32)],
-        compiler_params=pltpu.CompilerParams(vmem_limit_bytes=VMEM_LIMIT),
-        name="place",
-    )(incoming, order, z_table)
+        name="arrive",
+    )(positions, route, order, z_table)
 
 
 def wave_kernel(
@@ -680,11 +771,16 @@
 
 def reply_kernel(
     members, n_gx, n_gy, own_ref, far_ref, wave_ref, order_ref, z_ref, in_ref, out_ref,
-    beside_ref, hi_ref, lo_ref, send_sem, recv_sem, far_send, far_recv,
+    beside_ref, hi_ref, lo_ref, low_a, low_b, send_sem, recv_sem, far_send, far_recv,
 ):
     g_x = lax.axis_index("gx")
     me = g_x * n_gy + lax.axis_index("gy")
     greet_all(me, n_gy, members)
+    waves = []
+    for c in range(3):
+        kind = 0 if c < 2 else 1
+        hi, lo = split2(jnp.transpose(wave_ref[:, c, :]))
+        waves.append(own_ref[c] + dot3(hi, lo, z_ref[0, kind], z_ref[1, kind]))
     wait_for_all(members)
     far = pltpu.make_async_remote_copy(
         src_ref=far_ref,
@@ -695,29 +791,23 @@
         device_id_type=pl.DeviceIdType.MESH,
     )
     far.start()
-    waves = []
-    for c in range(3):
-        kind = 0 if c < 2 else 1
-        hi, lo = split2(jnp.transpose(wave_ref[:, c, :]))
-        waves.append(own_ref[c] + dot3(hi, lo, z_ref[0, kind], z_ref[1, kind]))
     far.wait()
     for c in range(3):
         fill_table(c, waves[c] + beside_ref[c], hi_ref, lo_ref)
 
-    def turn(g, _):
-        rows = [lax.rem(me + 1 + g * WIDTH + j, members) for j in range(WIDTH)]
-
-        def put(c, n, row):
-            out_ref[rows[n], c : c + 1, :] = row
-
-        gather_rows(3, hi_ref, lo_ref, order_ref, rows, put)
-        for j, row in enumerate(rows):
-            pl.when(g * WIDTH + j < members - 1)(
-                partial(send_row, out_ref, in_ref, me, row, n_gy, send_sem, recv_sem)
-            )
-        return 0
-
-    lax.fori_loop(0, members // WIDTH, turn, 0)
+    def row_at(g, n):
+        return lax.rem(me + 1 + g * WIDTH + n, members)
+
+    def put(g, c, n, row):
+        there = row_at(g, n)
+        out_ref[there, c : c + 1, :] = row
+        if c == 2:
+            go = partial(send_row, out_ref, in_ref, me, there, n_gy, send_sem, recv_sem)
+            pl.when(g * WIDTH + n < members - 1)(go)
+
+    gather_rows(
+        3, members // WIDTH, row_at, hi_ref, lo_ref, order_ref, (low_a, low_b), put
+    )
     in_ref[me] = out_ref[me]
     wait_rows(out_ref, in_ref, members, send_sem, recv_sem)
 
@@ -735,6 +825,8 @@
             pltpu.VMEM((3, 128, 128), f32),
             pltpu.VMEM((192, 256), bf16),
             pltpu.VMEM((192, 256), bf16),
+            pltpu.VMEM((256, WIDTH * 128), bf16),
+            pltpu.VMEM((256, WIDTH * 128), bf16),
             pltpu.SemaphoreType.DMA,
             pltpu.SemaphoreType.DMA,
             pltpu.SemaphoreType.DMA,
@@ -747,19 +839,21 @@
     )(own_vel, far_vel, wave, order, z_table)
 
 
-def move_kernel(in_ref, route_ref, pos_ref, noise_ref, moved_ref, drift_ref, hi_ref, lo_ref, vel_ref):
+def move_kernel(
+    in_ref, route_ref, pos_ref, noise_ref, moved_ref, drift_ref, hi_ref, lo_ref, vel_ref, low_a,
+    low_b,
+):
     rows = route_ref.shape[0]
     for c in range(3):
         fill_table(c, in_ref[:, c, :], hi_ref, lo_ref)
 
-    def turn(g, _):
-        def put(c, n, row):
-            vel_ref[c, pl.ds(g * WIDTH + n, 1), :] = row
-
-        gather_rows(3, hi_ref, lo_ref, route_ref, [g * WIDTH + j for j in range(WIDTH)], put)
-        return 0
-
-    lax.fori_loop(0, rows // WIDTH, turn, 0)
+    def row_at(g, n):
+        return g * WIDTH + n
+
+    def put(g, c, n, row):
+        vel_ref[c, pl.ds(row_at(g, n), 1), :] = row
+
+    gather_rows(3, rows // WIDTH, row_at, hi_ref, lo_ref, route_ref, (low_a, low_b), put)
     for c in range(3):
         for r in range(rows):
             drift_ref[c : c + 1, r * 128 : (r + 1) * 128] = time_step * vel_ref[c, r : r + 1, :]
@@ -777,15 +871,12 @@
             pltpu.VMEM((192, 256), bf16),
             pltpu.VMEM((192, 256), bf16),
             pltpu.VMEM((3, 64, 128), f32),
+            pltpu.VMEM((256, WIDTH * 128), bf16),
+            pltpu.VMEM((256, WIDTH * 128), bf16),
         ],
         compiler_params=pltpu.CompilerParams(vmem_limit_bytes=VMEM_LIMIT),
         name="move",
     )(arrived, route, positions, noise)
-
-
-def shifted(value, axis, by):
-    devices = lax.axis_size(axis)
-    return lax.ppermute(value, axis, [(i, (i + by) % devices) for i in range(devices)])
 
 
 def exchange(value):
@@ -798,10 +889,8 @@
     member = row_gx * lax.axis_size("gy") + lax.axis_index("gy")
     route = route.reshape(64, 128)
     order = lax.dynamic_index_in_dim(node_perm, row_gx, 0, keepdims=False).reshape(128, 128)
-    incoming = send_message(positions, route)
-    grid, spec = place_on_grid(incoming, order, table["z"])
-    beside = shifted(grid, "gx", -1)
-    wave = wave_flow(exchange(spec), table, member)
+    grid, beside, spec = arrive_on_grid(positions, route, order, table["z"])
+    wave = wave_flow(spec, table, member)
     grid, wave = lax.optimization_barrier((grid, wave))
     wave = exchange(wave)
     lists = pair_lists(pair_first[0], pair_second[0], pair_count[0])

time: 150 us -> 174 us (1.16)
  Pallas kernels: 125 us -> 157 us
  starting transfers between devices: 16.2 us -> 7.82 us
  local copies, waits for them, and re-layouts: 2.1 us -> 7.15 us
  waiting for transfers between devices: 4.67 us -> 0.01 us
    pallas_call x2 -> x1, Pallas kernels: 33.2 us -> 66.1 us  [arrive_on_grid(): pl.pallas_call(partial(arrive_kernel, members, n_gx, n_gy), out_shape=[ja...]
    ppermute x1 -> x0, starting transfers between devices: 5.48 us -> none  [shifted(): lax.ppermute(value, axis, [(i, (i + by) % devices) for i in range(devices)])]
    unnamed x28, local copies, waits for them, and re-layouts: 2.02 us -> 7.07 us
    all_to_all x2 -> x1, waiting for transfers between devices: 4.67 us -> 0.01 us  [exchange(): lax.all_to_all(value, ('gx', 'gy'), split_axis=0, concat_axis=0, tiled=True)]
    all_to_all x2 -> x1, starting transfers between devices: 10.8 us -> 7.82 us  [exchange(): lax.all_to_all(value, ('gx', 'gy'), split_axis=0, concat_axis=0, tiled=True)]
  transfers between devices with their start and end apart: 3 -> 1, of which waited for: 1 -> 0; matrix products, arithmetic and copies ran while one was open for 0% -> 0% of each run, Pallas kernels for 24% -> 19%
where the time goes in v4:
time: 174 us
  Pallas kernels  157 us (90%)
  starting transfers between devices  7.82 us (4%)
  local copies, waits for them, and re-layouts  7.15 us (4%)
    pallas_call x1, Pallas kernels, arrive_on_grid(): pl.pallas_call(partial(arrive_kernel, members, n_gx, n_gy), out_shape=[ja...  66.1 us
    pallas_call x1, Pallas kernels, reply_message(): pl.pallas_call(partial(reply_kernel, members, n_gx, n_gy), out_shape=jax....  50.7 us
    pallas_call x1, Pallas kernels, pair_velocities(): pl.pallas_call(pair_kernel, out_shape=[plane, plane], in_specs=[pl.BlockS...  33 us
    all_to_all x1, starting transfers between devices, exchange(): lax.all_to_all(value, ('gx', 'gy'), split_axis=0, concat_axis=0, tiled=True)  7.82 us
    unnamed x28, local copies, waits for them, and re-layouts  7.07 us
    pallas_call x1, Pallas kernels, move_beads(): pl.pallas_call(move_kernel, out_shape=[flat, flat], in_specs=vmem(4), out...  4.73 us
  transfers between devices with their start and end apart: 1, of which 0 were waited for; matrix products, arithmetic and copies ran while one was open for 0% of the time, Pallas kernels for 19%

profile of v4, /device:TPU:1, one launch (start us, length us, event | category | flops | bytes accessed | tf_op | source)
XLA Modules:
  0.0 174.0 jit_solution(13289037007626783084)
XLA Ops:
  0.6 0.0 copy-start
  0.6 0.0 copy-start.1
  0.7 1.2 copy-done
  1.9 0.0 copy-start.7
  1.9 0.1 pad_maximum_fusion.part_ref
  1.9 0.0 copy-done.1
  1.9 0.7 copy-done.7
  2.6 0.0 copy-start.2
  2.6 0.9 copy-done.2
  3.5 0.0 copy-start.4
  3.5 66.1 %arrive.1 = (f32[6,128,128]{2,1,0:T(8,128)S(1)}, f32[6,128,128]{2,1,0:T(8,128)S(1)}, f32[128,3,128]{2,1,0:T(4,128)S(1)}) custom-call(f32[3,8192]{1,0:T(4,128)S(1)} %copy-done.1, s32[64,128]{1,0:T(8,128)S(1)} %bitcast.10, s32[128,128]{1,0:T(8,128)S(1)} %bitcast.8, bf16[2,2,128,128]{3,2,1,0:T(8,128)(2,1)S(1)} %copy-done.2), custom_call_target="tpu_custom_call" | custom-call | tf_op jit(solution)/shard_map/arrive/pallas_call | solution.py:372
  69.6 0.0 copy-done.4
  69.7 0.0 copy-start.5
  69.7 0.9 copy-done.5
  70.6 0.9 copy-done.8
  71.5 0.9 copy-done.9
  72.4 0.9 copy-done.10
  73.3 2.9 %wave.1 = f32[128,3,128]{2,1,0:T(4,128)} custom-call(f32[4]{0:T(128)S(1)} %pad_maximum_fusion.part_ref, f32[128,3,128]{2,1,0:T(4,128)S(1)} %get-tuple-element.10.in_ref, bf16[2,256,128]{2,1,0:T(8,128)(2,1)S(1)} %copy-done.10, bf16[2,128,256]{2,1,0:T(8,128)(2,1)S(1)} %copy-done.9, bf16[2,256,256]{2,1,0:T(8,128)(2,1)S(1)} %copy-done.5, ...), custom_call_target="tpu_custom_call" | custom-call | tf_op jit(solution)/shard_map/wave/pallas_call | solution.py:480
  76.2 7.8 %all-to-all-start = ((f32[128,3,128]{2,1,0:T(4,128)}), f32[128,3,128]{2,1,0:T(4,128)S(1)}, u32[]{:S(2)}, u32[]{:S(2)}) async-start(f32[128,3,128]{2,1,0:T(4,128)} %wave.1), calls=%async_computation | async-start | bytes 524288 | tf_op jit(solution)/shard_map/all_to_all | solution.py:883
  84.7 0.0 copy-done.11
  84.7 0.0 copy-done.12
  84.7 0.0 copy-start.13
  84.7 0.6 copy-done.13
  85.4 0.1 broadcast_in_dim.15
  85.5 0.0 copy-start.3
  85.5 33.0 %pairs.1 = (f32[3,128,128]{2,1,0:T(8,128)S(1)}, f32[3,128,128]{2,1,0:T(8,128)S(1)}) custom-call(s32[4,1152]{1,0:T(4,128)S(1)} %pad_add_fusion.list_ref, s32[1]{0:T(128)} %copy.16.count_ref, f32[6,128,128]{2,1,0:T(8,128)S(1)} %get-tuple-element.11.own_ref, f32[6,128,128]{2,1,0:T(8,128)S(1)} %get-tuple-element.12.beside_ref), custom_call_target="tpu_custom_call" | custom-call | flops 49999998976 | bytes 1048576 | tf_op jit(solution)/shard_map/pairs/pallas_call | solution.py:747
  118.5 0.0 all-to-all-done.wave_ref
  118.5 0.0 copy-done.3
  118.5 0.0 copy-start.6
  118.5 50.7 %reply.1.in_ref = f32[128,3,128]{2,1,0:T(4,128)S(1)} custom-call(f32[3,128,128]{2,1,0:T(8,128)S(1)} %get-tuple-element.13.own_ref, f32[3,128,128]{2,1,0:T(8,128)S(1)} %get-tuple-element.14.far_ref, f32[128,3,128]{2,1,0:T(4,128)S(1)} %all-to-all-done.wave_ref, s32[128,128]{1,0:T(8,128)S(1)} %bitcast.9, bf16[2,2,128,128]{3,2,1,0:T(8,128)(2,1)S(1)} %copy-done.3), custom_call_target="tpu_custom_call" | custom-call | tf_op jit(solution)/shard_map/reply/pallas_call | solution.py:818
  169.2 0.0 copy-done.6
  169.2 4.7 %move.1 = (f32[3,8192]{1,0:T(4,128)}, f32[3,8192]{1,0:T(4,128)}) custom-call(f32[128,3,128]{2,1,0:T(4,128)S(1)} %reply.1.in_ref, s32[64,128]{1,0:T(8,128)S(1)} %bitcast.11, f32[3,8192]{1,0:T(4,128)S(1)} %copy-done.1, f32[3,8192]{1,0:T(4,128)S(1)} %copy-done.6), custom_call_target="tpu_custom_call" | custom-call | tf_op jit(solution)/shard_map/move/pallas_call | solution.py:865
  (8 shorter events, 0.1 us)
Async XLA Ops:
  0.6 1.2 copy-start
  0.6 1.3 copy-start.1
  1.9 0.8 copy-start.7
  2.6 0.9 copy-start.2
  3.5 66.1 %copy-start.4 = (bf16[2,256,256]{2,1,0:T(8,128)(2,1)S(1)}, bf16[2,256,256]{2,1,0:T(8,128)(2,1)}, u32[]{:S(2)}) copy-start(bf16[2,256,256]{2,1,0:T(8,128)(2,1)} %constant.72.clone.inner_back_ref) | copy-start | bytes 786436
  69.7 1.0 copy-start.5
  70.6 0.9 copy-start.8
  71.5 0.9 copy-start.9
  72.4 0.9 copy-start.10
  76.2 8.5 %copy-start.11 = (s32[1,1024]{1,0:T(1,128)S(1)}, s32[1,1024]{1,0:T(1,128)}, u32[]{:S(2)}) copy-start(s32[1,1024]{1,0:T(1,128)} %param.18) | copy-start | bytes 12292
  76.2 8.5 %copy-start.12 = (s32[1,1024]{1,0:T(1,128)S(1)}, s32[1,1024]{1,0:T(1,128)}, u32[]{:S(2)}) copy-start(s32[1,1024]{1,0:T(1,128)} %param.19) | copy-start | bytes 12292
  76.2 42.3 %all-to-all-start = ((f32[128,3,128]{2,1,0:T(4,128)}), f32[128,3,128]{2,1,0:T(4,128)S(1)}, u32[]{:S(2)}, u32[]{:S(2)}) async-start(f32[128,3,128]{2,1,0:T(4,128)} %wave.1), calls=%async_computation | async-start | bytes 524288 | tf_op jit(solution)/shard_map/all_to_all | solution.py:883
  84.7 0.7 copy-start.13
  85.5 33.0 %copy-start.3 = (bf16[2,2,128,128]{3,2,1,0:T(8,128)(2,1)S(1)}, bf16[2,2,128,128]{3,2,1,0:T(8,128)(2,1)}, u32[]{:S(2)}) copy-start(bf16[2,2,128,128]{3,2,1,0:T(8,128)(2,1)} %constant.68.clone.z_ref) | copy-start | bytes 393220
  118.5 50.7 %copy-start.6 = (f32[3,8192]{1,0:T(4,128)S(1)}, f32[3,8192]{1,0:T(4,128)}, u32[]{:S(2)}) copy-start(f32[3,8192]{1,0:T(4,128)} %noise_ref.1) | copy-start | bytes 294916

commit v5 on v3

--- a/solution.py
+++ b/solution.py
@@ -105,6 +105,9 @@
     return ((place >> 13) << 7) | (place & 127)
 
 
+WIDTH = 4
+
+
 def scatter_rows(channels, rows, value_row, place_ref, left_ref, sum_ref):
     group = left_ref.shape[1] // 128
     span = 128 * group
@@ -130,25 +133,40 @@
     lax.fori_loop(0, rows // group, turn, 0)
 
 
-def gather_rows(channels, table_hi_ref, table_lo_ref, place_ref, rows, put):
-    low, high = [], []
-    for r in rows:
-        place = place_ref[pl.ds(r, 1), :]
-        low.append(onehot(low_part(place), 256, 128))
-        high.append(high_part(place))
-    low = jnp.concatenate(low, axis=1)
-    high = jnp.concatenate(high, axis=1)
-    found = dot(table_hi_ref[...], low) + dot(table_lo_ref[...], low)
-    rows_of = lax.broadcasted_iota(jnp.int32, (64, len(rows) * 128), 0) == high
+def unpack_sums(channels, sum_ref, put):
     for c in range(channels):
-        got = jnp.sum(
-            jnp.where(rows_of, found[c * 64 : (c + 1) * 64], 0.0), axis=0, keepdims=True
-        )
-        for n in range(len(rows)):
-            put(c, n, got[:, n * 128 : (n + 1) * 128])
-
-
-WIDTH = 4
+        for half in range(2):
+            put(c, half, sum_ref[c * 64 : (c + 1) * 64, half * 128 : (half + 1) * 128])
+
+
+def gather_rows(channels, turns, row_at, table_hi_ref, table_lo_ref, place_ref, low, put):
+    def build(g, side):
+        for n in range(WIDTH):
+            place = place_ref[pl.ds(row_at(g, n), 1), :]
+            low[side][:, n * 128 : (n + 1) * 128] = onehot(low_part(place), 256, 128)
+
+    def use(g, side):
+        found = dot(table_hi_ref[...], low[side][...]) + dot(table_lo_ref[...], low[side][...])
+        for n in range(WIDTH):
+            high = high_part(place_ref[pl.ds(row_at(g, n), 1), :])
+            rows_of = lax.broadcasted_iota(jnp.int32, (64, 128), 0) == high
+            for c in range(channels):
+                part = found[c * 64 : (c + 1) * 64, n * 128 : (n + 1) * 128]
+                put(g, c, n, jnp.sum(jnp.where(rows_of, part, 0.0), axis=0, keepdims=True))
+
+    build(0, 0)
+
+    def turn(h, _):
+        build(2 * h + 1, 1)
+        use(2 * h, 0)
+        build(2 * h + 2, 0)
+        use(2 * h + 1, 1)
+        return 0
+
+    lax.fori_loop(0, turns // 2 - 1, turn, 0)
+    build(turns - 1, 1)
+    use(turns - 2, 0)
+    use(turns - 1, 1)
 
 
 def fill_table(c, plane, table_hi_ref, table_lo_ref):
@@ -285,28 +303,71 @@
     )(positions, route)
 
 
-def place_kernel(in_ref, order_ref, z_ref, out_ref, spec_ref, left_ref, sum_ref):
-    scatter_rows(6, 128, lambda c, r: in_ref[r, c : c + 1, :], order_ref, left_ref, sum_ref)
-    for c in range(6):
-        out_ref[c, 0:64, :] = sum_ref[c * 64 : (c + 1) * 64, 0:128]
-        out_ref[c, 64:128, :] = sum_ref[c * 64 : (c + 1) * 64, 128:256]
-    for c in range(3):
-        hi, lo = split2(out_ref[3 + c])
+def place_kernel(
+    members, n_gx, n_gy, in_ref, order_ref, z_ref, grid_ref, beside_ref, spec_in_ref,
+    left_ref, sum_ref, spec_ref, spec_send, spec_recv, side_send, side_recv,
+):
+    g_x = lax.axis_index("gx")
+    me = g_x * n_gy + lax.axis_index("gy")
+    greet_all(me, n_gy, members)
+    scatter_rows(
+        6, members, lambda c, r: in_ref[r, c : c + 1, :], order_ref, left_ref, sum_ref
+    )
+
+    def to_grid(c, half, value):
+        grid_ref[c, half * 64 : (half + 1) * 64, :] = value
+
+    unpack_sums(6, sum_ref, to_grid)
+    for c in range(3):
+        hi, lo = split2(grid_ref[3 + c])
         kind = 0 if c < 2 else 1
         spec_ref[:, c, :] = dot3(z_ref[0, kind], z_ref[1, kind], hi, lo, dot_t)
+    wait_for_all(members)
+    side = pltpu.make_async_remote_copy(
+        src_ref=grid_ref,
+        dst_ref=beside_ref,
+        send_sem=side_send,
+        recv_sem=side_recv,
+        device_id=(lax.rem(g_x + n_gx - 1, n_gx), lax.axis_index("gy")),
+        device_id_type=pl.DeviceIdType.MESH,
+    )
+
+    def go(d, _):
+        there = lax.rem(me + d, members)
+        send_row(spec_ref, spec_in_ref, me, there, n_gy, spec_send, spec_recv)
+        return 0
+
+    lax.fori_loop(1, members, go, 0)
+    side.start()
+    spec_in_ref[me] = spec_ref[me]
+    wait_rows(spec_ref, spec_in_ref, members, spec_send, spec_recv)
+    side.wait()
 
 
 def place_on_grid(incoming, order, z_table):
+    n_gx, n_gy = lax.axis_size("gx"), lax.axis_size("gy")
+    members = n_gx * n_gy
     return pl.pallas_call(
-        place_kernel,
+        partial(place_kernel, members, n_gx, n_gy),
         out_shape=[
+            jax.ShapeDtypeStruct((6, 128, 128), f32),
             jax.ShapeDtypeStruct((6, 128, 128), f32),
             jax.ShapeDtypeStruct((128, 3, 128), f32),
         ],
         in_specs=vmem(3),
-        out_specs=vmem(2),
-        scratch_shapes=[pltpu.VMEM((768, 1024), bf16), pltpu.VMEM((384, 256), f32)],
-        compiler_params=pltpu.CompilerParams(vmem_limit_bytes=VMEM_LIMIT),
+        out_specs=vmem(3),
+        scratch_shapes=[
+            pltpu.VMEM((768, 1024), bf16),
+            pltpu.VMEM((384, 256), f32),
+            pltpu.VMEM((128, 3, 128), f32),
+            pltpu.SemaphoreType.DMA,
+            pltpu.SemaphoreType.DMA,
+            pltpu.SemaphoreType.DMA,
+            pltpu.SemaphoreType.DMA,
+        ],
+        compiler_params=pltpu.CompilerParams(
+            vmem_limit_bytes=VMEM_LIMIT, collective_id=3, has_side_effects=True
+        ),
         name="place",
     )(incoming, order, z_table)
 
@@ -680,11 +741,16 @@
 
 def reply_kernel(
     members, n_gx, n_gy, own_ref, far_ref, wave_ref, order_ref, z_ref, in_ref, out_ref,
-    beside_ref, hi_ref, lo_ref, send_sem, recv_sem, far_send, far_recv,
+    beside_ref, hi_ref, lo_ref, low_a, low_b, send_sem, recv_sem, far_send, far_recv,
 ):
     g_x = lax.axis_index("gx")
     me = g_x * n_gy + lax.axis_index("gy")
     greet_all(me, n_gy, members)
+    waves = []
+    for c in range(3):
+        kind = 0 if c < 2 else 1
+        hi, lo = split2(jnp.transpose(wave_ref[:, c, :]))
+        waves.append(own_ref[c] + dot3(hi, lo, z_ref[0, kind], z_ref[1, kind]))
     wait_for_all(members)
     far = pltpu.make_async_remote_copy(
         src_ref=far_ref,
@@ -695,29 +761,25 @@
         device_id_type=pl.DeviceIdType.MESH,
     )
     far.start()
-    waves = []
-    for c in range(3):
-        kind = 0 if c < 2 else 1
-        hi, lo = split2(jnp.transpose(wave_ref[:, c, :]))
-        waves.append(own_ref[c] + dot3(hi, lo, z_ref[0, kind], z_ref[1, kind]))
     far.wait()
     for c in range(3):
         fill_table(c, waves[c] + beside_ref[c], hi_ref, lo_ref)
 
-    def turn(g, _):
-        rows = [lax.rem(me + 1 + g * WIDTH + j, members) for j in range(WIDTH)]
-
-        def put(c, n, row):
-            out_ref[rows[n], c : c + 1, :] = row
-
-        gather_rows(3, hi_ref, lo_ref, order_ref, rows, put)
-        for j, row in enumerate(rows):
-            pl.when(g * WIDTH + j < members - 1)(
-                partial(send_row, out_ref, in_ref, me, row, n_gy, send_sem, recv_sem)
-            )
-        return 0
-
-    lax.fori_loop(0, members // WIDTH, turn, 0)
+    def row_at(g, n):
+        return g * WIDTH + n
+
+    def put(g, c, n, row):
+        out_ref[row_at(g, n), c : c + 1, :] = row
+
+    gather_rows(
+        3, members // WIDTH, row_at, hi_ref, lo_ref, order_ref, (low_a, low_b), put
+    )
+
+    def go(d, _):
+        send_row(out_ref, in_ref, me, lax.rem(me + d, members), n_gy, send_sem, recv_sem)
+        return 0
+
+    lax.fori_loop(1, members, go, 0)
     in_ref[me] = out_ref[me]
     wait_rows(out_ref, in_ref, members, send_sem, recv_sem)
 
@@ -735,6 +797,8 @@
             pltpu.VMEM((3, 128, 128), f32),
             pltpu.VMEM((192, 256), bf16),
             pltpu.VMEM((192, 256), bf16),
+            pltpu.VMEM((256, WIDTH * 128), bf16),
+            pltpu.VMEM((256, WIDTH * 128), bf16),
             pltpu.SemaphoreType.DMA,
             pltpu.SemaphoreType.DMA,
             pltpu.SemaphoreType.DMA,
@@ -747,19 +811,21 @@
     )(own_vel, far_vel, wave, order, z_table)
 
 
-def move_kernel(in_ref, route_ref, pos_ref, noise_ref, moved_ref, drift_ref, hi_ref, lo_ref, vel_ref):
+def move_kernel(
+    in_ref, route_ref, pos_ref, noise_ref, moved_ref, drift_ref, hi_ref, lo_ref, vel_ref, low_a,
+    low_b,
+):
     rows = route_ref.shape[0]
     for c in range(3):
         fill_table(c, in_ref[:, c, :], hi_ref, lo_ref)
 
-    def turn(g, _):
-        def put(c, n, row):
-            vel_ref[c, pl.ds(g * WIDTH + n, 1), :] = row
-
-        gather_rows(3, hi_ref, lo_ref, route_ref, [g * WIDTH + j for j in range(WIDTH)], put)
-        return 0
-
-    lax.fori_loop(0, rows // WIDTH, turn, 0)
+    def row_at(g, n):
+        return g * WIDTH + n
+
+    def put(g, c, n, row):
+        vel_ref[c, pl.ds(row_at(g, n), 1), :] = row
+
+    gather_rows(3, rows // WIDTH, row_at, hi_ref, lo_ref, route_ref, (low_a, low_b), put)
     for c in range(3):
         for r in range(rows):
             drift_ref[c : c + 1, r * 128 : (r + 1) * 128] = time_step * vel_ref[c, r : r + 1, :]
@@ -777,15 +843,12 @@
             pltpu.VMEM((192, 256), bf16),
             pltpu.VMEM((192, 256), bf16),
             pltpu.VMEM((3, 64, 128), f32),
+            pltpu.VMEM((256, WIDTH * 128), bf16),
+            pltpu.VMEM((256, WIDTH * 128), bf16),
         ],
         compiler_params=pltpu.CompilerParams(vmem_limit_bytes=VMEM_LIMIT),
         name="move",
     )(arrived, route, positions, noise)
-
-
-def shifted(value, axis, by):
-    devices = lax.axis_size(axis)
-    return lax.ppermute(value, axis, [(i, (i + by) % devices) for i in range(devices)])
 
 
 def exchange(value):
@@ -799,9 +862,8 @@
     route = route.reshape(64, 128)
     order = lax.dynamic_index_in_dim(node_perm, row_gx, 0, keepdims=False).reshape(128, 128)
     incoming = send_message(positions, route)
-    grid, spec = place_on_grid(incoming, order, table["z"])
-    beside = shifted(grid, "gx", -1)
-    wave = wave_flow(exchange(spec), table, member)
+    grid, beside, spec = place_on_grid(incoming, order, table["z"])
+    wave = wave_flow(spec, table, member)
     grid, wave = lax.optimization_barrier((grid, wave))
     wave = exchange(wave)
     lists = pair_lists(pair_first[0], pair_second[0], pair_count[0])

time: 150 us -> 150 us (level)
  Pallas kernels: 125 us -> 137 us
  starting transfers between devices: 16.2 us -> 8.44 us
  waiting for transfers between devices: 4.67 us -> 0.01 us
    pallas_call x1, Pallas kernels: 49.8 us -> 29.4 us  [reply_message(): pl.pallas_call(partial(reply_kernel, members, n_gx, n_gy), out_shape=jax....]
    pallas_call x1, Pallas kernels: 33 us -> 52.5 us  [pair_velocities(): pl.pallas_call(pair_kernel, out_shape=[plane, plane], in_specs=[pl.BlockS...]
    pallas_call x1, Pallas kernels: 11.5 us -> 26 us  [place_on_grid(): pl.pallas_call(partial(place_kernel, members, n_gx, n_gy), out_shape=[jax...]
    ppermute x1 -> x0, starting transfers between devices: 5.48 us -> none  [shifted(): lax.ppermute(value, axis, [(i, (i + by) % devices) for i in range(devices)])]
    all_to_all x2 -> x1, waiting for transfers between devices: 4.67 us -> 0.01 us  [exchange(): lax.all_to_all(value, ('gx', 'gy'), split_axis=0, concat_axis=0, tiled=True)]
    all_to_all x2 -> x1, starting transfers between devices: 10.8 us -> 8.44 us  [exchange(): lax.all_to_all(value, ('gx', 'gy'), split_axis=0, concat_axis=0, tiled=True)]
  transfers between devices with their start and end apart: 3 -> 1, of which waited for: 1 -> 0; matrix products, arithmetic and copies ran while one was open for 0% -> 0% of each run, Pallas kernels for 24% -> 35%
where the time goes in v5:
time: 150 us
  Pallas kernels  137 us (91%)
  starting transfers between devices  8.44 us (6%)
  local copies, waits for them, and re-layouts  2.68 us (2%)
  between operations  1.5 us (1%)
    pallas_call x1, Pallas kernels, pair_velocities(): pl.pallas_call(pair_kernel, out_shape=[plane, plane], in_specs=[pl.BlockS...  52.5 us
    pallas_call x1, Pallas kernels, reply_message(): pl.pallas_call(partial(reply_kernel, members, n_gx, n_gy), out_shape=jax....  29.4 us
    pallas_call x1, Pallas kernels, place_on_grid(): pl.pallas_call(partial(place_kernel, members, n_gx, n_gy), out_shape=[jax...  26 us
    pallas_call x1, Pallas kernels, send_message(): pl.pallas_call(partial(send_kernel, members, n_gy), out_shape=jax.ShapeDt...  21.9 us
    all_to_all x1, starting transfers between devices, exchange(): lax.all_to_all(value, ('gx', 'gy'), split_axis=0, concat_axis=0, tiled=True)  8.44 us
    pallas_call x1, Pallas kernels, move_beads(): pl.pallas_call(move_kernel, out_shape=[flat, flat], in_specs=vmem(4), out...  4.73 us
  transfers between devices with their start and end apart: 1, of which 0 were waited for; matrix products, arithmetic and copies ran while one was open for 0% of the time, Pallas kernels for 35%

profile of v5, /device:TPU:1, one launch (start us, length us, event | category | flops | bytes accessed | tf_op | source)
XLA Modules:
  0.0 150.1 jit_solution(3267104307474403401)
XLA Ops:
  0.6 0.0 copy-start
  0.6 0.0 copy-start.1
  0.7 1.2 copy-done
  1.9 0.0 copy-start.9
  1.9 0.0 copy-done.1
  1.9 0.7 copy-done.9
  2.6 0.0 copy-start.2
  2.6 21.9 %send.1.in_ref = f32[128,6,128]{2,1,0:T(8,128)S(1)} custom-call(f32[3,8192]{1,0:T(4,128)S(1)} %copy-done.1, s32[64,128]{1,0:T(8,128)S(1)} %bitcast.10), custom_call_target="tpu_custom_call" | custom-call | tf_op jit(solution)/shard_map/send/pallas_call | solution.py:286
  24.5 0.0 copy-done.2
  24.5 0.0 copy-start.3
  24.5 0.0 copy-start.4
  24.5 0.0 copy-start.6
  24.5 26.0 %place.1 = (f32[6,128,128]{2,1,0:T(8,128)S(1)}, f32[6,128,128]{2,1,0:T(8,128)S(1)}, f32[128,3,128]{2,1,0:T(4,128)S(1)}) custom-call(f32[128,6,128]{2,1,0:T(8,128)S(1)} %send.1.in_ref, s32[128,128]{1,0:T(8,128)S(1)} %bitcast.8, bf16[2,2,128,128]{3,2,1,0:T(8,128)(2,1)S(1)} %copy-done.2), custom_call_target="tpu_custom_call" | custom-call | tf_op jit(solution)/shard_map/place/pallas_call | solution.py:350
  50.6 0.1 pad_maximum_fusion.part_ref
  50.7 0.0 copy-done.7
  50.7 0.0 copy-done.8
  50.7 0.0 copy-done.3
  50.7 0.0 copy-done.4
  50.7 0.0 copy-done.6
  50.7 2.8 %wave.1 = f32[128,3,128]{2,1,0:T(4,128)} custom-call(f32[4]{0:T(128)S(1)} %pad_maximum_fusion.part_ref, f32[128,3,128]{2,1,0:T(4,128)S(1)} %get-tuple-element.10.in_ref, bf16[2,256,128]{2,1,0:T(8,128)(2,1)S(1)} %copy-done.6, bf16[2,128,256]{2,1,0:T(8,128)(2,1)S(1)} %copy-done.7, bf16[2,256,256]{2,1,0:T(8,128)(2,1)S(1)} %copy-done.3, ...), custom_call_target="tpu_custom_call" | custom-call | tf_op jit(solution)/shard_map/wave/pallas_call | solution.py:450
  53.6 8.4 %all-to-all-start = ((f32[128,3,128]{2,1,0:T(4,128)}), f32[128,3,128]{2,1,0:T(4,128)S(1)}, u32[]{:S(2)}, u32[]{:S(2)}) async-start(f32[128,3,128]{2,1,0:T(4,128)} %wave.1), calls=%async_computation | async-start | bytes 524288 | tf_op jit(solution)/shard_map/all_to_all | solution.py:855
  62.7 0.0 copy-done.10
  62.7 0.0 copy-done.11
  62.7 0.0 copy-start.12
  62.7 0.6 copy-done.12
  63.4 0.1 broadcast_in_dim.15
  63.5 52.5 %pairs.1 = (f32[3,128,128]{2,1,0:T(8,128)S(1)}, f32[3,128,128]{2,1,0:T(8,128)S(1)}) custom-call(s32[4,1152]{1,0:T(4,128)S(1)} %pad_add_fusion.list_ref, s32[1]{0:T(128)} %copy.16.count_ref, f32[6,128,128]{2,1,0:T(8,128)S(1)} %get-tuple-element.11.own_ref, f32[6,128,128]{2,1,0:T(8,128)S(1)} %get-tuple-element.12.beside_ref), custom_call_target="tpu_custom_call" | custom-call | flops 49999998976 | bytes 1048576 | tf_op jit(solution)/shard_map/pairs/pallas_call | solution.py:717
  115.9 0.0 all-to-all-done.wave_ref
  116.0 0.0 copy-start.5
  116.0 29.4 %reply.1.in_ref = f32[128,3,128]{2,1,0:T(4,128)S(1)} custom-call(f32[3,128,128]{2,1,0:T(8,128)S(1)} %get-tuple-element.13.own_ref, f32[3,128,128]{2,1,0:T(8,128)S(1)} %get-tuple-element.14.far_ref, f32[128,3,128]{2,1,0:T(4,128)S(1)} %all-to-all-done.wave_ref, s32[128,128]{1,0:T(8,128)S(1)} %bitcast.9, bf16[2,2,128,128]{3,2,1,0:T(8,128)(2,1)S(1)} %copy-done.2), custom_call_target="tpu_custom_call" | custom-call | tf_op jit(solution)/shard_map/reply/pallas_call | solution.py:790
  145.3 0.0 copy-done.5
  145.3 4.7 %move.1 = (f32[3,8192]{1,0:T(4,128)}, f32[3,8192]{1,0:T(4,128)}) custom-call(f32[128,3,128]{2,1,0:T(4,128)S(1)} %reply.1.in_ref, s32[64,128]{1,0:T(8,128)S(1)} %bitcast.11, f32[3,8192]{1,0:T(4,128)S(1)} %copy-done.1, f32[3,8192]{1,0:T(4,128)S(1)} %copy-done.5), custom_call_target="tpu_custom_call" | custom-call | tf_op jit(solution)/shard_map/move/pallas_call | solution.py:837
  (7 shorter events, 0.0 us)
Async XLA Ops:
  0.6 1.2 copy-start
  0.6 1.2 copy-start.1
  1.9 0.8 copy-start.9
  2.6 21.9 %copy-start.2 = (bf16[2,2,128,128]{3,2,1,0:T(8,128)(2,1)S(1)}, bf16[2,2,128,128]{3,2,1,0:T(8,128)(2,1)}, u32[]{:S(2)}) copy-start(bf16[2,2,128,128]{3,2,1,0:T(8,128)(2,1)} %constant.68.clone.z_ref) | copy-start | bytes 393220
  2.6 48.1 %copy-start.7 = (bf16[2,128,256]{2,1,0:T(8,128)(2,1)S(1)}, bf16[2,128,256]{2,1,0:T(8,128)(2,1)}, u32[]{:S(2)}) copy-start(bf16[2,128,256]{2,1,0:T(8,128)(2,1)} %constant.70.clone.outer_back_ref) | copy-start | bytes 393220
  2.6 48.1 %copy-start.8 = (f32[2,128,128]{2,1,0:T(8,128)S(1)}, f32[2,128,128]{2,1,0:T(8,128)}, u32[]{:S(2)}) copy-start(f32[2,128,128]{2,1,0:T(8,128)} %constant.73.clone.twist_ref) | copy-start | bytes 393220
  24.5 26.2 %copy-start.3 = (bf16[2,256,256]{2,1,0:T(8,128)(2,1)S(1)}, bf16[2,256,256]{2,1,0:T(8,128)(2,1)}, u32[]{:S(2)}) copy-start(bf16[2,256,256]{2,1,0:T(8,128)(2,1)} %constant.71.clone.inner_ref) | copy-start | bytes 786436
  24.5 26.2 %copy-start.4 = (bf16[2,256,256]{2,1,0:T(8,128)(2,1)S(1)}, bf16[2,256,256]{2,1,0:T(8,128)(2,1)}, u32[]{:S(2)}) copy-start(bf16[2,256,256]{2,1,0:T(8,128)(2,1)} %constant.72.clone.inner_back_ref) | copy-start | bytes 786436
  24.5 26.2 %copy-start.6 = (bf16[2,256,128]{2,1,0:T(8,128)(2,1)S(1)}, bf16[2,256,128]{2,1,0:T(8,128)(2,1)}, u32[]{:S(2)}) copy-start(bf16[2,256,128]{2,1,0:T(8,128)(2,1)} %constant.69.clone.outer_ref) | copy-start | bytes 393220
  53.6 9.1 %copy-start.10 = (s32[1,1024]{1,0:T(1,128)S(1)}, s32[1,1024]{1,0:T(1,128)}, u32[]{:S(2)}) copy-start(s32[1,1024]{1,0:T(1,128)} %param.18) | copy-start | bytes 12292
  53.6 9.1 %copy-start.11 = (s32[1,1024]{1,0:T(1,128)S(1)}, s32[1,1024]{1,0:T(1,128)}, u32[]{:S(2)}) copy-start(s32[1,1024]{1,0:T(1,128)} %param.19) | copy-start | bytes 12292
  53.6 62.4 %all-to-all-start = ((f32[128,3,128]{2,1,0:T(4,128)}), f32[128,3,128]{2,1,0:T(4,128)S(1)}, u32[]{:S(2)}, u32[]{:S(2)}) async-start(f32[128,3,128]{2,1,0:T(4,128)} %wave.1), calls=%async_computation | async-start | bytes 524288 | tf_op jit(solution)/shard_map/all_to_all | solution.py:855
  62.7 0.7 copy-start.12
  116.0 29.4 %copy-start.5 = (f32[3,8192]{1,0:T(4,128)S(1)}, f32[3,8192]{1,0:T(4,128)}, u32[]{:S(2)}) copy-start(f32[3,8192]{1,0:T(4,128)} %noise_ref.1) | copy-start | bytes 294916

commit v6 on v5

--- a/solution.py
+++ b/solution.py
@@ -176,35 +176,52 @@
         ref[c * 64 : (c + 1) * 64, 128:256] = part[64:128]
 
 
-def greet_all(me, n_gy, members):
+def wrapped(index, size):
+    return jnp.where(index >= size, index - size, index)
+
+
+def for_peers(n_gx, n_gy, do):
+    me_x, me_y = lax.axis_index("gx"), lax.axis_index("gy")
+    ys = [wrapped(me_y + d, n_gy) for d in range(n_gy)]
+    for y in ys[1:]:
+        do(me_x, y)
+
+    def turn(d, _):
+        x = wrapped(me_x + d, n_gx)
+        for y in ys:
+            do(x, y)
+        return 0
+
+    lax.fori_loop(1, n_gx, turn, 0)
+
+
+def greet_all(n_gx, n_gy):
     barrier = pltpu.get_barrier_semaphore()
 
-    def greet(d, _):
-        there = lax.rem(me + d, members)
+    def greet(x, y):
         pl.semaphore_signal(
-            barrier,
-            inc=1,
-            device_id=(there // n_gy, lax.rem(there, n_gy)),
-            device_id_type=pl.DeviceIdType.MESH,
+            barrier, inc=1, device_id=(x, y), device_id_type=pl.DeviceIdType.MESH
         )
-        return 0
-
-    lax.fori_loop(1, members, greet, 0)
+
+    for_peers(n_gx, n_gy, greet)
 
 
 def wait_for_all(members):
     pl.semaphore_wait(pltpu.get_barrier_semaphore(), members - 1)
 
 
-def send_row(out_ref, in_ref, me, there, n_gy, send_sem, recv_sem):
-    pltpu.make_async_remote_copy(
-        src_ref=out_ref.at[there],
-        dst_ref=in_ref.at[me],
-        send_sem=send_sem,
-        recv_sem=recv_sem,
-        device_id=(there // n_gy, lax.rem(there, n_gy)),
-        device_id_type=pl.DeviceIdType.MESH,
-    ).start()
+def send_rows(out_ref, in_ref, me, n_gx, n_gy, send_sem, recv_sem):
+    def send(x, y):
+        pltpu.make_async_remote_copy(
+            src_ref=out_ref.at[x * n_gy + y],
+            dst_ref=in_ref.at[me],
+            send_sem=send_sem,
+            recv_sem=recv_sem,
+            device_id=(x, y),
+            device_id_type=pl.DeviceIdType.MESH,
+        ).start()
+
+    for_peers(n_gx, n_gy, send)
 
 
 def wait_rows(out_ref, in_ref, members, send_sem, recv_sem):
@@ -247,11 +264,11 @@
 
 
 def send_kernel(
-    members, n_gy, pos_ref, route_ref, in_ref, out_ref, plane_ref, left_ref, sum_ref, send_sem,
+    members, n_gx, n_gy, pos_ref, route_ref, in_ref, out_ref, plane_ref, left_ref, sum_ref, send_sem,
     recv_sem,
 ):
     me = lax.axis_index("gx") * n_gy + lax.axis_index("gy")
-    greet_all(me, n_gy, members)
+    greet_all(n_gx, n_gy)
     rows = route_ref.shape[0]
     for c in range(3):
         for r in range(rows):
@@ -267,11 +284,7 @@
         out_ref[64:128, c, :] = sum_ref[c * 64 : (c + 1) * 64, 128:256]
     wait_for_all(members)
 
-    def go(d, _):
-        send_row(out_ref, in_ref, me, lax.rem(me + d, members), n_gy, send_sem, recv_sem)
-        return 0
-
-    lax.fori_loop(1, members, go, 0)
+    send_rows(out_ref, in_ref, me, n_gx, n_gy, send_sem, recv_sem)
     in_ref[me] = out_ref[me]
     wait_rows(out_ref, in_ref, members, send_sem, recv_sem)
 
@@ -281,10 +294,10 @@
 
 
 def send_message(positions, route):
-    n_gy = lax.axis_size("gy")
-    members = lax.axis_size("gx") * n_gy
+    n_gx, n_gy = lax.axis_size("gx"), lax.axis_size("gy")
+    members = n_gx * n_gy
     return pl.pallas_call(
-        partial(send_kernel, members, n_gy),
+        partial(send_kernel, members, n_gx, n_gy),
         out_shape=jax.ShapeDtypeStruct((128, 6, 128), f32),
         in_specs=vmem(2),
         out_specs=pl.BlockSpec(memory_space=pltpu.VMEM),
@@ -309,7 +322,7 @@
 ):
     g_x = lax.axis_index("gx")
     me = g_x * n_gy + lax.axis_index("gy")
-    greet_all(me, n_gy, members)
+    greet_all(n_gx, n_gy)
     scatter_rows(
         6, members, lambda c, r: in_ref[r, c : c + 1, :], order_ref, left_ref, sum_ref
     )
@@ -328,16 +341,11 @@
         dst_ref=beside_ref,
         send_sem=side_send,
         recv_sem=side_recv,
-        device_id=(lax.rem(g_x + n_gx - 1, n_gx), lax.axis_index("gy")),
+        device_id=(wrapped(g_x + n_gx - 1, n_gx), lax.axis_index("gy")),
         device_id_type=pl.DeviceIdType.MESH,
     )
 
-    def go(d, _):
-        there = lax.rem(me + d, members)
-        send_row(spec_ref, spec_in_ref, me, there, n_gy, spec_send, spec_recv)
-        return 0
-
-    lax.fori_loop(1, members, go, 0)
+    send_rows(spec_ref, spec_in_ref, me, n_gx, n_gy, spec_send, spec_recv)
     side.start()
     spec_in_ref[me] = spec_ref[me]
     wait_rows(spec_ref, spec_in_ref, members, spec_send, spec_recv)
@@ -745,7 +753,7 @@
 ):
     g_x = lax.axis_index("gx")
     me = g_x * n_gy + lax.axis_index("gy")
-    greet_all(me, n_gy, members)
+    greet_all(n_gx, n_gy)
     waves = []
     for c in range(3):
         kind = 0 if c < 2 else 1
@@ -757,7 +765,7 @@
         dst_ref=beside_ref,
         send_sem=far_send,
         recv_sem=far_recv,
-        device_id=(lax.rem(g_x + 1, n_gx), lax.axis_index("gy")),
+        device_id=(wrapped(g_x + 1, n_gx), lax.axis_index("gy")),
         device_id_type=pl.DeviceIdType.MESH,
     )
     far.start()
@@ -775,11 +783,7 @@
         3, members // WIDTH, row_at, hi_ref, lo_ref, order_ref, (low_a, low_b), put
     )
 
-    def go(d, _):
-        send_row(out_ref, in_ref, me, lax.rem(me + d, members), n_gy, send_sem, recv_sem)
-        return 0
-
-    lax.fori_loop(1, members, go, 0)
+    send_rows(out_ref, in_ref, me, n_gx, n_gy, send_sem, recv_sem)
     in_ref[me] = out_ref[me]
     wait_rows(out_ref, in_ref, members, send_sem, recv_sem)
 

time: 150 us -> 145 us (0.967)
  Pallas kernels: 137 us -> 132 us
    pallas_call x1, Pallas kernels: 52.5 us -> 32.9 us  [pair_velocities(): pl.pallas_call(pair_kernel, out_shape=[plane, plane], in_specs=[pl.BlockS...]
    pallas_call x1, Pallas kernels: 29.4 us -> 47.6 us  [reply_message(): pl.pallas_call(partial(reply_kernel, members, n_gx, n_gy), out_shape=jax....]
    pallas_call x1, Pallas kernels: 26 us -> 23.1 us  [place_on_grid(): pl.pallas_call(partial(place_kernel, members, n_gx, n_gy), out_shape=[jax...]
  transfers between devices with their start and end apart: 1 -> 1, of which waited for: 0 -> 0; matrix products, arithmetic and copies ran while one was open for 0% -> 0% of each run, Pallas kernels for 35% -> 23%
where the time goes in v6:
time: 145 us
  Pallas kernels  132 us (91%)
  starting transfers between devices  8.67 us (6%)
  local copies, waits for them, and re-layouts  2.68 us (2%)
  between operations  1.5 us (1%)
    pallas_call x1, Pallas kernels, reply_message(): pl.pallas_call(partial(reply_kernel, members, n_gx, n_gy), out_shape=jax....  47.6 us
    pallas_call x1, Pallas kernels, pair_velocities(): pl.pallas_call(pair_kernel, out_shape=[plane, plane], in_specs=[pl.BlockS...  32.9 us
    pallas_call x1, Pallas kernels, place_on_grid(): pl.pallas_call(partial(place_kernel, members, n_gx, n_gy), out_shape=[jax...  23.1 us
    pallas_call x1, Pallas kernels, send_message(): pl.pallas_call(partial(send_kernel, members, n_gx, n_gy), out_shape=jax.S...  20.4 us
    all_to_all x1, starting transfers between devices, exchange(): lax.all_to_all(value, ('gx', 'gy'), split_axis=0, concat_axis=0, tiled=True)  8.67 us
    pallas_call x1, Pallas kernels, move_beads(): pl.pallas_call(move_kernel, out_shape=[flat, flat], in_specs=vmem(4), out...  4.73 us
  transfers between devices with their start and end apart: 1, of which 0 were waited for; matrix products, arithmetic and copies ran while one was open for 0% of the time, Pallas kernels for 23%

profile of v6, /device:TPU:1, one launch (start us, length us, event | category | flops | bytes accessed | tf_op | source)
XLA Modules:
  0.0 144.6 jit_solution(17363396717798385686)
XLA Ops:
  0.6 0.0 copy-start
  0.6 0.0 copy-start.1
  0.7 1.2 copy-done
  1.9 0.0 copy-start.9
  1.9 0.0 copy-done.1
  1.9 0.7 copy-done.9
  2.6 0.0 copy-start.2
  2.6 20.4 %send.1.in_ref = f32[128,6,128]{2,1,0:T(8,128)S(1)} custom-call(f32[3,8192]{1,0:T(4,128)S(1)} %copy-done.1, s32[64,128]{1,0:T(8,128)S(1)} %bitcast.10), custom_call_target="tpu_custom_call" | custom-call | tf_op jit(solution)/shard_map/send/pallas_call | solution.py:299
  23.0 0.0 copy-done.2
  23.1 0.0 copy-start.3
  23.1 0.0 copy-start.4
  23.1 0.0 copy-start.6
  23.1 23.1 %place.1 = (f32[6,128,128]{2,1,0:T(8,128)S(1)}, f32[6,128,128]{2,1,0:T(8,128)S(1)}, f32[128,3,128]{2,1,0:T(4,128)S(1)}) custom-call(f32[128,6,128]{2,1,0:T(8,128)S(1)} %send.1.in_ref, s32[128,128]{1,0:T(8,128)S(1)} %bitcast.8, bf16[2,2,128,128]{3,2,1,0:T(8,128)(2,1)S(1)} %copy-done.2), custom_call_target="tpu_custom_call" | custom-call | tf_op jit(solution)/shard_map/place/pallas_call | solution.py:358
  46.2 0.1 pad_maximum_fusion.part_ref
  46.3 0.0 copy-done.7
  46.3 0.0 copy-done.8
  46.3 0.0 copy-done.3
  46.3 0.0 copy-done.4
  46.3 0.0 copy-done.6
  46.3 2.8 %wave.1 = f32[128,3,128]{2,1,0:T(4,128)} custom-call(f32[4]{0:T(128)S(1)} %pad_maximum_fusion.part_ref, f32[128,3,128]{2,1,0:T(4,128)S(1)} %get-tuple-element.10.in_ref, bf16[2,256,128]{2,1,0:T(8,128)(2,1)S(1)} %copy-done.6, bf16[2,128,256]{2,1,0:T(8,128)(2,1)S(1)} %copy-done.7, bf16[2,256,256]{2,1,0:T(8,128)(2,1)S(1)} %copy-done.3, ...), custom_call_target="tpu_custom_call" | custom-call | tf_op jit(solution)/shard_map/wave/pallas_call | solution.py:458
  49.2 8.7 %all-to-all-start = ((f32[128,3,128]{2,1,0:T(4,128)}), f32[128,3,128]{2,1,0:T(4,128)S(1)}, u32[]{:S(2)}, u32[]{:S(2)}) async-start(f32[128,3,128]{2,1,0:T(4,128)} %wave.1), calls=%async_computation | async-start | bytes 524288 | tf_op jit(solution)/shard_map/all_to_all | solution.py:859
  58.5 0.0 copy-done.10
  58.5 0.0 copy-done.11
  58.5 0.0 copy-start.12
  58.5 0.6 copy-done.12
  59.2 0.1 broadcast_in_dim.15
  59.3 32.9 %pairs.1 = (f32[3,128,128]{2,1,0:T(8,128)S(1)}, f32[3,128,128]{2,1,0:T(8,128)S(1)}) custom-call(s32[4,1152]{1,0:T(4,128)S(1)} %pad_add_fusion.list_ref, s32[1]{0:T(128)} %copy.16.count_ref, f32[6,128,128]{2,1,0:T(8,128)S(1)} %get-tuple-element.11.own_ref, f32[6,128,128]{2,1,0:T(8,128)S(1)} %get-tuple-element.12.beside_ref), custom_call_target="tpu_custom_call" | custom-call | flops 49999998976 | bytes 1048576 | tf_op jit(solution)/shard_map/pairs/pallas_call | solution.py:725
  92.2 0.0 all-to-all-done.wave_ref
  92.2 0.0 copy-start.5
  92.2 47.6 %reply.1.in_ref = f32[128,3,128]{2,1,0:T(4,128)S(1)} custom-call(f32[3,128,128]{2,1,0:T(8,128)S(1)} %get-tuple-element.13.own_ref, f32[3,128,128]{2,1,0:T(8,128)S(1)} %get-tuple-element.14.far_ref, f32[128,3,128]{2,1,0:T(4,128)S(1)} %all-to-all-done.wave_ref, s32[128,128]{1,0:T(8,128)S(1)} %bitcast.9, bf16[2,2,128,128]{3,2,1,0:T(8,128)(2,1)S(1)} %copy-done.2), custom_call_target="tpu_custom_call" | custom-call | tf_op jit(solution)/shard_map/reply/pallas_call | solution.py:794
  139.9 0.0 copy-done.5
  139.9 4.7 %move.1 = (f32[3,8192]{1,0:T(4,128)}, f32[3,8192]{1,0:T(4,128)}) custom-call(f32[128,3,128]{2,1,0:T(4,128)S(1)} %reply.1.in_ref, s32[64,128]{1,0:T(8,128)S(1)} %bitcast.11, f32[3,8192]{1,0:T(4,128)S(1)} %copy-done.1, f32[3,8192]{1,0:T(4,128)S(1)} %copy-done.5), custom_call_target="tpu_custom_call" | custom-call | tf_op jit(solution)/shard_map/move/pallas_call | solution.py:841
  (7 shorter events, 0.0 us)
Async XLA Ops:
  0.6 1.2 copy-start
  0.6 1.2 copy-start.1
  1.9 0.8 copy-start.9
  2.6 20.4 %copy-start.2 = (bf16[2,2,128,128]{3,2,1,0:T(8,128)(2,1)S(1)}, bf16[2,2,128,128]{3,2,1,0:T(8,128)(2,1)}, u32[]{:S(2)}) copy-start(bf16[2,2,128,128]{3,2,1,0:T(8,128)(2,1)} %constant.68.clone.z_ref) | copy-start | bytes 393220
  2.6 43.7 %copy-start.7 = (bf16[2,128,256]{2,1,0:T(8,128)(2,1)S(1)}, bf16[2,128,256]{2,1,0:T(8,128)(2,1)}, u32[]{:S(2)}) copy-start(bf16[2,128,256]{2,1,0:T(8,128)(2,1)} %constant.70.clone.outer_back_ref) | copy-start | bytes 393220
  2.6 43.7 %copy-start.8 = (f32[2,128,128]{2,1,0:T(8,128)S(1)}, f32[2,128,128]{2,1,0:T(8,128)}, u32[]{:S(2)}) copy-start(f32[2,128,128]{2,1,0:T(8,128)} %constant.73.clone.twist_ref) | copy-start | bytes 393220
  23.1 23.2 %copy-start.3 = (bf16[2,256,256]{2,1,0:T(8,128)(2,1)S(1)}, bf16[2,256,256]{2,1,0:T(8,128)(2,1)}, u32[]{:S(2)}) copy-start(bf16[2,256,256]{2,1,0:T(8,128)(2,1)} %constant.71.clone.inner_ref) | copy-start | bytes 786436
  23.1 23.2 %copy-start.4 = (bf16[2,256,256]{2,1,0:T(8,128)(2,1)S(1)}, bf16[2,256,256]{2,1,0:T(8,128)(2,1)}, u32[]{:S(2)}) copy-start(bf16[2,256,256]{2,1,0:T(8,128)(2,1)} %constant.72.clone.inner_back_ref) | copy-start | bytes 786436
  23.1 23.2 %copy-start.6 = (bf16[2,256,128]{2,1,0:T(8,128)(2,1)S(1)}, bf16[2,256,128]{2,1,0:T(8,128)(2,1)}, u32[]{:S(2)}) copy-start(bf16[2,256,128]{2,1,0:T(8,128)(2,1)} %constant.69.clone.outer_ref) | copy-start | bytes 393220
  49.2 9.3 %copy-start.10 = (s32[1,1024]{1,0:T(1,128)S(1)}, s32[1,1024]{1,0:T(1,128)}, u32[]{:S(2)}) copy-start(s32[1,1024]{1,0:T(1,128)} %param.18) | copy-start | bytes 12292
  49.2 9.3 %copy-start.11 = (s32[1,1024]{1,0:T(1,128)S(1)}, s32[1,1024]{1,0:T(1,128)}, u32[]{:S(2)}) copy-start(s32[1,1024]{1,0:T(1,128)} %param.19) | copy-start | bytes 12292
  49.2 43.0 %all-to-all-start = ((f32[128,3,128]{2,1,0:T(4,128)}), f32[128,3,128]{2,1,0:T(4,128)S(1)}, u32[]{:S(2)}, u32[]{:S(2)}) async-start(f32[128,3,128]{2,1,0:T(4,128)} %wave.1), calls=%async_computation | async-start | bytes 524288 | tf_op jit(solution)/shard_map/all_to_all | solution.py:859
  58.5 0.7 copy-start.12
  92.2 47.6 %copy-start.5 = (f32[3,8192]{1,0:T(4,128)S(1)}, f32[3,8192]{1,0:T(4,128)}, u32[]{:S(2)}) copy-start(f32[3,8192]{1,0:T(4,128)} %noise_ref.1) | copy-start | bytes 294916

commit v7 on v6

--- a/solution.py
+++ b/solution.py
@@ -264,11 +264,17 @@
 
 
 def send_kernel(
-    members, n_gx, n_gy, pos_ref, route_ref, in_ref, out_ref, plane_ref, left_ref, sum_ref, send_sem,
-    recv_sem,
+    members, n_gx, n_gy, pos_hbm, route_hbm, in_ref, pos_ref, route_ref, out_ref, plane_ref,
+    left_ref, sum_ref, send_sem, recv_sem, pos_sem, route_sem,
 ):
+    pos_copy = pltpu.make_async_copy(pos_hbm, pos_ref, pos_sem)
+    route_copy = pltpu.make_async_copy(route_hbm, route_ref, route_sem)
+    pos_copy.start()
+    route_copy.start()
     me = lax.axis_index("gx") * n_gy + lax.axis_index("gy")
     greet_all(n_gx, n_gy)
+    pos_copy.wait()
+    route_copy.wait()
     rows = route_ref.shape[0]
     for c in range(3):
         for r in range(rows):
@@ -299,13 +305,17 @@
     return pl.pallas_call(
         partial(send_kernel, members, n_gx, n_gy),
         out_shape=jax.ShapeDtypeStruct((128, 6, 128), f32),
-        in_specs=vmem(2),
+        in_specs=[pl.BlockSpec(memory_space=pltpu.HBM)] * 2,
         out_specs=pl.BlockSpec(memory_space=pltpu.VMEM),
         scratch_shapes=[
+            pltpu.VMEM(positions.shape, f32),
+            pltpu.VMEM(route.shape, jnp.int32),
             pltpu.VMEM((128, 6, 128), f32),
             pltpu.VMEM((6, 64, 128), f32),
             pltpu.VMEM((768, 1024), bf16),
             pltpu.VMEM((384, 256), f32),
+            pltpu.SemaphoreType.DMA,
+            pltpu.SemaphoreType.DMA,
             pltpu.SemaphoreType.DMA,
             pltpu.SemaphoreType.DMA,
         ],
@@ -331,10 +341,6 @@
         grid_ref[c, half * 64 : (half + 1) * 64, :] = value
 
     unpack_sums(6, sum_ref, to_grid)
-    for c in range(3):
-        hi, lo = split2(grid_ref[3 + c])
-        kind = 0 if c < 2 else 1
-        spec_ref[:, c, :] = dot3(z_ref[0, kind], z_ref[1, kind], hi, lo, dot_t)
     wait_for_all(members)
     side = pltpu.make_async_remote_copy(
         src_ref=grid_ref,
@@ -345,8 +351,12 @@
         device_id_type=pl.DeviceIdType.MESH,
     )
 
+    side.start()
+    for c in range(3):
+        hi, lo = split2(grid_ref[3 + c])
+        kind = 0 if c < 2 else 1
+        spec_ref[:, c, :] = dot3(z_ref[0, kind], z_ref[1, kind], hi, lo, dot_t)
     send_rows(spec_ref, spec_in_ref, me, n_gx, n_gy, spec_send, spec_recv)
-    side.start()
     spec_in_ref[me] = spec_ref[me]
     wait_rows(spec_ref, spec_in_ref, members, spec_send, spec_recv)
     side.wait()
@@ -618,37 +628,38 @@
         return found
 
     def scalars(s2_ref, tile_ref, pack):
-        half = pack % 2
-        along, across = pair_scalars(s2_ref[pack // 2, :, half * 128 : (half + 1) * 128])
+        lanes = slice(pack % 2 * 128, (pack % 2 + 1) * 128)
+        along, across = pair_scalars(s2_ref[pack // 2, :, lanes])
         for at, value in ((0, across), (128, along)):
             hi, lo = split2(value)
-            tile_ref[pack, at : at + 64, :] = hi
-            tile_ref[pack, at + 64 : at + 128, :] = lo
-
-    def sum_dots(step, tile_ref, pack):
-        tile = tile_ref[pack]
-        pairs = [blocks_of((step * 2 * GROUPS + pack) * 2 + s) for s in range(2)]
-        a = jnp.concatenate([weight_ref[i] for i, _ in pairs], axis=0)
-        b = jnp.concatenate(
-            [half_of(weight_ref[j], s) for s, (_, j) in enumerate(pairs)], axis=0
-        )
-        to_far = dot(a, jnp.concatenate([tile[0:128], tile[128:256]], axis=1))
-        return dot_t(b, tile), to_far
-
-    def add_sums(step, pack, to_near, to_far):
-        for s in range(2):
-            number = (step * 2 * GROUPS + pack) * 2 + s
-            for out, acc_ref, row, keep in (
-                (to_near, near_acc, list_ref[2, number], None),
-                (to_far, far_acc, list_ref[3, number], half_keep[s]),
-            ):
-                top = 32 * s
-                add_h = out[top : top + 16, 0:128] + out[top + 16 : top + 32, 0:128]
-                add_f = out[top : top + 8, 128:256] + out[top + 16 : top + 24, 128:256]
-                add = jnp.concatenate([add_h, add_f], axis=0)
-                if keep is not None:
-                    add = jnp.where(keep, add, 0.0)
-                acc_ref[pl.ds(pl.multiple_of(row, 8), W_ROWS), :] += add
+            tile_ref[pack // 2, at : at + 64, lanes] = hi
+            tile_ref[pack // 2, at + 64 : at + 128, lanes] = lo
+
+    def add_to(acc_ref, row, out, top, keep):
+        add_h = out[top : top + 16, 0:128] + out[top + 16 : top + 32, 0:128]
+        add_f = out[top : top + 8, 128:256] + out[top + 16 : top + 24, 128:256]
+        add = jnp.concatenate([add_h, add_f], axis=0)
+        if keep is not None:
+            add = jnp.where(keep, add, 0.0)
+        acc_ref[pl.ds(pl.multiple_of(row, 8), W_ROWS), :] += add
+
+    def sums(step, tile_ref, g):
+        numbers = [(step * GROUPS + g) * STEP + s for s in range(STEP)]
+        pairs = [blocks_of(n) for n in numbers]
+        near = []
+        for s, (_, j) in enumerate(pairs):
+            part = half_of(weight_ref[j], s % 2)
+            near.append(jnp.concatenate([nothing, part] if s // 2 else [part, nothing], axis=1))
+        to_near = dot_t(jnp.concatenate(near, axis=0), tile_ref[g])
+        for half in range(2):
+            lanes = slice(half * 128, (half + 1) * 128)
+            a = jnp.concatenate([weight_ref[pairs[2 * half + s][0]] for s in range(2)], axis=0)
+            tile = jnp.concatenate([tile_ref[g, 0:128, lanes], tile_ref[g, 128:256, lanes]], axis=1)
+            to_far = dot(a, tile)
+            for s in range(2):
+                add_to(far_acc, list_ref[3, numbers[2 * half + s]], to_far, 32 * s, half_keep[s])
+        for s in range(STEP):
+            add_to(near_acc, list_ref[2, numbers[s]], to_near, 32 * s, None)
 
     packs = range(2 * GROUPS)
 
@@ -659,8 +670,8 @@
     def stage(k, s2_next, s2_now, tile_now, tile_last):
         for pack in packs:
             scalars(s2_now, tile_now, pack)
-        for pack in packs:
-            add_sums(k - 1, pack, *sum_dots(k - 1, tile_last, pack))
+        for g in range(GROUPS):
+            sums(k - 1, tile_last, g)
         keep_distances(distance_dots(k + 1), s2_next)
 
     steps = (count + (STEP * GROUPS - 1)) // (STEP * GROUPS)
@@ -738,8 +749,8 @@
             pltpu.VMEM(((2 * BLOCKS + 1) * W_ROWS, 128), f32),
             pltpu.VMEM((GROUPS, 64, 256), f32),
             pltpu.VMEM((GROUPS, 64, 256), f32),
-            pltpu.VMEM((2 * GROUPS, 256, 128), bf16),
-            pltpu.VMEM((2 * GROUPS, 256, 128), bf16),
+            pltpu.VMEM((GROUPS, 256, 256), bf16),
+            pltpu.VMEM((GROUPS, 256, 256), bf16),
         ],
         compiler_params=pltpu.CompilerParams(vmem_limit_bytes=PAIR_VMEM),
         cost_estimate=cost(50),
@@ -748,17 +759,13 @@
 
 
 def reply_kernel(
-    members, n_gx, n_gy, own_ref, far_ref, wave_ref, order_ref, z_ref, in_ref, out_ref,
-    beside_ref, hi_ref, lo_ref, low_a, low_b, send_sem, recv_sem, far_send, far_recv,
+    members, n_gx, n_gy, own_ref, far_ref, flow_ref, order_ref, z_ref, in_ref, out_ref,
+    wave_ref, beside_ref, hi_ref, lo_ref, low_a, low_b, send_sem, recv_sem, far_send, far_recv,
+    wave_send, wave_recv,
 ):
     g_x = lax.axis_index("gx")
     me = g_x * n_gy + lax.axis_index("gy")
     greet_all(n_gx, n_gy)
-    waves = []
-    for c in range(3):
-        kind = 0 if c < 2 else 1
-        hi, lo = split2(jnp.transpose(wave_ref[:, c, :]))
-        waves.append(own_ref[c] + dot3(hi, lo, z_ref[0, kind], z_ref[1, kind]))
     wait_for_all(members)
     far = pltpu.make_async_remote_copy(
         src_ref=far_ref,
@@ -769,9 +776,15 @@
         device_id_type=pl.DeviceIdType.MESH,
     )
     far.start()
+    send_rows(flow_ref, wave_ref, me, n_gx, n_gy, wave_send, wave_recv)
+    wave_ref[me] = flow_ref[me]
     far.wait()
+    wait_rows(flow_ref, wave_ref, members, wave_send, wave_recv)
     for c in range(3):
-        fill_table(c, waves[c] + beside_ref[c], hi_ref, lo_ref)
+        kind = 0 if c < 2 else 1
+        hi, lo = split2(jnp.transpose(wave_ref[:, c, :]))
+        wave = dot3(hi, lo, z_ref[0, kind], z_ref[1, kind])
+        fill_table(c, own_ref[c] + beside_ref[c] + wave, hi_ref, lo_ref)
 
     def row_at(g, n):
         return g * WIDTH + n
@@ -798,11 +811,14 @@
         out_specs=pl.BlockSpec(memory_space=pltpu.VMEM),
         scratch_shapes=[
             pltpu.VMEM((128, 3, 128), f32),
+            pltpu.VMEM((128, 3, 128), f32),
             pltpu.VMEM((3, 128, 128), f32),
             pltpu.VMEM((192, 256), bf16),
             pltpu.VMEM((192, 256), bf16),
             pltpu.VMEM((256, WIDTH * 128), bf16),
             pltpu.VMEM((256, WIDTH * 128), bf16),
+            pltpu.SemaphoreType.DMA,
+            pltpu.SemaphoreType.DMA,
             pltpu.SemaphoreType.DMA,
             pltpu.SemaphoreType.DMA,
             pltpu.SemaphoreType.DMA,
@@ -855,10 +871,6 @@
     )(arrived, route, positions, noise)
 
 
-def exchange(value):
-    return lax.all_to_all(value, ("gx", "gy"), split_axis=0, concat_axis=0, tiled=True)
-
-
 def shards(positions, noise, route, node_perm, pair_first, pair_second, pair_count):
     table = {name: jnp.asarray(value) for name, value in tables().items()}
     row_gx = lax.axis_index("gx")
@@ -869,7 +881,6 @@
     grid, beside, spec = place_on_grid(incoming, order, table["z"])
     wave = wave_flow(spec, table, member)
     grid, wave = lax.optimization_barrier((grid, wave))
-    wave = exchange(wave)
     lists = pair_lists(pair_first[0], pair_second[0], pair_count[0])
     own_vel, far_vel = pair_velocities(grid, beside, lists, pair_count)
     reply = reply_message(own_vel, far_vel, wave, order, table["z"])

time: 145 us -> 145 us (level)
  starting transfers between devices: 8.67 us -> 0 us
  Pallas kernels: 132 us -> 140 us
    pallas_call x1, Pallas kernels: 32.9 us -> 54.2 us  [pair_velocities(): pl.pallas_call(pair_kernel, out_shape=[plane, plane], in_specs=[pl.BlockS...]
    pallas_call x1, Pallas kernels: 47.6 us -> 32.8 us  [reply_message(): pl.pallas_call(partial(reply_kernel, members, n_gx, n_gy), out_shape=jax....]
    all_to_all x1 -> x0, starting transfers between devices: 8.67 us -> none  [exchange(): lax.all_to_all(value, ('gx', 'gy'), split_axis=0, concat_axis=0, tiled=True)]
    pallas_call x1, Pallas kernels: 23.1 us -> 25.5 us  [place_on_grid(): pl.pallas_call(partial(place_kernel, members, n_gx, n_gy), out_shape=[jax...]
  transfers between devices with their start and end apart: 1 -> 0, of which waited for: 0 -> 0; matrix products, arithmetic and copies ran while one was open for 0% -> 0% of each run, Pallas kernels for 23% -> 0%
where the time goes in v7:
time: 145 us; the launch traced here: 144 us
  Pallas kernels  140 us (97%)
  local copies, waits for them, and re-layouts  2.62 us (2%)
  between operations  1.53 us (1%)
    pallas_call x1, Pallas kernels, pair_velocities(): pl.pallas_call(pair_kernel, out_shape=[plane, plane], in_specs=[pl.BlockS...  54.2 us
    pallas_call x1, Pallas kernels, reply_message(): pl.pallas_call(partial(reply_kernel, members, n_gx, n_gy), out_shape=jax....  32.8 us
    pallas_call x1, Pallas kernels, place_on_grid(): pl.pallas_call(partial(place_kernel, members, n_gx, n_gy), out_shape=[jax...  25.5 us
    pallas_call x1, Pallas kernels, send_message(): pl.pallas_call(partial(send_kernel, members, n_gx, n_gy), out_shape=jax.S...  20.7 us
    pallas_call x1, Pallas kernels, move_beads(): pl.pallas_call(move_kernel, out_shape=[flat, flat], in_specs=vmem(4), out...  4.73 us

profile of v7, /device:TPU:1, one launch (start us, length us, event | category | flops | bytes accessed | tf_op | source)
XLA Modules:
  0.0 144.3 jit_solution(14572024003942253589)
XLA Ops:
  0.6 0.0 copy-start
  0.6 0.0 copy-start.1
  0.7 0.1 pad_maximum_fusion.part_ref
  0.8 1.1 copy-done
  1.9 0.0 copy-start.9
  1.9 0.0 copy-done.1
  1.9 0.7 copy-done.9
  2.6 0.0 copy-start.2
  2.6 20.7 %send.1.in_ref = f32[128,6,128]{2,1,0:T(8,128)S(1)} custom-call(f32[3,8192]{1,0:T(4,128)S(1)} %copy-done.1, s32[64,128]{1,0:T(8,128)S(1)} %bitcast.10), custom_call_target="tpu_custom_call" | custom-call | tf_op jit(solution)/shard_map/send/pallas_call | solution.py:305
  23.3 0.0 copy-done.2
  23.3 0.0 copy-start.3
  23.3 0.0 copy-start.4
  23.3 0.0 copy-start.6
  23.3 25.5 %place.1 = (f32[6,128,128]{2,1,0:T(8,128)S(1)}, f32[6,128,128]{2,1,0:T(8,128)S(1)}, f32[128,3,128]{2,1,0:T(4,128)S(1)}) custom-call(f32[128,6,128]{2,1,0:T(8,128)S(1)} %send.1.in_ref, s32[128,128]{1,0:T(8,128)S(1)} %bitcast.8, bf16[2,2,128,128]{3,2,1,0:T(8,128)(2,1)S(1)} %copy-done.2), custom_call_target="tpu_custom_call" | custom-call | tf_op jit(solution)/shard_map/place/pallas_call | solution.py:368
  48.9 0.0 copy-done.7
  48.9 0.0 copy-done.8
  48.9 0.0 copy-done.3
  48.9 0.0 copy-done.4
  48.9 0.0 copy-done.6
  48.9 0.0 copy-start.11
  49.0 2.2 %wave.1.flow_ref = f32[128,3,128]{2,1,0:T(4,128)S(1)} custom-call(f32[4]{0:T(128)S(1)} %pad_maximum_fusion.part_ref, f32[128,3,128]{2,1,0:T(4,128)S(1)} %get-tuple-element.10.in_ref, bf16[2,256,128]{2,1,0:T(8,128)(2,1)S(1)} %copy-done.6, bf16[2,128,256]{2,1,0:T(8,128)(2,1)S(1)} %copy-done.7, bf16[2,256,256]{2,1,0:T(8,128)(2,1)S(1)} %copy-done.3, ...), custom_call_target="tpu_custom_call" | custom-call | tf_op jit(solution)/shard_map/wave/pallas_call | solution.py:468
  51.1 0.0 copy-start.10
  51.8 0.0 copy-done.11
  51.8 0.0 copy-done.10
  51.8 0.0 copy-start.12
  51.8 0.6 copy-done.12
  52.5 0.1 broadcast_in_dim.15
  52.6 54.2 %pairs.1 = (f32[3,128,128]{2,1,0:T(8,128)S(1)}, f32[3,128,128]{2,1,0:T(8,128)S(1)}) custom-call(s32[4,1152]{1,0:T(4,128)S(1)} %pad_add_fusion.list_ref, s32[1]{0:T(128)} %copy.16.count_ref, f32[6,128,128]{2,1,0:T(8,128)S(1)} %get-tuple-element.11.own_ref, f32[6,128,128]{2,1,0:T(8,128)S(1)} %get-tuple-element.12.beside_ref), custom_call_target="tpu_custom_call" | custom-call | flops 49999998976 | bytes 1048576 | tf_op jit(solution)/shard_map/pairs/pallas_call | solution.py:736
  106.8 0.0 copy-start.5
  106.8 32.8 %reply.1.in_ref = f32[128,3,128]{2,1,0:T(4,128)S(1)} custom-call(f32[3,128,128]{2,1,0:T(8,128)S(1)} %get-tuple-element.13.own_ref, f32[3,128,128]{2,1,0:T(8,128)S(1)} %get-tuple-element.14.far_ref, f32[128,3,128]{2,1,0:T(4,128)S(1)} %wave.1.flow_ref, s32[128,128]{1,0:T(8,128)S(1)} %bitcast.9, bf16[2,2,128,128]{3,2,1,0:T(8,128)(2,1)S(1)} %copy-done.2), custom_call_target="tpu_custom_call" | custom-call | tf_op jit(solution)/shard_map/reply/pallas_call | solution.py:807
  139.6 0.0 copy-done.5
  139.6 4.7 %move.1 = (f32[3,8192]{1,0:T(4,128)}, f32[3,8192]{1,0:T(4,128)}) custom-call(f32[128,3,128]{2,1,0:T(4,128)S(1)} %reply.1.in_ref, s32[64,128]{1,0:T(8,128)S(1)} %bitcast.11, f32[3,8192]{1,0:T(4,128)S(1)} %copy-done.1, f32[3,8192]{1,0:T(4,128)S(1)} %copy-done.5), custom_call_target="tpu_custom_call" | custom-call | tf_op jit(solution)/shard_map/move/pallas_call | solution.py:857
  (5 shorter events, 0.0 us)
Async XLA Ops:
  0.6 1.2 copy-start
  0.6 1.2 copy-start.1
  1.9 0.8 copy-start.9
  2.6 20.7 %copy-start.2 = (bf16[2,2,128,128]{3,2,1,0:T(8,128)(2,1)S(1)}, bf16[2,2,128,128]{3,2,1,0:T(8,128)(2,1)}, u32[]{:S(2)}) copy-start(bf16[2,2,128,128]{3,2,1,0:T(8,128)(2,1)} %constant.68.clone.z_ref) | copy-start | bytes 393220
  2.6 46.3 %copy-start.7 = (bf16[2,128,256]{2,1,0:T(8,128)(2,1)S(1)}, bf16[2,128,256]{2,1,0:T(8,128)(2,1)}, u32[]{:S(2)}) copy-start(bf16[2,128,256]{2,1,0:T(8,128)(2,1)} %constant.70.clone.outer_back_ref) | copy-start | bytes 393220
  2.6 46.3 %copy-start.8 = (f32[2,128,128]{2,1,0:T(8,128)S(1)}, f32[2,128,128]{2,1,0:T(8,128)}, u32[]{:S(2)}) copy-start(f32[2,128,128]{2,1,0:T(8,128)} %constant.73.clone.twist_ref) | copy-start | bytes 393220
  23.3 25.6 %copy-start.3 = (bf16[2,256,256]{2,1,0:T(8,128)(2,1)S(1)}, bf16[2,256,256]{2,1,0:T(8,128)(2,1)}, u32[]{:S(2)}) copy-start(bf16[2,256,256]{2,1,0:T(8,128)(2,1)} %constant.71.clone.inner_ref) | copy-start | bytes 786436
  23.3 25.6 %copy-start.4 = (bf16[2,256,256]{2,1,0:T(8,128)(2,1)S(1)}, bf16[2,256,256]{2,1,0:T(8,128)(2,1)}, u32[]{:S(2)}) copy-start(bf16[2,256,256]{2,1,0:T(8,128)(2,1)} %constant.72.clone.inner_back_ref) | copy-start | bytes 786436
  23.3 25.6 %copy-start.6 = (bf16[2,256,128]{2,1,0:T(8,128)(2,1)S(1)}, bf16[2,256,128]{2,1,0:T(8,128)(2,1)}, u32[]{:S(2)}) copy-start(bf16[2,256,128]{2,1,0:T(8,128)(2,1)} %constant.69.clone.outer_ref) | copy-start | bytes 393220
  48.9 2.8 %copy-start.11 = (s32[1,1024]{1,0:T(1,128)S(1)}, s32[1,1024]{1,0:T(1,128)}, u32[]{:S(2)}) copy-start(s32[1,1024]{1,0:T(1,128)} %param.19) | copy-start | bytes 12292
  51.1 0.7 copy-start.10
  51.8 0.7 copy-start.12
  106.8 32.8 %copy-start.5 = (f32[3,8192]{1,0:T(4,128)S(1)}, f32[3,8192]{1,0:T(4,128)}, u32[]{:S(2)}) copy-start(f32[3,8192]{1,0:T(4,128)} %noise_ref.1) | copy-start | bytes 294916

commit v8 on v6

--- a/solution.py
+++ b/solution.py
@@ -748,17 +748,13 @@
 
 
 def reply_kernel(
-    members, n_gx, n_gy, own_ref, far_ref, wave_ref, order_ref, z_ref, in_ref, out_ref,
-    beside_ref, hi_ref, lo_ref, low_a, low_b, send_sem, recv_sem, far_send, far_recv,
+    members, n_gx, n_gy, own_ref, far_ref, flow_ref, order_ref, z_ref, in_ref, out_ref,
+    wave_ref, beside_ref, hi_ref, lo_ref, low_a, low_b, send_sem, recv_sem, far_send, far_recv,
+    wave_send, wave_recv,
 ):
     g_x = lax.axis_index("gx")
     me = g_x * n_gy + lax.axis_index("gy")
     greet_all(n_gx, n_gy)
-    waves = []
-    for c in range(3):
-        kind = 0 if c < 2 else 1
-        hi, lo = split2(jnp.transpose(wave_ref[:, c, :]))
-        waves.append(own_ref[c] + dot3(hi, lo, z_ref[0, kind], z_ref[1, kind]))
     wait_for_all(members)
     far = pltpu.make_async_remote_copy(
         src_ref=far_ref,
@@ -769,9 +765,15 @@
         device_id_type=pl.DeviceIdType.MESH,
     )
     far.start()
+    send_rows(flow_ref, wave_ref, me, n_gx, n_gy, wave_send, wave_recv)
+    wave_ref[me] = flow_ref[me]
     far.wait()
+    wait_rows(flow_ref, wave_ref, members, wave_send, wave_recv)
     for c in range(3):
-        fill_table(c, waves[c] + beside_ref[c], hi_ref, lo_ref)
+        kind = 0 if c < 2 else 1
+        hi, lo = split2(jnp.transpose(wave_ref[:, c, :]))
+        wave = dot3(hi, lo, z_ref[0, kind], z_ref[1, kind])
+        fill_table(c, own_ref[c] + beside_ref[c] + wave, hi_ref, lo_ref)
 
     def row_at(g, n):
         return g * WIDTH + n
@@ -798,11 +800,14 @@
         out_specs=pl.BlockSpec(memory_space=pltpu.VMEM),
         scratch_shapes=[
             pltpu.VMEM((128, 3, 128), f32),
+            pltpu.VMEM((128, 3, 128), f32),
             pltpu.VMEM((3, 128, 128), f32),
             pltpu.VMEM((192, 256), bf16),
             pltpu.VMEM((192, 256), bf16),
             pltpu.VMEM((256, WIDTH * 128), bf16),
             pltpu.VMEM((256, WIDTH * 128), bf16),
+            pltpu.SemaphoreType.DMA,
+            pltpu.SemaphoreType.DMA,
             pltpu.SemaphoreType.DMA,
             pltpu.SemaphoreType.DMA,
             pltpu.SemaphoreType.DMA,
@@ -855,10 +860,6 @@
     )(arrived, route, positions, noise)
 
 
-def exchange(value):
-    return lax.all_to_all(value, ("gx", "gy"), split_axis=0, concat_axis=0, tiled=True)
-
-
 def shards(positions, noise, route, node_perm, pair_first, pair_second, pair_count):
     table = {name: jnp.asarray(value) for name, value in tables().items()}
     row_gx = lax.axis_index("gx")
@@ -869,7 +870,6 @@
     grid, beside, spec = place_on_grid(incoming, order, table["z"])
     wave = wave_flow(spec, table, member)
     grid, wave = lax.optimization_barrier((grid, wave))
-    wave = exchange(wave)
     lists = pair_lists(pair_first[0], pair_second[0], pair_count[0])
     own_vel, far_vel = pair_velocities(grid, beside, lists, pair_count)
     reply = reply_message(own_vel, far_vel, wave, order, table["z"])

time: 145 us -> 140 us (0.966)
  starting transfers between devices: 8.67 us -> 0 us
  Pallas kernels: 132 us -> 136 us
    pallas_call x1, Pallas kernels: 32.9 us -> 52.4 us  [pair_velocities(): pl.pallas_call(pair_kernel, out_shape=[plane, plane], in_specs=[pl.BlockS...]
    pallas_call x1, Pallas kernels: 47.6 us -> 33 us  [reply_message(): pl.pallas_call(partial(reply_kernel, members, n_gx, n_gy), out_shape=jax....]
    all_to_all x1 -> x0, starting transfers between devices: 8.67 us -> none  [exchange(): lax.all_to_all(value, ('gx', 'gy'), split_axis=0, concat_axis=0, tiled=True)]
  transfers between devices with their start and end apart: 1 -> 0, of which waited for: 0 -> 0; matrix products, arithmetic and copies ran while one was open for 0% -> 0% of each run, Pallas kernels for 23% -> 0%
where the time goes in v8:
time: 140 us
  Pallas kernels  136 us (97%)
  local copies, waits for them, and re-layouts  2.62 us (2%)
  between operations  1.53 us (1%)
    pallas_call x1, Pallas kernels, pair_velocities(): pl.pallas_call(pair_kernel, out_shape=[plane, plane], in_specs=[pl.BlockS...  52.4 us
    pallas_call x1, Pallas kernels, reply_message(): pl.pallas_call(partial(reply_kernel, members, n_gx, n_gy), out_shape=jax....  33 us
    pallas_call x1, Pallas kernels, place_on_grid(): pl.pallas_call(partial(place_kernel, members, n_gx, n_gy), out_shape=[jax...  23.1 us
    pallas_call x1, Pallas kernels, send_message(): pl.pallas_call(partial(send_kernel, members, n_gx, n_gy), out_shape=jax.S...  20.4 us
    pallas_call x1, Pallas kernels, move_beads(): pl.pallas_call(move_kernel, out_shape=[flat, flat], in_specs=vmem(4), out...  4.72 us

profile of v8, /device:TPU:1, one launch (start us, length us, event | category | flops | bytes accessed | tf_op | source)
XLA Modules:
  0.0 140.1 jit_solution(17603021771427873706)
XLA Ops:
  0.6 0.0 copy-start
  0.6 0.0 copy-start.1
  0.7 0.1 pad_maximum_fusion.part_ref
  0.8 1.1 copy-done
  1.9 0.0 copy-start.9
  1.9 0.0 copy-done.1
  1.9 0.7 copy-done.9
  2.6 0.0 copy-start.2
  2.6 20.4 %send.1.in_ref = f32[128,6,128]{2,1,0:T(8,128)S(1)} custom-call(f32[3,8192]{1,0:T(4,128)S(1)} %copy-done.1, s32[64,128]{1,0:T(8,128)S(1)} %bitcast.10), custom_call_target="tpu_custom_call" | custom-call | tf_op jit(solution)/shard_map/send/pallas_call | solution.py:299
  23.0 0.0 copy-done.2
  23.1 0.0 copy-start.3
  23.1 0.0 copy-start.4
  23.1 0.0 copy-start.6
  23.1 23.1 %place.1 = (f32[6,128,128]{2,1,0:T(8,128)S(1)}, f32[6,128,128]{2,1,0:T(8,128)S(1)}, f32[128,3,128]{2,1,0:T(4,128)S(1)}) custom-call(f32[128,6,128]{2,1,0:T(8,128)S(1)} %send.1.in_ref, s32[128,128]{1,0:T(8,128)S(1)} %bitcast.8, bf16[2,2,128,128]{3,2,1,0:T(8,128)(2,1)S(1)} %copy-done.2), custom_call_target="tpu_custom_call" | custom-call | tf_op jit(solution)/shard_map/place/pallas_call | solution.py:358
  46.2 0.0 copy-done.7
  46.2 0.0 copy-done.8
  46.2 0.0 copy-done.3
  46.2 0.0 copy-done.4
  46.3 0.0 copy-done.6
  46.3 0.0 copy-start.11
  46.3 2.2 %wave.1.flow_ref = f32[128,3,128]{2,1,0:T(4,128)S(1)} custom-call(f32[4]{0:T(128)S(1)} %pad_maximum_fusion.part_ref, f32[128,3,128]{2,1,0:T(4,128)S(1)} %get-tuple-element.10.in_ref, bf16[2,256,128]{2,1,0:T(8,128)(2,1)S(1)} %copy-done.6, bf16[2,128,256]{2,1,0:T(8,128)(2,1)S(1)} %copy-done.7, bf16[2,256,256]{2,1,0:T(8,128)(2,1)S(1)} %copy-done.3, ...), custom_call_target="tpu_custom_call" | custom-call | tf_op jit(solution)/shard_map/wave/pallas_call | solution.py:458
  48.4 0.0 copy-start.10
  49.1 0.0 copy-done.11
  49.1 0.0 copy-done.10
  49.2 0.0 copy-start.12
  49.2 0.6 copy-done.12
  49.8 0.1 broadcast_in_dim.15
  49.9 52.4 %pairs.1 = (f32[3,128,128]{2,1,0:T(8,128)S(1)}, f32[3,128,128]{2,1,0:T(8,128)S(1)}) custom-call(s32[4,1152]{1,0:T(4,128)S(1)} %pad_add_fusion.list_ref, s32[1]{0:T(128)} %copy.16.count_ref, f32[6,128,128]{2,1,0:T(8,128)S(1)} %get-tuple-element.11.own_ref, f32[6,128,128]{2,1,0:T(8,128)S(1)} %get-tuple-element.12.beside_ref), custom_call_target="tpu_custom_call" | custom-call | flops 49999998976 | bytes 1048576 | tf_op jit(solution)/shard_map/pairs/pallas_call | solution.py:725
  102.4 0.0 copy-start.5
  102.4 33.0 %reply.1.in_ref = f32[128,3,128]{2,1,0:T(4,128)S(1)} custom-call(f32[3,128,128]{2,1,0:T(8,128)S(1)} %get-tuple-element.13.own_ref, f32[3,128,128]{2,1,0:T(8,128)S(1)} %get-tuple-element.14.far_ref, f32[128,3,128]{2,1,0:T(4,128)S(1)} %wave.1.flow_ref, s32[128,128]{1,0:T(8,128)S(1)} %bitcast.9, bf16[2,2,128,128]{3,2,1,0:T(8,128)(2,1)S(1)} %copy-done.2), custom_call_target="tpu_custom_call" | custom-call | tf_op jit(solution)/shard_map/reply/pallas_call | solution.py:796
  135.4 0.0 copy-done.5
  135.4 4.7 %move.1 = (f32[3,8192]{1,0:T(4,128)}, f32[3,8192]{1,0:T(4,128)}) custom-call(f32[128,3,128]{2,1,0:T(4,128)S(1)} %reply.1.in_ref, s32[64,128]{1,0:T(8,128)S(1)} %bitcast.11, f32[3,8192]{1,0:T(4,128)S(1)} %copy-done.1, f32[3,8192]{1,0:T(4,128)S(1)} %copy-done.5), custom_call_target="tpu_custom_call" | custom-call | tf_op jit(solution)/shard_map/move/pallas_call | solution.py:846
  (5 shorter events, 0.0 us)
Async XLA Ops:
  0.6 1.2 copy-start
  0.6 1.2 copy-start.1
  1.9 0.8 copy-start.9
  2.6 20.4 %copy-start.2 = (bf16[2,2,128,128]{3,2,1,0:T(8,128)(2,1)S(1)}, bf16[2,2,128,128]{3,2,1,0:T(8,128)(2,1)}, u32[]{:S(2)}) copy-start(bf16[2,2,128,128]{3,2,1,0:T(8,128)(2,1)} %constant.68.clone.z_ref) | copy-start | bytes 393220
  2.6 43.6 %copy-start.7 = (bf16[2,128,256]{2,1,0:T(8,128)(2,1)S(1)}, bf16[2,128,256]{2,1,0:T(8,128)(2,1)}, u32[]{:S(2)}) copy-start(bf16[2,128,256]{2,1,0:T(8,128)(2,1)} %constant.70.clone.outer_back_ref) | copy-start | bytes 393220
  2.6 43.6 %copy-start.8 = (f32[2,128,128]{2,1,0:T(8,128)S(1)}, f32[2,128,128]{2,1,0:T(8,128)}, u32[]{:S(2)}) copy-start(f32[2,128,128]{2,1,0:T(8,128)} %constant.73.clone.twist_ref) | copy-start | bytes 393220
  23.1 23.2 %copy-start.3 = (bf16[2,256,256]{2,1,0:T(8,128)(2,1)S(1)}, bf16[2,256,256]{2,1,0:T(8,128)(2,1)}, u32[]{:S(2)}) copy-start(bf16[2,256,256]{2,1,0:T(8,128)(2,1)} %constant.71.clone.inner_ref) | copy-start | bytes 786436
  23.1 23.2 %copy-start.4 = (bf16[2,256,256]{2,1,0:T(8,128)(2,1)S(1)}, bf16[2,256,256]{2,1,0:T(8,128)(2,1)}, u32[]{:S(2)}) copy-start(bf16[2,256,256]{2,1,0:T(8,128)(2,1)} %constant.72.clone.inner_back_ref) | copy-start | bytes 786436
  23.1 23.2 %copy-start.6 = (bf16[2,256,128]{2,1,0:T(8,128)(2,1)S(1)}, bf16[2,256,128]{2,1,0:T(8,128)(2,1)}, u32[]{:S(2)}) copy-start(bf16[2,256,128]{2,1,0:T(8,128)(2,1)} %constant.69.clone.outer_ref) | copy-start | bytes 393220
  46.3 2.9 %copy-start.11 = (s32[1,1024]{1,0:T(1,128)S(1)}, s32[1,1024]{1,0:T(1,128)}, u32[]{:S(2)}) copy-start(s32[1,1024]{1,0:T(1,128)} %param.19) | copy-start | bytes 12292
  48.4 0.7 copy-start.10
  49.2 0.7 copy-start.12
  102.4 33.0 %copy-start.5 = (f32[3,8192]{1,0:T(4,128)S(1)}, f32[3,8192]{1,0:T(4,128)}, u32[]{:S(2)}) copy-start(f32[3,8192]{1,0:T(4,128)} %noise_ref.1) | copy-start | bytes 294916

commit v9 on v8

--- a/solution.py
+++ b/solution.py
@@ -317,8 +317,9 @@
 
 
 def place_kernel(
-    members, n_gx, n_gy, in_ref, order_ref, z_ref, grid_ref, beside_ref, spec_in_ref,
-    left_ref, sum_ref, spec_ref, spec_send, spec_recv, side_send, side_recv,
+    members, n_gx, n_gy, part_ref, in_ref, order_ref, z_ref, outer_ref, outer_back_ref, inner_ref,
+    inner_back_ref, twist_ref, grid_ref, beside_ref, flow_ref, left_ref, sum_ref, spec_ref,
+    spec_in_ref, mid_ref, spec_send, spec_recv, side_send, side_recv,
 ):
     g_x = lax.axis_index("gx")
     me = g_x * n_gy + lax.axis_index("gy")
@@ -349,10 +350,14 @@
     side.start()
     spec_in_ref[me] = spec_ref[me]
     wait_rows(spec_ref, spec_in_ref, members, spec_send, spec_recv)
+    wave_part(
+        part_ref, spec_in_ref, outer_ref, outer_back_ref, inner_ref, inner_back_ref, twist_ref,
+        flow_ref, mid_ref,
+    )
     side.wait()
 
 
-def place_on_grid(incoming, order, z_table):
+def place_on_grid(incoming, order, table, member):
     n_gx, n_gy = lax.axis_size("gx"), lax.axis_size("gy")
     members = n_gx * n_gy
     return pl.pallas_call(
@@ -362,12 +367,14 @@
             jax.ShapeDtypeStruct((6, 128, 128), f32),
             jax.ShapeDtypeStruct((128, 3, 128), f32),
         ],
-        in_specs=vmem(3),
+        in_specs=[pl.BlockSpec(memory_space=pltpu.SMEM)] + vmem(8),
         out_specs=vmem(3),
         scratch_shapes=[
             pltpu.VMEM((768, 1024), bf16),
             pltpu.VMEM((384, 256), f32),
             pltpu.VMEM((128, 3, 128), f32),
+            pltpu.VMEM((128, 3, 128), f32),
+            pltpu.VMEM((128, 256), f32),
             pltpu.SemaphoreType.DMA,
             pltpu.SemaphoreType.DMA,
             pltpu.SemaphoreType.DMA,
@@ -377,10 +384,13 @@
             vmem_limit_bytes=VMEM_LIMIT, collective_id=3, has_side_effects=True
         ),
         name="place",
-    )(incoming, order, z_table)
-
-
-def wave_kernel(
+    )(
+        frequency_part(member), incoming, order, table["z"], table["outer"],
+        table["outer_back"], table["inner"], table["inner_back"], table["twist"],
+    )
+
+
+def wave_part(
     part_ref, in_ref, outer_ref, outer_back_ref, inner_ref, inner_back_ref, twist_ref,
     out_ref, mid_ref,
 ):
@@ -442,12 +452,12 @@
         out_ref[:, c, :] = dot3(outer_back_ref[0], outer_back_ref[1], hi, lo)
 
 
-def wave_flow(spec, table, member):
+def frequency_part(member):
     special = member % 64 == 63
     freq = jnp.where(member < 64, member + 1, (member - 63) % 64)
     freq = jnp.where(member == 63, -64, freq)
     side = jnp.where(member < 64, 1.0, -1.0)
-    part = jnp.stack(
+    return jnp.stack(
         [
             freq.astype(f32),
             jnp.where(special, 1.0, 0.0),
@@ -455,18 +465,6 @@
             jnp.where(special, 1.0, 2.0),
         ]
     ).astype(f32)
-    return pl.pallas_call(
-        wave_kernel,
-        out_shape=jax.ShapeDtypeStruct((128, 3, 128), f32),
-        in_specs=[pl.BlockSpec(memory_space=pltpu.SMEM)] + vmem(6),
-        out_specs=pl.BlockSpec(memory_space=pltpu.VMEM),
-        scratch_shapes=[pltpu.VMEM((128, 256), f32)],
-        compiler_params=pltpu.CompilerParams(vmem_limit_bytes=VMEM_LIMIT),
-        name="wave",
-    )(
-        part, spec, table["outer"], table["outer_back"], table["inner"],
-        table["inner_back"], table["twist"],
-    )
 
 
 ERFC_SHIFT = 4.0
@@ -867,9 +865,7 @@
     route = route.reshape(64, 128)
     order = lax.dynamic_index_in_dim(node_perm, row_gx, 0, keepdims=False).reshape(128, 128)
     incoming = send_message(positions, route)
-    grid, beside, spec = place_on_grid(incoming, order, table["z"])
-    wave = wave_flow(spec, table, member)
-    grid, wave = lax.optimization_barrier((grid, wave))
+    grid, beside, wave = place_on_grid(incoming, order, table, member)
     lists = pair_lists(pair_first[0], pair_second[0], pair_count[0])
     own_vel, far_vel = pair_velocities(grid, beside, lists, pair_count)
     reply = reply_message(own_vel, far_vel, wave, order, table["z"])

time: 140 us -> 141 us (level)
  local copies, waits for them, and re-layouts: 2.62 us -> 4.45 us
    pallas_call x1 -> x0, Pallas kernels: 2.16 us -> none  [wave_flow(): pl.pallas_call(wave_kernel, out_shape=jax.ShapeDtypeStruct((128, 3, 128),...]
    unnamed x26 -> x28, local copies, waits for them, and re-layouts: 2.55 us -> 4.38 us
where the time goes in v9:
time: 141 us
  Pallas kernels  135 us (96%)
  local copies, waits for them, and re-layouts  4.45 us (3%)
  between operations  1.51 us (1%)
    pallas_call x1, Pallas kernels, pair_velocities(): pl.pallas_call(pair_kernel, out_shape=[plane, plane], in_specs=[pl.BlockS...  52.6 us
    pallas_call x1, Pallas kernels, reply_message(): pl.pallas_call(partial(reply_kernel, members, n_gx, n_gy), out_shape=jax....  33.2 us
    pallas_call x1, Pallas kernels, place_on_grid(): pl.pallas_call(partial(place_kernel, members, n_gx, n_gy), out_shape=[jax...  23.6 us
    pallas_call x1, Pallas kernels, send_message(): pl.pallas_call(partial(send_kernel, members, n_gx, n_gy), out_shape=jax.S...  20.4 us
    pallas_call x1, Pallas kernels, move_beads(): pl.pallas_call(move_kernel, out_shape=[flat, flat], in_specs=vmem(4), out...  4.73 us
    unnamed x28, local copies, waits for them, and re-layouts  4.38 us

profile of v9, /device:TPU:1, one launch (start us, length us, event | category | flops | bytes accessed | tf_op | source)
XLA Modules:
  0.0 140.6 jit_solution(12510969661984303334)
XLA Ops:
  0.6 0.0 copy-start
  0.6 0.0 copy-start.2
  0.7 0.1 pad_maximum_fusion.part_ref
  0.8 1.1 copy-done
  1.9 0.0 copy-done.2
  1.9 0.0 copy-start.9
  1.9 0.8 copy-done.9
  2.7 0.0 copy-start.1
  2.7 0.0 copy-start.3
  2.7 0.0 copy-start.4
  2.7 20.4 %send.1.in_ref = f32[128,6,128]{2,1,0:T(8,128)S(1)} custom-call(f32[3,8192]{1,0:T(4,128)S(1)} %copy-done.2, s32[64,128]{1,0:T(8,128)S(1)} %bitcast.10), custom_call_target="tpu_custom_call" | custom-call | tf_op jit(solution)/shard_map/send/pallas_call | solution.py:299
  23.1 0.0 copy-done.6
  23.1 0.0 copy-done.1
  23.1 0.0 copy-done.3
  23.1 0.0 copy-done.4
  23.1 0.0 copy-start.7
  23.2 0.9 copy-done.7
  24.0 0.9 copy-done.8
  25.0 23.6 %place.1 = (f32[6,128,128]{2,1,0:T(8,128)S(1)}, f32[6,128,128]{2,1,0:T(8,128)S(1)}, f32[128,3,128]{2,1,0:T(4,128)S(1)}) custom-call(f32[4]{0:T(128)S(1)} %pad_maximum_fusion.part_ref, f32[128,6,128]{2,1,0:T(8,128)S(1)} %send.1.in_ref, s32[128,128]{1,0:T(8,128)S(1)} %bitcast.8, bf16[2,2,128,128]{3,2,1,0:T(8,128)(2,1)S(1)} %copy-done.1, ...), custom_call_target="tpu_custom_call" | custom-call | tf_op jit(solution)/shard_map/place/pallas_call | solution.py:363
  48.6 0.0 copy-start.11
  49.2 0.0 copy-done.12
  49.3 0.0 copy-done.11
  49.3 0.0 copy-start.13
  49.3 0.6 copy-done.13
  49.9 0.1 broadcast_in_dim.15
  50.0 52.6 %pairs.1 = (f32[3,128,128]{2,1,0:T(8,128)S(1)}, f32[3,128,128]{2,1,0:T(8,128)S(1)}) custom-call(s32[4,1152]{1,0:T(4,128)S(1)} %pad_add_fusion.list_ref, s32[1]{0:T(128)} %copy.16.count_ref, f32[6,128,128]{2,1,0:T(8,128)S(1)} %get-tuple-element.7.own_ref, f32[6,128,128]{2,1,0:T(8,128)S(1)} %get-tuple-element.8.beside_ref), custom_call_target="tpu_custom_call" | custom-call | flops 49999998976 | bytes 1048576 | tf_op jit(solution)/shard_map/pairs/pallas_call | solution.py:723
  102.7 0.0 copy-start.5
  102.7 0.0 copy-start.10
  102.7 33.2 %reply.1.in_ref = f32[128,3,128]{2,1,0:T(4,128)S(1)} custom-call(f32[3,128,128]{2,1,0:T(8,128)S(1)} %get-tuple-element.9.own_ref, f32[3,128,128]{2,1,0:T(8,128)S(1)} %get-tuple-element.10.far_ref, f32[128,3,128]{2,1,0:T(4,128)S(1)} %get-tuple-element.11.flow_ref, s32[128,128]{1,0:T(8,128)S(1)} %bitcast.9, bf16[2,2,128,128]{3,2,1,0:T(8,128)(2,1)S(1)} %copy-done.1), custom_call_target="tpu_custom_call" | custom-call | tf_op jit(solution)/shard_map/reply/pallas_call | solution.py:794
  135.9 0.0 copy-done.5
  135.9 0.0 copy-done.10
  135.9 4.7 %move.1 = (f32[3,8192]{1,0:T(4,128)}, f32[3,8192]{1,0:T(4,128)}) custom-call(f32[128,3,128]{2,1,0:T(4,128)S(1)} %reply.1.in_ref, s32[64,128]{1,0:T(8,128)S(1)} %bitcast.11, f32[3,8192]{1,0:T(4,128)S(1)} %copy-done.2, f32[3,8192]{1,0:T(4,128)S(1)} %copy-done.5), custom_call_target="tpu_custom_call" | custom-call | tf_op jit(solution)/shard_map/move/pallas_call | solution.py:844
  (6 shorter events, 0.0 us)
Async XLA Ops:
  0.6 1.2 copy-start
  0.6 1.2 copy-start.2
  1.9 21.2 %copy-start.6 = (bf16[2,256,128]{2,1,0:T(8,128)(2,1)S(1)}, bf16[2,256,128]{2,1,0:T(8,128)(2,1)}, u32[]{:S(2)}) copy-start(bf16[2,256,128]{2,1,0:T(8,128)(2,1)} %constant.69.clone.outer_ref) | copy-start | bytes 393220
  1.9 0.8 copy-start.9
  2.7 20.4 %copy-start.1 = (bf16[2,2,128,128]{3,2,1,0:T(8,128)(2,1)S(1)}, bf16[2,2,128,128]{3,2,1,0:T(8,128)(2,1)}, u32[]{:S(2)}) copy-start(bf16[2,2,128,128]{3,2,1,0:T(8,128)(2,1)} %constant.68.clone.z_ref) | copy-start | bytes 393220
  2.7 20.4 %copy-start.3 = (bf16[2,256,256]{2,1,0:T(8,128)(2,1)S(1)}, bf16[2,256,256]{2,1,0:T(8,128)(2,1)}, u32[]{:S(2)}) copy-start(bf16[2,256,256]{2,1,0:T(8,128)(2,1)} %constant.71.clone.inner_ref) | copy-start | bytes 786436
  2.7 20.5 %copy-start.4 = (bf16[2,256,256]{2,1,0:T(8,128)(2,1)S(1)}, bf16[2,256,256]{2,1,0:T(8,128)(2,1)}, u32[]{:S(2)}) copy-start(bf16[2,256,256]{2,1,0:T(8,128)(2,1)} %constant.72.clone.inner_back_ref) | copy-start | bytes 786436
  23.1 0.9 copy-start.7
  24.0 0.9 copy-start.8
  25.0 24.3 %copy-start.12 = (s32[1,1024]{1,0:T(1,128)S(1)}, s32[1,1024]{1,0:T(1,128)}, u32[]{:S(2)}) copy-start(s32[1,1024]{1,0:T(1,128)} %param.19) | copy-start | bytes 12292
  48.6 0.7 copy-start.11
  49.3 0.7 copy-start.13
  102.7 33.2 %copy-start.5 = (f32[3,8192]{1,0:T(4,128)S(1)}, f32[3,8192]{1,0:T(4,128)}, u32[]{:S(2)}) copy-start(f32[3,8192]{1,0:T(4,128)} %noise_ref.1) | copy-start | bytes 294916
  102.7 33.2 %copy-start.10 = (s32[8192]{0:T(1024)S(1)}, s32[8192]{0:T(1024)}, u32[]{:S(2)}) copy-start(s32[8192]{0:T(1024)} %param.16) | copy-start | bytes 98308

commit v10 on v9

--- a/solution.py
+++ b/solution.py
@@ -78,12 +78,13 @@
     inner = 2.0 * np.pi * (a[:, None] * a[None, :] / 8.0 + b[:, None] * b[None, :] / 16.0)
     twist = turn * (k1[:, None] * a[None, :] + k2[:, None] * b[None, :])
     c_out, s_out, c_in, s_in = np.cos(outer), np.sin(outer), np.cos(inner), np.sin(inner)
+    inner = np.block([[c_in, -s_in], [s_in, c_in]])
+    inner_back = np.block([[c_in, s_in], [-s_in, c_in]])
+    outer_and_z = np.block([[c_out, z_xy], [-s_out, z_z]])
+    outer_back = np.concatenate([c_out, -s_out], 1)
     return {
         "z": split_table(np.stack([z_xy, z_z])),
-        "outer": split_table(np.concatenate([c_out, -s_out], 0)),
-        "outer_back": split_table(np.concatenate([c_out, -s_out], 1)),
-        "inner": split_table(np.block([[c_in, -s_in], [s_in, c_in]])),
-        "inner_back": split_table(np.block([[c_in, s_in], [-s_in, c_in]])),
+        "all": split_table(np.concatenate([inner, inner_back, outer_and_z, outer_back], 0)),
         "twist": np.stack([np.cos(twist), np.sin(twist)]).astype(np.float32),
     }
 
@@ -317,13 +318,14 @@
 
 
 def place_kernel(
-    members, n_gx, n_gy, part_ref, in_ref, order_ref, z_ref, outer_ref, outer_back_ref, inner_ref,
-    inner_back_ref, twist_ref, grid_ref, beside_ref, flow_ref, left_ref, sum_ref, spec_ref,
+    members, n_gx, n_gy, part_ref, in_ref, order_ref, all_ref, twist_ref, grid_ref, beside_ref, flow_ref, left_ref, sum_ref, spec_ref,
     spec_in_ref, mid_ref, spec_send, spec_recv, side_send, side_recv,
 ):
     g_x = lax.axis_index("gx")
     me = g_x * n_gy + lax.axis_index("gy")
     greet_all(n_gx, n_gy)
+    inner_ref, inner_back_ref = all_ref.at[:, 0:256, :], all_ref.at[:, 256:512, :]
+    outer_ref, outer_back_ref = all_ref.at[:, 512:768, 0:128], all_ref.at[:, 768:896, :]
     scatter_rows(
         6, members, lambda c, r: in_ref[r, c : c + 1, :], order_ref, left_ref, sum_ref
     )
@@ -334,8 +336,8 @@
     unpack_sums(6, sum_ref, to_grid)
     for c in range(3):
         hi, lo = split2(grid_ref[3 + c])
-        kind = 0 if c < 2 else 1
-        spec_ref[:, c, :] = dot3(z_ref[0, kind], z_ref[1, kind], hi, lo, dot_t)
+        kind = slice(512, 640) if c < 2 else slice(640, 768)
+        spec_ref[:, c, :] = dot3(all_ref[0, kind, 128:256], all_ref[1, kind, 128:256], hi, lo, dot_t)
     wait_for_all(members)
     side = pltpu.make_async_remote_copy(
         src_ref=grid_ref,
@@ -367,7 +369,7 @@
             jax.ShapeDtypeStruct((6, 128, 128), f32),
             jax.ShapeDtypeStruct((128, 3, 128), f32),
         ],
-        in_specs=[pl.BlockSpec(memory_space=pltpu.SMEM)] + vmem(8),
+        in_specs=[pl.BlockSpec(memory_space=pltpu.SMEM)] + vmem(4),
         out_specs=vmem(3),
         scratch_shapes=[
             pltpu.VMEM((768, 1024), bf16),
@@ -385,8 +387,7 @@
         ),
         name="place",
     )(
-        frequency_part(member), incoming, order, table["z"], table["outer"],
-        table["outer_back"], table["inner"], table["inner_back"], table["twist"],
+        frequency_part(member), incoming, order, table["all"], table["twist"]
     )
 
 

time: 141 us -> 141 us (level)
    unnamed x28 -> x24, local copies, waits for them, and re-layouts: 4.38 us -> 4.35 us
where the time goes in v10:
time: 141 us; the launch traced here: 140 us
  Pallas kernels  134 us (95%)
  local copies, waits for them, and re-layouts  4.42 us (3%)
  between operations  1.5 us (1%)
    pallas_call x1, Pallas kernels, pair_velocities(): pl.pallas_call(pair_kernel, out_shape=[plane, plane], in_specs=[pl.BlockS...  52.5 us
    pallas_call x1, Pallas kernels, reply_message(): pl.pallas_call(partial(reply_kernel, members, n_gx, n_gy), out_shape=jax....  33.3 us
    pallas_call x1, Pallas kernels, place_on_grid(): pl.pallas_call(partial(place_kernel, members, n_gx, n_gy), out_shape=[jax...  23.6 us
    pallas_call x1, Pallas kernels, send_message(): pl.pallas_call(partial(send_kernel, members, n_gx, n_gy), out_shape=jax.S...  20.3 us
    pallas_call x1, Pallas kernels, move_beads(): pl.pallas_call(move_kernel, out_shape=[flat, flat], in_specs=vmem(4), out...  4.73 us
    unnamed x24, local copies, waits for them, and re-layouts  4.35 us

profile of v10, /device:TPU:1, one launch (start us, length us, event | category | flops | bytes accessed | tf_op | source)
XLA Modules:
  0.0 140.5 jit_solution(1465519900722707909)
XLA Ops:
  0.6 0.0 copy-start
  0.6 0.0 copy-start.1
  0.7 0.1 pad_maximum_fusion.part_ref
  0.8 1.1 copy-done
  1.9 0.0 copy-start.2
  1.9 0.9 copy-done.2
  2.8 0.0 copy-start.7
  2.8 0.8 copy-done.7
  3.5 20.3 %send.1.in_ref = f32[128,6,128]{2,1,0:T(8,128)S(1)} custom-call(f32[3,8192]{1,0:T(4,128)S(1)} %copy-done.2, s32[64,128]{1,0:T(8,128)S(1)} %bitcast.10), custom_call_target="tpu_custom_call" | custom-call | tf_op jit(solution)/shard_map/send/pallas_call | solution.py:300
  23.9 0.0 copy-done.1
  23.9 0.0 copy-start.6
  23.9 0.9 copy-done.6
  24.8 0.0 copy-start.10
  24.8 23.6 %place.1 = (f32[6,128,128]{2,1,0:T(8,128)S(1)}, f32[6,128,128]{2,1,0:T(8,128)S(1)}, f32[128,3,128]{2,1,0:T(4,128)S(1)}) custom-call(f32[4]{0:T(128)S(1)} %pad_maximum_fusion.part_ref, f32[128,6,128]{2,1,0:T(8,128)S(1)} %send.1.in_ref, s32[128,128]{1,0:T(8,128)S(1)} %bitcast.8, bf16[2,896,256]{2,1,0:T(8,128)(2,1)S(1)} %copy-done.1, f32[2,128,128]{2,1,0:T(8,128)S(1)} %copy-done.6), custom_call_target="tpu_custom_call" | custom-call | tf_op jit(solution)/shard_map/place/pallas_call | solution.py:365
  48.4 0.0 copy-start.9
  49.0 0.0 copy-done.10
  49.1 0.0 copy-done.9
  49.1 0.0 copy-start.11
  49.1 0.6 copy-done.11
  49.7 0.1 broadcast_in_dim.15
  49.8 0.0 copy-start.5
  49.9 52.5 %pairs.1 = (f32[3,128,128]{2,1,0:T(8,128)S(1)}, f32[3,128,128]{2,1,0:T(8,128)S(1)}) custom-call(s32[4,1152]{1,0:T(4,128)S(1)} %pad_add_fusion.list_ref, s32[1]{0:T(128)} %copy.13.count_ref, f32[6,128,128]{2,1,0:T(8,128)S(1)} %get-tuple-element.7.own_ref, f32[6,128,128]{2,1,0:T(8,128)S(1)} %get-tuple-element.8.beside_ref), custom_call_target="tpu_custom_call" | custom-call | flops 49999998976 | bytes 1048576 | tf_op jit(solution)/shard_map/pairs/pallas_call | solution.py:724
  102.3 0.0 copy-done.5
  102.3 0.0 copy-start.3
  102.3 0.0 copy-start.4
  102.4 0.0 copy-start.8
  102.4 33.3 %reply.1.in_ref = f32[128,3,128]{2,1,0:T(4,128)S(1)} custom-call(f32[3,128,128]{2,1,0:T(8,128)S(1)} %get-tuple-element.9.own_ref, f32[3,128,128]{2,1,0:T(8,128)S(1)} %get-tuple-element.10.far_ref, f32[128,3,128]{2,1,0:T(4,128)S(1)} %get-tuple-element.11.flow_ref, s32[128,128]{1,0:T(8,128)S(1)} %bitcast.9, bf16[2,2,128,128]{3,2,1,0:T(8,128)(2,1)S(1)} %copy-done.5), custom_call_target="tpu_custom_call" | custom-call | tf_op jit(solution)/shard_map/reply/pallas_call | solution.py:795
  135.7 0.0 copy-done.3
  135.7 0.0 copy-done.4
  135.7 0.0 copy-done.8
  135.7 4.7 %move.1 = (f32[3,8192]{1,0:T(4,128)}, f32[3,8192]{1,0:T(4,128)}) custom-call(f32[128,3,128]{2,1,0:T(4,128)S(1)} %reply.1.in_ref, s32[64,128]{1,0:T(8,128)S(1)} %bitcast.11, f32[3,8192]{1,0:T(4,128)S(1)} %copy-done.3, f32[3,8192]{1,0:T(4,128)S(1)} %copy-done.4), custom_call_target="tpu_custom_call" | custom-call | tf_op jit(solution)/shard_map/move/pallas_call | solution.py:845
  (3 shorter events, 0.0 us)
Async XLA Ops:
  0.6 1.2 copy-start
  0.6 23.2 %copy-start.1 = (bf16[2,896,256]{2,1,0:T(8,128)(2,1)S(1)}, bf16[2,896,256]{2,1,0:T(8,128)(2,1)}, u32[]{:S(2)}) copy-start(bf16[2,896,256]{2,1,0:T(8,128)(2,1)} %constant.63.clone.all_ref) | copy-start | bytes 2752516
  1.9 0.9 copy-start.2
  2.8 0.8 copy-start.7
  23.9 0.9 copy-start.6
  24.8 24.2 %copy-start.10 = (s32[1,1024]{1,0:T(1,128)S(1)}, s32[1,1024]{1,0:T(1,128)}, u32[]{:S(2)}) copy-start(s32[1,1024]{1,0:T(1,128)} %param.16) | copy-start | bytes 12292
  48.4 0.7 copy-start.9
  49.1 0.7 copy-start.11
  49.8 52.5 %copy-start.5 = (bf16[2,2,128,128]{3,2,1,0:T(8,128)(2,1)S(1)}, bf16[2,2,128,128]{3,2,1,0:T(8,128)(2,1)}, u32[]{:S(2)}) copy-start(bf16[2,2,128,128]{3,2,1,0:T(8,128)(2,1)} %constant.62.clone.z_ref) | copy-start | bytes 393220
  102.3 33.4 %copy-start.3 = (f32[3,8192]{1,0:T(4,128)S(1)}, f32[3,8192]{1,0:T(4,128)}, u32[]{:S(2)}) copy-start(f32[3,8192]{1,0:T(4,128)} %pos_ref.3) | copy-start | bytes 294916
  102.3 33.4 %copy-start.4 = (f32[3,8192]{1,0:T(4,128)S(1)}, f32[3,8192]{1,0:T(4,128)}, u32[]{:S(2)}) copy-start(f32[3,8192]{1,0:T(4,128)} %noise_ref.1) | copy-start | bytes 294916
  102.4 33.4 %copy-start.8 = (s32[8192]{0:T(1024)S(1)}, s32[8192]{0:T(1024)}, u32[]{:S(2)}) copy-start(s32[8192]{0:T(1024)} %param.13) | copy-start | bytes 98308
